TPU v7x, 128 devices: a whole 4x4x4 slice. The times are simulated.
128 devices in a mesh: dp: 32 (over x, z, core), row: 2 (over y_lo), col: 2 (over y_hi).
Axes of the slice: x: 4, y: 4 (y_hi: 2, y_lo: 2; y = y_hi * 2 + y_lo), z: 4, core: 2. Of those that a mesh axis runs over, the one named last changes fastest.
Arguments:
- tokens: bfloat16 [32768, 1536], P(('dp', 'row'), 'col'), may hold values from -6 to 6
- cotangent: bfloat16 [32768, 1536], P(('dp', 'row'), 'col'), may hold values from -6 to 6
- attn_gain: float32 [1536], P('col'), may hold values from 0.25 to 1.75
- ffn_gain: float32 [1536], P('col'), may hold values from 0.25 to 1.75
- qkv_weight: bfloat16 [1536, 2048], P('col', 'row'), may hold values from -0.15625 to 0.15625
- out_weight: bfloat16 [1536, 1536], P('row', 'col'), may hold values from -1.25 to 1.25
- router_weight: bfloat16 [1536, 6], P('col'), may hold values from -0.078125 to 0.078125
- gate_weight: bfloat16 [6, 1536, 768], P(None, 'col', 'row'), may hold values from -0.15625 to 0.15625
- up_weight: bfloat16 [6, 1536, 768], P(None, 'col', 'row'), may hold values from -0.15625 to 0.15625
- down_weight: bfloat16 [6, 768, 1536], P(None, 'row', 'col'), may hold values from -0.625 to 0.625
- routes: int32 [32768, 4], P('dp'), may hold values from 0 to 5, all different within a row
- segments: int32 [32768], P('dp'), may hold values from 0 to 4, as said below
Outputs:
- layer_out: bfloat16 [32768, 1536], P(('dp', 'row'), 'col')
- input_grad: float32 [32768, 1536], P(('dp', 'row'), 'col')
- attn_gain_grad: float32 [1536], P('col')
- ffn_gain_grad: float32 [1536], P('col')
- qkv_grad: float32 [1536, 2048], P('col', 'row')
- out_grad: float32 [1536, 1536], P('row', 'col')
- router_grad: float32 [1536, 6], P('col')
- gate_grad: float32 [6, 1536, 768], P(None, 'col', 'row')
- up_grad: float32 [6, 1536, 768], P(None, 'col', 'row')
- down_grad: float32 [6, 768, 1536], P(None, 'row', 'col')
Inputs may be any that keep to these rules, and one draw needn't show every extreme that they name: `routes`: each token names 4 different experts; every expert is named by some token. Within each packed sequence of 1024 tokens the segment numbers run from 0 to 4 without falling; segment 2 holds exactly 512 tokens and contains the sequence's middle, the other segments are shorter.
All inputs are finite; a program needn't handle non-finite values.
Results may differ from a plain program's by a relative error of at most 0.022.
Values may be sent and summed in bfloat16 or wider, within the bound.
A program may use at most 256 MiB of HBM per device.

v0:
```python
import math

import jax
import jax.numpy as jnp
from jax import lax
from jax.sharding import PartitionSpec as P

QUERY_HEADS = 12
KEY_VALUE_HEADS = 2
HEAD_SIZE = 128


epsilon = 1e-06
rope_base = 10000.0
masked_value = -1e30


def tables(positions):
    steps_up = jnp.arange(HEAD_SIZE // 2, dtype=jnp.float32) * (2.0 / HEAD_SIZE)
    inverse = jnp.exp(-math.log(rope_base) * steps_up)
    angles = positions[:, None] * inverse[None, :]
    return (jnp.cos(angles), jnp.sin(angles))


def rotate(values, cosine_table, sine_table):
    half_width = values.shape[-1] // 2
    first_half = values[..., :half_width]
    second_half = values[..., half_width:]
    return jnp.concatenate(
        [
            first_half * cosine_table - second_half * sine_table,
            second_half * cosine_table + first_half * sine_table,
        ],
        axis=-1,
    )


def unrotate(values, cosine_table, sine_table):
    half_width = values.shape[-1] // 2
    first_half = values[..., :half_width]
    second_half = values[..., half_width:]
    return jnp.concatenate(
        [
            first_half * cosine_table + second_half * sine_table,
            second_half * cosine_table - first_half * sine_table,
        ],
        axis=-1,
    )


def feature_total(values):
    return lax.psum(values, "col")


def collect_rows(values):
    return lax.all_gather(values, "row", axis=0, tiled=True)


def collect_cols(values):
    return lax.all_gather(values, "col", axis=0, tiled=True)


def reduce_cols(term_fn, row_count):
    return lax.psum_scatter(
        term_fn(jnp.int32(0), row_count * lax.axis_size("col")),
        "col",
        scatter_dimension=0,
        tiled=True,
    )


def reduce_rows(term_fn, row_count):
    return lax.psum_scatter(
        term_fn(jnp.int32(0), row_count * lax.axis_size("row")),
        "row",
        scatter_dimension=0,
        tiled=True,
    )


def norm_scale(values, model_width):
    return lax.rsqrt(feature_total(jnp.sum(values * values, axis=1)) / model_width + epsilon)


def norm_back(grad_normed, values, scale, gain, model_width):
    scaled_grad = grad_normed * gain
    inner = feature_total(jnp.sum(scaled_grad * values, axis=1))
    values_grad = (
        scale[:, None] * scaled_grad
        - values * (scale * scale * scale * inner / model_width)[:, None]
    )
    gain_part = jnp.sum(grad_normed * values * scale[:, None], axis=0)
    return (values_grad, gain_part)


def local(
    tokens,
    cotangent,
    attn_gain,
    ffn_gain,
    qkv_weight,
    out_weight,
    router_weight,
    gate_weight,
    up_weight,
    down_weight,
    routes,
    segments,
):
    f32 = jnp.float32
    bf16 = jnp.bfloat16
    row_devices = lax.axis_size("row")
    col_devices = lax.axis_size("col")
    row_index = lax.axis_index("row")
    col_index = lax.axis_index("col")
    group_tokens = segments.shape[0]
    row_share = group_tokens // row_devices
    col_share = group_tokens // col_devices
    model_width = tokens.shape[1] * col_devices
    tokens_per_group = QUERY_HEADS // KEY_VALUE_HEADS
    local_groups = qkv_weight.shape[1] // ((tokens_per_group + 2) * HEAD_SIZE)
    inverse_root = HEAD_SIZE ** (-0.5)
    experts = gate_weight.shape[0]
    residual = tokens.astype(f32)
    scale_one = norm_scale(residual, model_width)
    normed_one = (residual * scale_one[:, None] * attn_gain).astype(bf16)
    normed_one_all = collect_rows(normed_one)
    router_logits = lax.psum(
        jnp.dot(normed_one_all, router_weight, preferred_element_type=f32), "col"
    )
    chosen = jnp.any(
        routes[:, :, None] == jnp.arange(experts, dtype=jnp.int32)[None, None, :], axis=1
    )
    masked = jnp.where(chosen, router_logits, masked_value)
    top_logit = jnp.max(masked, axis=1, keepdims=True)
    raised_values = jnp.exp(masked - top_logit)
    gate_values = raised_values / jnp.sum(raised_values, axis=1, keepdims=True)

    def qkv_term(first_row, row_count):
        return jnp.dot(normed_one_all, qkv_weight, preferred_element_type=f32)

    projected_rows = reduce_cols(qkv_term, col_share).reshape(
        col_share, local_groups, tokens_per_group + 2, HEAD_SIZE
    )
    query_first = col_index * col_share
    query_places = query_first + jnp.arange(col_share, dtype=jnp.int32)
    cosine_table, sine_table = tables(query_places.astype(f32))
    queries = rotate(
        projected_rows[:, :, :tokens_per_group],
        cosine_table[:, None, None],
        sine_table[:, None, None],
    ).astype(bf16)
    keys_local = rotate(
        projected_rows[:, :, tokens_per_group], cosine_table[:, None], sine_table[:, None]
    ).astype(bf16)
    values_local = projected_rows[:, :, tokens_per_group + 1].astype(bf16)
    keys_all, values_all = (
        lax.all_gather(keys_local, "col", axis=0, tiled=True),
        lax.all_gather(values_local, "col", axis=0, tiled=True),
    )
    block_rows = min(512, col_share)
    block_count = col_share // block_rows
    key_places = jnp.arange(group_tokens, dtype=jnp.int32)
    query_segments = lax.dynamic_slice_in_dim(segments, query_first, col_share, 0)
    query_blocks = queries.reshape(
        block_count, block_rows, local_groups, tokens_per_group, HEAD_SIZE
    )
    place_blocks = query_places.reshape(block_count, block_rows)
    segment_blocks = query_segments.reshape(block_count, block_rows)

    def block_scores(query_block, place_block, segment_block):
        scores = (
            jnp.einsum("qgnd,kgd->gnqk", query_block, keys_all, preferred_element_type=f32)
            * inverse_root
        )
        allowed = (key_places[None, :] <= place_block[:, None]) & (
            segments[None, :] == segment_block[:, None]
        )
        return jnp.where(allowed[None, None], scores, masked_value)

    def forward_block(pieces):
        query_block, place_block, segment_block = pieces
        scores = block_scores(query_block, place_block, segment_block)
        top_score = jnp.max(scores, axis=-1, keepdims=True)
        raised_scores = jnp.exp(scores - top_score)
        score_totals = jnp.sum(raised_scores, axis=-1, keepdims=True)
        probabilities = (raised_scores / score_totals).astype(bf16)
        context_block = jnp.einsum(
            "gnqk,kgd->qgnd", probabilities, values_all, preferred_element_type=f32
        )
        return (context_block, top_score[..., 0] + jnp.log(score_totals[..., 0]))

    context, log_totals = lax.map(forward_block, (query_blocks, place_blocks, segment_blocks))
    context_local = context.reshape(col_share, local_groups * tokens_per_group * HEAD_SIZE).astype(
        bf16
    )
    context_all = collect_cols(context_local)

    def out_term(first_row, row_count):
        return jnp.dot(context_all, out_weight, preferred_element_type=f32)

    hidden_in = residual + reduce_rows(out_term, row_share)
    scale_two = norm_scale(hidden_in, model_width)
    normed_two = (hidden_in * scale_two[:, None] * ffn_gain).astype(bf16)
    normed_two_all = collect_rows(normed_two)

    def expert_term(first_row, row_count):
        return jnp.stack(
            [
                jnp.einsum("td,edh->teh", normed_two_all, gate_weight, preferred_element_type=f32),
                jnp.einsum("td,edh->teh", normed_two_all, up_weight, preferred_element_type=f32),
            ],
            axis=1,
        )

    gate_up = reduce_cols(expert_term, col_share)
    gate_pre = gate_up[:, 0]
    up_pre = gate_up[:, 1]
    local_gates = lax.dynamic_slice_in_dim(gate_values, query_first, col_share, 0)
    sigmoid_gate = jax.nn.sigmoid(gate_pre)
    silu_gate = gate_pre * sigmoid_gate
    activated = silu_gate * up_pre
    weighted = (local_gates[:, :, None] * activated).astype(bf16)
    weighted_all = collect_cols(weighted)

    def down_term(first_row, row_count):
        return jnp.einsum("teh,ehd->td", weighted_all, down_weight, preferred_element_type=f32)

    layer_out = (hidden_in + reduce_rows(down_term, row_share)).astype(bf16)
    out_grad_all = collect_rows(cotangent)
    down_grad = jnp.einsum("teh,td->ehd", weighted_all, out_grad_all, preferred_element_type=f32)

    def weighted_term(first_row, row_count):
        return jnp.einsum("td,ehd->teh", out_grad_all, down_weight, preferred_element_type=f32)

    weighted_grad = reduce_cols(weighted_term, col_share)
    gate_part = jnp.sum(activated * weighted_grad, axis=2)
    gate_slots = lax.dynamic_update_slice_in_dim(
        jnp.zeros((group_tokens, experts), f32), gate_part, query_first, 0
    )
    gates_grad = lax.psum(gate_slots, ("row", "col"))
    activated_grad = local_gates[:, :, None] * weighted_grad
    silu_grad = sigmoid_gate * (1.0 + gate_pre * (1.0 - sigmoid_gate))
    gate_up_grad = jnp.stack(
        [activated_grad * up_pre * silu_grad, activated_grad * silu_gate], axis=1
    ).astype(bf16)
    gate_up_all = collect_cols(gate_up_grad)
    gate_grad = jnp.einsum(
        "td,teh->edh", normed_two_all, gate_up_all[:, 0], preferred_element_type=f32
    )
    up_grad = jnp.einsum(
        "td,teh->edh", normed_two_all, gate_up_all[:, 1], preferred_element_type=f32
    )

    def normed_term(first_row, row_count):
        return jnp.einsum(
            "teh,edh->td", gate_up_all[:, 0], gate_weight, preferred_element_type=f32
        ) + jnp.einsum("teh,edh->td", gate_up_all[:, 1], up_weight, preferred_element_type=f32)

    normed_two_grad = reduce_rows(normed_term, row_share)
    hidden_norm_grad, ffn_gain_part = norm_back(
        normed_two_grad, hidden_in, scale_two, ffn_gain, model_width
    )
    hidden_grad = cotangent.astype(f32) + hidden_norm_grad
    hidden_low = hidden_grad.astype(bf16)
    hidden_grad_all = collect_rows(hidden_low)
    out_weight_grad = jnp.einsum(
        "tq,td->qd", context_all, hidden_grad_all, preferred_element_type=f32
    )

    def context_term(first_row, row_count):
        return jnp.einsum("td,qd->tq", hidden_grad_all, out_weight, preferred_element_type=f32)

    context_grad = reduce_cols(context_term, col_share).astype(bf16)
    context_grad = context_grad.reshape(
        block_count, block_rows, local_groups, tokens_per_group, HEAD_SIZE
    )

    def backward_block(carry, pieces):
        key_acc, value_acc = carry
        query_block, grad_block, log_block, place_block, segment_block = pieces
        scores = block_scores(query_block, place_block, segment_block)
        probabilities = jnp.exp(scores - log_block[..., None])
        prob_grad = jnp.einsum("qgnd,kgd->gnqk", grad_block, values_all, preferred_element_type=f32)
        score_grad = (
            probabilities * (prob_grad - jnp.sum(prob_grad * probabilities, axis=-1, keepdims=True))
        ).astype(bf16)
        query_grad = (
            jnp.einsum("gnqk,kgd->qgnd", score_grad, keys_all, preferred_element_type=f32)
            * inverse_root
        )
        key_acc = (
            key_acc
            + jnp.einsum("gnqk,qgnd->kgd", score_grad, query_block, preferred_element_type=f32)
            * inverse_root
        )
        value_acc = value_acc + jnp.einsum(
            "gnqk,qgnd->kgd", probabilities.astype(bf16), grad_block, preferred_element_type=f32
        )
        return ((key_acc, value_acc), query_grad)

    zero_keys = jnp.zeros((group_tokens, local_groups, HEAD_SIZE), f32)
    (key_sum, value_sum), query_grads = lax.scan(
        backward_block,
        (zero_keys, zero_keys),
        (query_blocks, context_grad, log_totals, place_blocks, segment_blocks),
    )
    key_grad, value_grad = (
        lax.psum_scatter(key_sum, "col", scatter_dimension=0, tiled=True),
        lax.psum_scatter(value_sum, "col", scatter_dimension=0, tiled=True),
    )
    query_grad = unrotate(
        query_grads.reshape(col_share, local_groups, tokens_per_group, HEAD_SIZE),
        cosine_table[:, None, None],
        sine_table[:, None, None],
    )
    key_grad = unrotate(key_grad, cosine_table[:, None], sine_table[:, None])
    projected_grad = jnp.concatenate(
        [query_grad, key_grad[:, :, None], value_grad[:, :, None]], axis=2
    )
    projected_grad = projected_grad.reshape(
        col_share, local_groups * (tokens_per_group + 2) * HEAD_SIZE
    ).astype(bf16)
    projected_all = collect_cols(projected_grad)
    qkv_grad = jnp.einsum("td,tc->dc", normed_one_all, projected_all, preferred_element_type=f32)

    def input_term(first_row, row_count):
        return jnp.einsum("tc,dc->td", projected_all, qkv_weight, preferred_element_type=f32)

    normed_one_grad = reduce_rows(input_term, row_share)
    logits_grad = (
        gate_values * (gates_grad - jnp.sum(gate_values * gates_grad, axis=1, keepdims=True))
    ).astype(bf16)
    router_grad = jnp.einsum("td,te->de", normed_one_all, logits_grad, preferred_element_type=f32)
    own_logits_grad = lax.dynamic_slice_in_dim(logits_grad, row_index * row_share, row_share, 0)
    normed_one_grad = normed_one_grad + jnp.einsum(
        "te,de->td", own_logits_grad, router_weight, preferred_element_type=f32
    )
    input_norm_grad, attn_gain_part = norm_back(
        normed_one_grad, residual, scale_one, attn_gain, model_width
    )
    input_grad = hidden_grad + input_norm_grad
    attn_gain_grad, ffn_gain_grad = lax.psum((attn_gain_part, ffn_gain_part), ("dp", "row"))
    qkv_grad, out_weight_grad, router_grad, gate_grad, up_grad, down_grad = (
        lax.psum(qkv_grad.astype(jnp.bfloat16), "dp").astype(jnp.float32),
        lax.psum(out_weight_grad.astype(jnp.bfloat16), "dp").astype(jnp.float32),
        lax.psum(router_grad.astype(jnp.bfloat16), "dp").astype(jnp.float32),
        lax.psum(gate_grad.astype(jnp.bfloat16), "dp").astype(jnp.float32),
        lax.psum(up_grad.astype(jnp.bfloat16), "dp").astype(jnp.float32),
        lax.psum(down_grad.astype(jnp.bfloat16), "dp").astype(jnp.float32),
    )
    return (
        layer_out,
        input_grad,
        attn_gain_grad,
        ffn_gain_grad,
        qkv_grad,
        out_weight_grad,
        router_grad,
        gate_grad,
        up_grad,
        down_grad,
    )


def solution(mesh):
    in_specs = (
        P(("dp", "row"), "col"),
        P(("dp", "row"), "col"),
        P("col"),
        P("col"),
        P("col", "row"),
        P("row", "col"),
        P("col", None),
        P(None, "col", "row"),
        P(None, "col", "row"),
        P(None, "row", "col"),
        P("dp", None),
        P("dp"),
    )
    out_specs = (
        P(("dp", "row"), "col"),
        P(("dp", "row"), "col"),
        P("col"),
        P("col"),
        P("col", "row"),
        P("row", "col"),
        P("col", None),
        P(None, "col", "row"),
        P(None, "col", "row"),
        P(None, "row", "col"),
    )
    return jax.shard_map(local, mesh=mesh, in_specs=in_specs, out_specs=out_specs, check_vma=False)
```

profile of v0, /device:TPU:1, one launch (start us, length us, event | category | flops | bytes accessed | tf_op | source)
XLA Modules:
  0.0 1466.8 jit_solution(10886527914398628943)
XLA Ops:
  17.8 33.5 %all-gather.10.cloned.1.call-done = bf16[1024,768]{1,0:T(8,128)(2,1)} async-done(((bf16[512,768]{1,0:T(8,128)(2,1)}), bf16[1024,768]{1,0:T(8,128)(2,1)}) %all-gather.10.cloned.1.call-update) | async-done | bytes 1572880 | tf_op jit(solution)/shard_map/all_gather | solution.py:56
  60.2 56.2 %reduce-scatter.11.cloned.1.call-done = f32[512,1024]{1,0:T(8,128)} async-done(((f32[1024,1024]{1,0:T(8,128)}), f32[512,1024]{1,0:T(8,128)}) %reduce-scatter.11.cloned.1.call-update) | async-done | bytes 2097168 | tf_op jit(solution)/shard_map/reduce_scatter | solution.py:64
  122.0 6.5 all_gather.32
  146.4 32.8 %all-gather.12.cloned.1.call-done = bf16[1024,768]{0,1:T(8,128)(2,1)} async-done(((bf16[512,768]{0,1:T(8,128)(2,1)}), bf16[1024,768]{0,1:T(8,128)(2,1)}) %all-gather.12.cloned.1.call-update) | async-done | bytes 1572880 | tf_op jit(solution)/shard_map/all_gather | solution.py:60
  187.2 42.2 %reduce-scatter.13.cloned.1.call-done = f32[512,768]{1,0:T(8,128)} async-done(((f32[1024,768]{1,0:T(8,128)}), f32[512,768]{1,0:T(8,128)}) %reduce-scatter.13.cloned.1.call-update) | async-done | bytes 1572880 | tf_op jit(solution)/shard_map/reduce_scatter | solution.py:73
  232.4 10.4 all-reduce.1
  245.5 16.2 %all-gather.18.cloned.1.call-done = bf16[1024,768]{1,0:T(8,128)(2,1)} async-done(((bf16[512,768]{1,0:T(8,128)(2,1)}), bf16[1024,768]{1,0:T(8,128)(2,1)}) %all-gather.18.cloned.1.call-update) | async-done | bytes 1572880 | tf_op jit(solution)/shard_map/all_gather | solution.py:56
  261.7 8.6 fusion.30
  270.3 24.2 %all-gather.14.cloned.1.call-done = bf16[1024,768]{1,0:T(8,128)(2,1)} async-done(((bf16[512,768]{1,0:T(8,128)(2,1)}), bf16[1024,768]{1,0:T(8,128)(2,1)}) %all-gather.14.cloned.1.call-update) | async-done | bytes 1572880 | tf_op jit(solution)/shard_map/all_gather | solution.py:56
  294.5 6.4 convolution_bitcast_fusion
  304.8 7.0 pad_maximum_fusion
  315.4 97.2 %reduce-scatter.19.cloned.1.call-done = f32[512,6,384]{2,0,1:T(8,128)} async-done(((f32[1024,6,384]{2,0,1:T(8,128)}), f32[512,6,384]{2,0,1:T(8,128)}) %reduce-scatter.19.cloned.1.call-update) | async-done | bytes 4718608 | tf_op jit(solution)/shard_map/reduce_scatter | solution.py:64
  412.5 217.6 %reduce-scatter.15.cloned.1.call-done = f32[512,2,6,384]{3,0,2,1:T(8,128)} async-done(((f32[1024,2,6,384]{3,0,2,1:T(8,128)}), f32[512,2,6,384]{3,0,2,1:T(8,128)}) %reduce-scatter.15.cloned.1.call-update) | async-done | bytes 9437200 | tf_op jit(solution)/shard_map/reduce_scatter | solution.py:64
  637.3 13.5 psum.102
  652.8 7.6 fusion.19
  663.1 11.5 reduce-scatter.21.cloned.1.call-start
  674.6 114.8 %all-gather.20.cloned.1.call-done = bf16[1024,2,6,384]{3,0,2,1:T(8,128)(2,1)} async-done(((bf16[512,2,6,384]{3,0,2,1:T(8,128)(2,1)}), bf16[1024,2,6,384]{3,0,2,1:T(8,128)(2,1)}) %all-gather.20.cloned.1.call-update) | async-done | bytes 9437200 | tf_op jit(solution)/shard_map/all_gather | solution.py:60
  801.1 45.4 %reduce-scatter.21.cloned.1.call-done = f32[512,768]{1,0:T(8,128)} async-done(((f32[1024,768]{1,0:T(8,128)}), f32[512,768]{1,0:T(8,128)}) %reduce-scatter.21.cloned.1.call-update) | async-done | bytes 1572880 | tf_op jit(solution)/shard_map/reduce_scatter | solution.py:73
  856.8 32.0 %all-gather.22.cloned.1.call-done = bf16[1024,768]{1,0:T(8,128)(2,1)} async-done(((bf16[512,768]{1,0:T(8,128)(2,1)}), bf16[1024,768]{1,0:T(8,128)(2,1)}) %all-gather.22.cloned.1.call-update) | async-done | bytes 1572880 | tf_op jit(solution)/shard_map/all_gather | solution.py:56
  894.4 47.8 %reduce-scatter.23.cloned.1.call-done = f32[512,768]{1,0:T(8,128)} async-done(((f32[1024,768]{1,0:T(8,128)}), f32[512,768]{1,0:T(8,128)}) %reduce-scatter.23.cloned.1.call-update) | async-done | bytes 1572880 | tf_op jit(solution)/shard_map/reduce_scatter | solution.py:64
  944.0 11.5 fusion
  956.2 6.8 fusion.8
  968.7 7.6 fusion.39
  988.4 19.4 %reduce-scatter.27.cloned.1.call-done = f32[512,1,128]{0,2,1:T(8,128)} async-done(((f32[1024,1,128]{0,2,1:T(8,128)}), f32[512,1,128]{0,2,1:T(8,128)}) %reduce-scatter.27.cloned.1.call-update) | async-done | bytes 262160 | tf_op jit(solution)/shard_map/reduce_scatter | solution.py:310
  1011.4 36.1 %all-gather.24.cloned.1.call-done = bf16[1024,1024]{0,1:T(8,128)(2,1)} async-done(((bf16[512,1024]{0,1:T(8,128)(2,1)}), bf16[1024,1024]{0,1:T(8,128)(2,1)}) %all-gather.24.cloned.1.call-update) | async-done | bytes 2097168 | tf_op jit(solution)/shard_map/all_gather | solution.py:60
  1052.7 63.0 %all-gather.16.cloned.1.call-done = bf16[1024,6,384]{2,0,1:T(8,128)(2,1)} async-done(((bf16[512,6,384]{2,0,1:T(8,128)(2,1)}), bf16[1024,6,384]{2,0,1:T(8,128)(2,1)}) %all-gather.16.cloned.1.call-update) | async-done | bytes 4718608 | tf_op jit(solution)/shard_map/all_gather | solution.py:60
  1115.8 7.9 convolution_bitcast_fusion.2
  1125.1 8.6 convolution_convert_fusion
  1133.7 7.8 convert_bitcast_fusion
  1155.0 124.3 %psum.108 = bf16[768,6]{0,1:T(8,128)(2,1)S(1)} all-reduce(bf16[768,6]{0,1:T(8,128)(2,1)S(1)} %convolution_convert_fusion.3), channel_id=1, replica_groups=mesh['dp'=32,'row'=2,'col'=2] {'dp'}, use_global_device_ids=true, to_apply=%region_34.35 | all-reduce | flops 4608 | bytes 18432 | tf_op jit(solution)/shard_map/psum | solution.py:347
  1288.4 145.4 %all-reduce = (f32[768]{0:T(1024)}, f32[768]{0:T(1024)}) all-reduce(f32[768]{0:T(1024)S(1)} %get-tuple-element.121, f32[768]{0:T(1024)S(1)} %copy-done.43), channel_id=1, replica_groups=mesh['dp'=32,'row'=2,'col'=2] {'dp','row'}, use_global_device_ids=true, to_apply=%region_29.30 | all-reduce | flops 1536 | bytes 12288 | tf_op jit(solution)/shard_map/psum | solution.py:343
  1443.9 6.6 copy.102
  (241 shorter events, 175.7 us)
Async XLA Ops:
  7.2 293.8 %copy-start = (bf16[6,768,384]{2,1,0:T(8,128)(2,1)S(1)}, bf16[6,768,384]{2,1,0:T(8,128)(2,1)}, u32[]{:S(2)}) copy-start(bf16[6,768,384]{2,1,0:T(8,128)(2,1)} %param.19) | copy-start | bytes 10616836
  7.2 44.0 %all-gather.10.cloned.1.call-start = ((), (), s32[]{:S(2)}) async-start(), calls=%async_computation.10 | async-start | bytes 2359296 | tf_op jit(solution)/shard_map/all_gather | solution.py:56
  17.7 98.7 %reduce-scatter.11.cloned.1.call-start = ((), (), s32[]{:S(2)}) async-start(), calls=%async_computation.11 | async-start | bytes 6291456 | tf_op jit(solution)/shard_map/reduce_scatter | solution.py:64
  56.9 122.2 %all-gather.12.cloned.1.call-start = ((), (), s32[]{:S(2)}) async-start(), calls=%async_computation.12 | async-start | bytes 2359296 | tf_op jit(solution)/shard_map/all_gather | solution.py:60
  57.7 63.7 %copy-start.48 = (f32[64]{0:T(128)}, f32[64]{0:T(128)S(1)}, u32[]{:S(2)}) copy-start(f32[64]{0:T(128)S(1)} %multiply_exponential_fusion) | copy-start | bytes 772
  57.7 63.7 %copy-start.35 = (f32[512]{0:T(512)}, f32[512]{0:T(512)S(1)}, u32[]{:S(2)}) copy-start(f32[512]{0:T(512)S(1)} %fusion.77) | copy-start | bytes 6148
  146.3 83.1 %reduce-scatter.13.cloned.1.call-start = ((), (), s32[]{:S(2)}) async-start(), calls=%async_computation.13 | async-start | bytes 4718592 | tf_op jit(solution)/shard_map/reduce_scatter | solution.py:73
  184.0 77.7 %all-gather.18.cloned.1.call-start = ((), (), s32[]{:S(2)}) async-start(), calls=%async_computation.18 | async-start | bytes 2359296 | tf_op jit(solution)/shard_map/all_gather | solution.py:56
  184.6 109.9 %all-gather.14.cloned.1.call-start = ((), (), s32[]{:S(2)}) async-start(), calls=%async_computation.14 | async-start | bytes 2359296 | tf_op jit(solution)/shard_map/all_gather | solution.py:56
  187.2 55.5 %copy-start.26 = (f32[768]{0:T(1024)S(1)}, f32[768]{0:T(1024)}, u32[]{:S(2)}) copy-start(f32[768]{0:T(1024)} %param.15) | copy-start | bytes 9220
  245.4 167.1 %reduce-scatter.19.cloned.1.call-start = ((), (), s32[]{:S(2)}) async-start(), calls=%async_computation.19 | async-start | bytes 14155776 | tf_op jit(solution)/shard_map/reduce_scatter | solution.py:64
  270.3 359.8 %reduce-scatter.15.cloned.1.call-start = ((), (), s32[]{:S(2)}) async-start(), calls=%async_computation.15 | async-start | bytes 28311552 | tf_op jit(solution)/shard_map/reduce_scatter | solution.py:64
  311.8 477.6 %all-gather.20.cloned.1.call-start = ((), (), s32[]{:S(2)}) async-start(), calls=%async_computation.20 | async-start | bytes 14155776 | tf_op jit(solution)/shard_map/all_gather | solution.py:60
  663.1 183.4 %reduce-scatter.21.cloned.1.call-start = ((), (), s32[]{:S(2)}) async-start(), calls=%async_computation.21 | async-start | bytes 4718592 | tf_op jit(solution)/shard_map/reduce_scatter | solution.py:73
  801.0 53.3 %copy-start.47 = (f32[512]{0:T(512)S(1)}, f32[512]{0:T(512)}, u32[]{:S(2)}) copy-start(f32[512]{0:T(512)} %copy-done.46) | copy-start | bytes 6148
  801.0 87.8 %all-gather.22.cloned.1.call-start = ((), (), s32[]{:S(2)}) async-start(), calls=%async_computation.22 | async-start | bytes 2359296 | tf_op jit(solution)/shard_map/all_gather | solution.py:56
  856.8 85.4 %reduce-scatter.23.cloned.1.call-start = ((), (), s32[]{:S(2)}) async-start(), calls=%async_computation.23 | async-start | bytes 4718592 | tf_op jit(solution)/shard_map/reduce_scatter | solution.py:64
  893.7 93.2 %reduce-scatter.25.cloned.1.call-start = ((), (), s32[]{:S(2)}) async-start(), calls=%async_computation.24 | async-start | bytes 786432 | tf_op jit(solution)/shard_map/reduce_scatter | solution.py:309
  968.7 39.1 %reduce-scatter.27.cloned.1.call-start = ((), (), s32[]{:S(2)}) async-start(), calls=%async_computation.25 | async-start | bytes 786432 | tf_op jit(solution)/shard_map/reduce_scatter | solution.py:310
  976.4 71.1 %all-gather.24.cloned.1.call-start = ((), (), s32[]{:S(2)}) async-start(), calls=%async_computation.26 | async-start | bytes 3145728 | tf_op jit(solution)/shard_map/all_gather | solution.py:60
  1010.8 104.9 %all-gather.16.cloned.1.call-start = ((), (), s32[]{:S(2)}) async-start(), calls=%async_computation.16 | async-start | bytes 7077888 | tf_op jit(solution)/shard_map/all_gather | solution.py:60
  1011.4 268.4 %reduce-scatter.29.cloned.1.call-start = ((), (), s32[]{:S(2)}) async-start(), calls=%async_computation.27 | async-start | bytes 4718592 | tf_op jit(solution)/shard_map/reduce_scatter | solution.py:73
  1052.7 381.1 %reduce-scatter.17.cloned.1.call-start = ((), (), s32[]{:S(2)}) async-start(), calls=%async_computation.17 | async-start | bytes 4718592 | tf_op jit(solution)/shard_map/reduce_scatter | solution.py:73
  1123.7 314.6 %all-reduce.5.cloned.1.call-start = ((), (), s32[]{:S(2)}) async-start(), calls=%async_computation.28 | async-start | bytes 26738688 | tf_op jit(solution)/shard_map/psum | solution.py:348
  1152.4 127.4 %copy-start.5 = (bf16[512,768]{1,0:T(8,128)(2,1)S(1)}, bf16[512,768]{1,0:T(8,128)(2,1)}, u32[]{:S(2)}) copy-start(bf16[512,768]{1,0:T(8,128)(2,1)} %param.12) | copy-start | bytes 2359300
  1152.4 127.4 %copy-start.32 = (bf16[768,6]{0,1:T(8,128)(2,1)S(1)}, bf16[768,6]{0,1:T(8,128)(2,1)}, u32[]{:S(2)}) copy-start(bf16[768,6]{0,1:T(8,128)(2,1)} %param.18) | copy-start | bytes 27652
  1152.5 127.4 %copy-start.33 = (f32[768]{0:T(1024)S(1)}, f32[768]{0:T(1024)}, u32[]{:S(2)}) copy-start(f32[768]{0:T(1024)} %param.14) | copy-start | bytes 9220
  1152.5 127.4 %copy-start.38 = (f32[512]{0:T(512)S(1)}, f32[512]{0:T(512)}, u32[]{:S(2)}) copy-start(f32[512]{0:T(512)} %copy-done.37) | copy-start | bytes 6148
  1154.9 133.4 %copy-start.43 = (f32[768]{0:T(1024)S(1)}, f32[768]{0:T(1024)}, u32[]{:S(2)}) copy-start(f32[768]{0:T(1024)} %get-tuple-element.119) | copy-start | bytes 9220
  1154.9 278.8 %copy-start.42 = (f32[512]{0:T(512)S(1)}, f32[512]{0:T(512)}, u32[]{:S(2)}) copy-start(f32[512]{0:T(512)} %copy-done.41) | copy-start | bytes 6148
  1154.9 278.8 %copy-start.8 = (bf16[512,768]{1,0:T(8,128)(2,1)S(1)}, bf16[512,768]{1,0:T(8,128)(2,1)}, u32[]{:S(2)}) copy-start(bf16[512,768]{1,0:T(8,128)(2,1)} %param.13) | copy-start | bytes 2359300
  1155.0 278.8 %copy-start.40 = (f32[512]{0:T(512)S(1)}, f32[512]{0:T(512)}, u32[]{:S(2)}) copy-start(f32[512]{0:T(512)} %copy-done.39) | copy-start | bytes 6148
  (52 other events, 469.7 us)
Sparse Core Ops, SparseCore 0:
  17.8 33.3 all-gather.9
  57.0 59.3 reduce-scatter.10
  146.4 32.6 all-gather.11
  184.1 45.2 reduce-scatter.12
  230.9 30.7 all-gather.17
  263.8 30.6 all-gather.13
  296.9 115.5 reduce-scatter.18
  415.0 215.1 reduce-scatter.14
  663.2 126.1 all-gather.19
  801.2 45.2 reduce-scatter.20
  856.9 31.8 all-gather.21
  893.8 48.3 reduce-scatter.22
  968.8 18.0 reduce-scatter.24
  989.7 17.9 reduce-scatter.26
  1010.9 36.5 all-gather.23
  1049.6 66.0 all-gather.15
  1118.5 45.2 reduce-scatter.28
  1166.2 46.8 reduce-scatter.16
  1218.3 138.5 all-reduce.4
where the time goes:
time: 1480 us; the launch traced here: 1470 us
  waiting for transfers between devices  885 us (60%)
  blocking collectives  323 us (22%)
  matrix products  125 us (8%)
  other arithmetic  77.8 us (5%)
  local copies, waits for them, and re-layouts  29 us (2%)
  between operations  15 us (1%)
    reduce_scatter x4, waiting for transfers between devices, reduce_cols(): lax.psum_scatter(term_fn(jnp.int32(0), row_count * lax.axis_size('col')),...  419 us
    all_gather x4, waiting for transfers between devices, collect_cols(): return lax.all_gather(values, 'col', axis=0, tiled=True)  247 us
    psum x1, blocking collectives, local(): lax.psum((attn_gain_part, ffn_gain_part), ('dp', 'row'))  145 us
    psum x1, blocking collectives, local(): lax.psum(router_grad.astype(jnp.bfloat16), 'dp').astype(jnp.float32)  124 us
    all_gather x4, waiting for transfers between devices, collect_rows(): return lax.all_gather(values, 'row', axis=0, tiled=True)  106 us
    reduce_scatter x4, waiting for transfers between devices, reduce_rows(): lax.psum_scatter(term_fn(jnp.int32(0), row_count * lax.axis_size('row')),...  87.6 us
  transfers between devices with their start and end apart: 19, of which 16 were waited for; matrix products, arithmetic and copies ran while one was open for 7% of the time, Pallas kernels for 0%

commit v1 on v0

v1 whole, which is shorter than its diff:
```python
import functools
import math

import jax
import jax.numpy as jnp
from jax import lax
from jax.experimental import pallas as pl
from jax.experimental.pallas import tpu as pltpu
from jax.sharding import PartitionSpec as P

f32 = jnp.float32
bf16 = jnp.bfloat16

HEAD = 128
GROUP_HEADS = 6
EPS = 1e-06
ROPE_BASE = 10000.0
MASKED = -1e30
BLOCK = 256


def flip(v, k):
    return lax.ppermute(v, ("row", "col"), [(i, i ^ k) for i in range(4)])


def gather4(x):
    half = x.shape[0] // 2
    a = flip(x, 2)
    b = flip(x, 3)
    c = jnp.concatenate([flip(b[:half], 2), flip(a[half:], 3)], axis=0)
    return x, c, a, b


def scatter4(p0, p1, p2, p3):
    half = p1.shape[0] // 2
    r2 = flip(p1[:half], 2)
    r3 = flip(p1[half:], 3)
    p3_top = (p3[:half].astype(f32) + r2.astype(f32)).astype(bf16)
    p2_end = (p2[half:].astype(f32) + r3.astype(f32)).astype(bf16)
    o3 = jnp.concatenate([flip(p3_top, 3), flip(p3[half:], 3)], axis=0)
    o2 = jnp.concatenate([flip(p2[:half], 2), flip(p2_end, 2)], axis=0)
    return p0.astype(f32) + o2.astype(f32) + o3.astype(f32)


def scatter_tokens(partial):
    rows, width = partial.shape[0] // 2, partial.shape[1] // 2
    low = partial.astype(bf16)
    return scatter4(
        partial[:rows, :width], low[:rows, width:], low[rows:, :width], low[rows:, width:]
    )


def dp_sizes():
    total = lax.axis_size("dp")
    cores = 2 if total % 2 == 0 else 1
    side = math.isqrt(total // cores)
    return side, side, cores


def dp_place():
    xs, zs, cs = dp_sizes()
    d = lax.axis_index("dp")
    return d // (zs * cs), (d // cs) % zs, d % cs


def shift(v, axis, k):
    xs, zs, cs = dp_sizes()
    pairs = []
    for x in range(xs):
        for z in range(zs):
            for c in range(cs):
                to = [x, z, c]
                to[axis] = (to[axis] + k) % (xs, zs, cs)[axis]
                pairs.append(((x * zs + z) * cs + c, (to[0] * zs + to[1]) * cs + to[2]))
    return lax.ppermute(v, "dp", pairs)


def pick(v, index):
    return lax.dynamic_index_in_dim(v, index, 0, keepdims=False)


def core_sum(part0, part1):
    xs, zs, cs = dp_sizes()
    if cs == 1:
        return jnp.concatenate([part0, part1], axis=0)
    core = dp_place()[2]
    send = jnp.where(core == 0, part1, part0)
    keep = jnp.where(core == 0, part0, part1)
    return (keep.astype(f32) + shift(send, 2, 1).astype(f32)).astype(bf16)


def axis_sum(v, axis):
    n = dp_sizes()[axis]
    place = dp_place()[axis]
    total = pick(v, place).astype(f32)
    for k in range(1, n):
        total = total + shift(pick(v, (place + k) % n), axis, k).astype(f32)
    return total.astype(bf16)


def plane_sums(a, b):
    xs, zs, _ = dp_sizes()
    width = a.shape[-1]
    a = axis_sum(a.reshape(xs, -1, width), 0)
    b = axis_sum(b.reshape(zs, -1, width), 1)
    a = axis_sum(a.reshape(zs, -1, width), 1)
    b = axis_sum(b.reshape(xs, -1, width), 0)
    return a, b


def small_sum(v):
    for axis, n in enumerate(dp_sizes()):
        total = v
        for k in range(1, n):
            total = total + shift(v, axis, k)
        v = total
    return v


def dp_gather(v):
    return lax.all_gather(v, "dp", axis=0, tiled=False).reshape(dp_sizes() + v.shape)


def by_col(col, mine, other, axis):
    return jnp.where(
        col == 0,
        jnp.concatenate([mine, other], axis=axis),
        jnp.concatenate([other, mine], axis=axis),
    )


def window(i, block):
    first = max(0, (i + 1) * block - 512 - block)
    return first, (i + 1) * block


def nt(a, b):
    return lax.dot_general(a, b, (((1,), (1,)), ((), ())), preferred_element_type=f32)


def nn(a, b):
    return lax.dot_general(a, b, (((1,), (0,)), ((), ())), preferred_element_type=f32)


def own_places(ref, out, row, half):
    for h in range(2):
        start = pl.multiple_of(half * jnp.bitwise_xor(row, h), half)
        out[h * half : (h + 1) * half] = ref[pl.ds(start, half)]


def allowed_keys(segk_ref, segq_ref, i, first, last):
    block = BLOCK
    width = last - first
    keys = lax.broadcasted_iota(jnp.int32, (width, block), 0) + first
    queries = lax.broadcasted_iota(jnp.int32, (width, block), 1) + i * block
    same = segk_ref[first:last] == segq_ref[:, i * block : (i + 1) * block]
    return (keys <= queries) & same


def attend_kernel(heads, q_ref, k_ref, v_ref, segk_ref, segq_ref, o_ref, lse_ref, q, k, vt):
    row = lax.axis_index("row")
    total = q_ref.shape[0]
    half = total // 2
    own_places(q_ref, q, row, half)
    own_places(k_ref, k, row, half)
    for h in range(2):
        start = pl.multiple_of(half * jnp.bitwise_xor(row, h), half)
        vt[:, h * half : (h + 1) * half] = v_ref[pl.ds(start, half)].astype(f32).T.astype(bf16)
    for i in range(total // BLOCK):
        first, last = window(i, BLOCK)
        at = slice(i * BLOCK, (i + 1) * BLOCK)
        allowed = allowed_keys(segk_ref, segq_ref, i, first, last)
        place = i * BLOCK // half
        start = pl.multiple_of(
            half * jnp.bitwise_xor(row, place) + (i * BLOCK - place * half), BLOCK
        )
        for h in range(heads):
            s = nt(k[first:last], q[at, h * HEAD : (h + 1) * HEAD]) * (HEAD**-0.5)
            s = jnp.where(allowed, s, MASKED)
            top = jnp.max(s, axis=0, keepdims=True)
            p = jnp.exp(s - top)
            total_p = jnp.sum(p, axis=0, keepdims=True)
            p = (p * (1.0 / total_p)).astype(bf16)
            ot = nn(vt[:, first:last], p)
            o_ref[pl.ds(start, BLOCK), h * HEAD : (h + 1) * HEAD] = ot.T.astype(bf16)
            lse_ref[h : h + 1, at] = top + jnp.log(total_p)


def attend(q, k, v, seg):
    total, width = q.shape
    heads = width // HEAD
    vm = pl.BlockSpec(memory_space=pltpu.VMEM)
    return pl.pallas_call(
        functools.partial(attend_kernel, heads),
        out_shape=(
            jax.ShapeDtypeStruct((total, width), bf16),
            jax.ShapeDtypeStruct((8, total), f32),
        ),
        in_specs=[vm] * 5,
        out_specs=(vm, vm),
        scratch_shapes=[
            pltpu.VMEM((total, width), bf16),
            pltpu.VMEM((total, HEAD), bf16),
            pltpu.VMEM((HEAD, total), bf16),
        ],
        compiler_params=pltpu.CompilerParams(vmem_limit_bytes=32 * 2**20),
        cost_estimate=pl.CostEstimate(
            flops=2 * heads * total * total * HEAD * 2,
            bytes_accessed=6 * total * width,
            transcendentals=heads * total * total,
        ),
        name="attend",
    )(q, k, v, seg.reshape(total, 1), seg.reshape(1, total))


def attend_back_kernel(
    heads,
    q_ref,
    k_ref,
    v_ref,
    do_ref,
    segk_ref,
    segq_ref,
    lse_ref,
    dq_ref,
    dk_ref,
    dv_ref,
    q,
    k,
    v,
    kt,
    do,
    dk,
    dv,
):
    row = lax.axis_index("row")
    total = q_ref.shape[0]
    half = total // 2
    scale = HEAD**-0.5
    own_places(q_ref, q, row, half)
    own_places(k_ref, k, row, half)
    own_places(v_ref, v, row, half)
    own_places(do_ref, do, row, half)
    kt[...] = k[...].astype(f32).T.astype(bf16)
    dk[...] = jnp.zeros_like(dk)
    dv[...] = jnp.zeros_like(dv)
    for i in range(total // BLOCK):
        first, last = window(i, BLOCK)
        at = slice(i * BLOCK, (i + 1) * BLOCK)
        allowed = allowed_keys(segk_ref, segq_ref, i, first, last)
        place = i * BLOCK // half
        start = pl.multiple_of(
            half * jnp.bitwise_xor(row, place) + (i * BLOCK - place * half), BLOCK
        )
        for h in range(heads):
            cols = slice(h * HEAD, (h + 1) * HEAD)
            s = nt(k[first:last], q[at, cols]) * scale
            s = jnp.where(allowed, s, MASKED)
            p = jnp.exp(s - lse_ref[h : h + 1, at])
            dp = nt(v[first:last], do[at, cols])
            inner = jnp.sum(dp * p, axis=0, keepdims=True)
            ds = (p * (dp - inner)).astype(bf16)
            dqt = nn(kt[:, first:last], ds) * scale
            dq_ref[pl.ds(start, BLOCK), cols] = dqt.T
            dk[first:last] += nn(ds, q[at, cols]) * scale
            dv[first:last] += nn(p.astype(bf16), do[at, cols])
    for h in range(2):
        start = pl.multiple_of(half * jnp.bitwise_xor(row, h), half)
        dk_ref[pl.ds(start, half)] = dk[h * half : (h + 1) * half]
        dv_ref[pl.ds(start, half)] = dv[h * half : (h + 1) * half]


def attend_back(q, k, v, do, seg, lse):
    total, width = q.shape
    heads = width // HEAD
    vm = pl.BlockSpec(memory_space=pltpu.VMEM)
    return pl.pallas_call(
        functools.partial(attend_back_kernel, heads),
        out_shape=(
            jax.ShapeDtypeStruct((total, width), f32),
            jax.ShapeDtypeStruct((total, HEAD), f32),
            jax.ShapeDtypeStruct((total, HEAD), f32),
        ),
        in_specs=[vm] * 7,
        out_specs=(vm, vm, vm),
        scratch_shapes=[
            pltpu.VMEM((total, width), bf16),
            pltpu.VMEM((total, HEAD), bf16),
            pltpu.VMEM((total, HEAD), bf16),
            pltpu.VMEM((HEAD, total), bf16),
            pltpu.VMEM((total, width), bf16),
            pltpu.VMEM((total, HEAD), f32),
            pltpu.VMEM((total, HEAD), f32),
        ],
        compiler_params=pltpu.CompilerParams(vmem_limit_bytes=40 * 2**20),
        cost_estimate=pl.CostEstimate(
            flops=5 * heads * total * total * HEAD * 2,
            bytes_accessed=10 * total * width,
            transcendentals=heads * total * total,
        ),
        name="attend_back",
    )(q, k, v, do, seg.reshape(total, 1), seg.reshape(1, total), lse)


def turn_tables(places):
    steps_up = jnp.arange(HEAD // 2, dtype=f32) * (2.0 / HEAD)
    inverse = jnp.exp(-math.log(ROPE_BASE) * steps_up)
    angles = places[:, None] * inverse[None, :]
    cosine, sine = jnp.cos(angles), jnp.sin(angles)
    return (
        jnp.concatenate([cosine, cosine], axis=1)[:, None],
        jnp.concatenate([-sine, sine], axis=1)[:, None],
    )


def swap_halves(v):
    half = v.shape[-1] // 2
    return jnp.concatenate([v[..., half:], v[..., :half]], axis=-1)


def turn(v, cosine, sine):
    return v * cosine + swap_halves(v) * sine


def turn_back(v, cosine, sine):
    return v * cosine - swap_halves(v) * sine


def dot(a, b):
    return jnp.dot(a, b, preferred_element_type=f32)


def local(
    tokens,
    cotangent,
    attn_gain,
    ffn_gain,
    qkv_weight,
    out_weight,
    router_weight,
    gate_weight,
    up_weight,
    down_weight,
    routes,
    segments,
):
    row = lax.axis_index("row")
    col = lax.axis_index("col")
    dp = lax.axis_index("dp")
    dp_count = lax.axis_size("dp")
    xs, zs, cs = dp_sizes()
    own_rows, own_width = tokens.shape
    total = 2 * own_rows
    width = 2 * own_width
    experts, _, hidden = gate_weight.shape
    own_experts = experts // 2
    own_heads = GROUP_HEADS // 2
    head_cols = own_heads * HEAD
    hid = own_experts * hidden
    other_col = 1 - col

    token_blocks = gather4(tokens)
    kv_first = 2 * head_cols

    def qkv_columns(weight, which):
        heads_part = lax.dynamic_slice_in_dim(weight, which * head_cols, head_cols, 1)
        return jnp.concatenate([heads_part, weight[:, kv_first:]], axis=1)

    core = dp_place()[2]
    piece = own_width // cs
    sent = flip(
        qkv_columns(lax.dynamic_slice_in_dim(qkv_weight, core * piece, piece, 0), other_col), 1
    )
    if cs == 2:
        swapped = shift(sent, 2, 1)
        qkv_other = by_col(core, sent, swapped, 0)
    else:
        qkv_other = sent
    qkv_local = jnp.concatenate([qkv_columns(qkv_weight, col), qkv_other], axis=0)
    small = jnp.concatenate(
        [router_weight.T.astype(f32), attn_gain[None], ffn_gain[None]], axis=0
    )
    small = jnp.concatenate([small, flip(small, 1)], axis=1)
    router_local = small[:experts].T.astype(bf16)
    gain_one = small[experts]
    gain_two = small[experts + 1]

    rolled = jnp.where(col == 0, out_weight, jnp.roll(out_weight, head_cols, axis=0))
    share = own_width // dp_count

    def dp_rows(v, count):
        return lax.dynamic_slice_in_dim(v, dp * count, count, v.ndim - 2)

    out_piece = dp_rows(rolled, share)
    out_pieces = jnp.concatenate([flip(out_piece, 1), flip(out_piece, 2), flip(out_piece, 3)], 0)

    def expert_half(v, which):
        return lax.dynamic_slice_in_dim(v, which * own_experts, own_experts, 0)

    gate_up_piece = jnp.concatenate(
        [
            dp_rows(expert_half(gate_weight, other_col), share),
            dp_rows(expert_half(up_weight, other_col), share),
        ],
        axis=2,
    ).reshape(own_experts * share, own_width)
    down_share = hid // dp_count
    down_piece = dp_rows(expert_half(down_weight, other_col).reshape(hid, own_width), down_share)
    expert_pieces = flip(jnp.concatenate([gate_up_piece, down_piece], axis=0), 1)
    gathered = lax.all_gather(
        jnp.concatenate([out_pieces, expert_pieces], axis=0), "dp", axis=0, tiled=False
    )
    out_other = (
        gathered[:, : 3 * share]
        .reshape(dp_count, 3, share, own_width)
        .transpose(1, 0, 2, 3)
        .reshape(3, own_width, own_width)
    )
    gate_up_other = (
        gathered[:, 3 * share : 3 * share + own_experts * share]
        .reshape(dp_count, own_experts, share, own_width)
        .transpose(1, 0, 2, 3)
        .reshape(own_experts, own_width, own_width)
    )
    down_other = gathered[:, (3 + own_experts) * share :].reshape(hid, own_width)

    o1, o2, o3 = out_other[0], out_other[1], out_other[2]
    out_local = jnp.concatenate(
        [
            jnp.concatenate([rolled, o2], axis=0),
            jnp.concatenate(
                [o1[head_cols:], o1[:head_cols], o3[head_cols:], o3[:head_cols]], axis=0
            ),
        ],
        axis=1,
    )
    gate_up_own = jnp.concatenate(
        [expert_half(gate_weight, col), expert_half(up_weight, col)], axis=2
    )
    gate_up_local = jnp.concatenate([gate_up_own, gate_up_other], axis=1)
    down_local = jnp.concatenate(
        [expert_half(down_weight, col).reshape(hid, own_width), down_other], axis=1
    )

    def own_order(v):
        return jnp.where(row == 0, v, jnp.roll(v, own_rows, axis=0))

    seg = segments
    routes_local = own_order(routes)
    places = own_order(jnp.arange(total, dtype=f32))
    cosine, sine = turn_tables(places)

    def two_by_two(blocks):
        return jnp.concatenate(
            [
                jnp.concatenate([blocks[0], blocks[1]], axis=1),
                jnp.concatenate([blocks[2], blocks[3]], axis=1),
            ],
            axis=0,
        )

    tokens_all = two_by_two(token_blocks)
    residual = tokens_all.astype(f32)
    scale_one = lax.rsqrt(jnp.mean(residual * residual, axis=1) + EPS)
    normed_one = (residual * scale_one[:, None] * gain_one).astype(bf16)
    logits = dot(normed_one, router_local)
    chosen = jnp.any(
        routes_local[:, :, None] == jnp.arange(experts, dtype=jnp.int32)[None, None, :], axis=1
    )
    masked = jnp.where(chosen, logits, MASKED)
    raised = jnp.exp(masked - jnp.max(masked, axis=1, keepdims=True))
    gate_values = raised / jnp.sum(raised, axis=1, keepdims=True)
    local_gates = lax.dynamic_slice_in_dim(gate_values, col * own_experts, own_experts, 1)

    projected = dot(normed_one, qkv_local).reshape(total, own_heads + 2, HEAD)
    turned = turn(projected[:, : own_heads + 1], cosine, sine).astype(bf16)
    queries = turned[:, :own_heads].reshape(total, head_cols)
    keys = turned[:, own_heads]
    values = projected[:, own_heads + 1].astype(bf16)
    context, lse = attend(queries, keys, values, seg)

    context_blocks = gather4(context)
    cot_blocks = gather4(cotangent)
    cot_all = two_by_two(cot_blocks)
    context_all = jnp.concatenate(
        [context, context_blocks[1]]
        + [jnp.roll(block, own_rows, axis=0) for block in context_blocks[2:]],
        axis=1,
    )
    mixed = dot(context_all, out_local)
    hidden_in = residual + mixed
    scale_two = lax.rsqrt(jnp.mean(hidden_in * hidden_in, axis=1) + EPS)
    normed_two = (hidden_in * scale_two[:, None] * gain_two).astype(bf16)

    weighted_list, gate_up_grads, gates_parts = [], [], []
    down_experts = down_local.reshape(own_experts, hidden, width)
    for e in range(own_experts):
        gate_up = dot(normed_two, gate_up_local[e])
        gate_pre, up_pre = gate_up[:, :hidden], gate_up[:, hidden:]
        sigmoid_gate = jax.nn.sigmoid(gate_pre)
        silu_gate = gate_pre * sigmoid_gate
        activated = silu_gate * up_pre
        gates = local_gates[:, e : e + 1]
        weighted_list.append((gates * activated).astype(bf16))
        weighted_grad = nt(cot_all, down_experts[e])
        gates_parts.append(jnp.sum(activated * weighted_grad, axis=1))
        activated_grad = gates * weighted_grad
        silu_grad = sigmoid_gate * (1.0 + gate_pre * (1.0 - sigmoid_gate))
        gate_up_grads.append(
            jnp.concatenate(
                [activated_grad * up_pre * silu_grad, activated_grad * silu_gate], axis=1
            ).astype(bf16)
        )
    weighted = jnp.concatenate(weighted_list, axis=1)

    normed_two_part = nt(gate_up_grads[0], gate_up_local[0])
    for e in range(1, own_experts):
        normed_two_part = normed_two_part + nt(gate_up_grads[e], gate_up_local[e])
    normed_two_grad = scatter_tokens(normed_two_part)

    gates_rows = jnp.stack(gates_parts, axis=0)
    gates_rows = gates_rows + jnp.roll(flip(gates_rows, 2), own_rows, axis=1)
    gates_other = flip(gates_rows, 1)
    gates_grad = by_col(col, gates_rows, gates_other, 0).T

    def tn(a, b):
        return lax.dot_general(a, b, (((0,), (0,)), ((), ())), preferred_element_type=f32)

    gate_up_weight_grads = [tn(normed_two, g).astype(bf16) for g in gate_up_grads]
    down_weight_grad = tn(weighted, cot_all).astype(bf16)

    def expert_part(feature_half, which):
        rows = slice(feature_half * own_width, (feature_half + 1) * own_width)
        cols = slice(which * hidden, (which + 1) * hidden)
        first = feature_half * own_width + which * hidden
        gate_or_up = jnp.concatenate([g[rows, cols] for g in gate_up_weight_grads], axis=0)
        down = down_weight_grad[:, first : first + hidden]
        pieces = xs * zs
        return jnp.concatenate(
            [gate_or_up.reshape(pieces, -1, hidden), down.reshape(pieces, -1, hidden)], axis=1
        ).reshape(-1, hidden)

    own_sum = core_sum(expert_part(0, 0), expert_part(0, 1))
    other_sum = core_sum(expert_part(1, 0), expert_part(1, 1))
    own_shard, other_shard = plane_sums(own_sum, other_sum)
    shard_rows = own_shard.shape[0]
    expert_sums = dp_gather(jnp.concatenate([own_shard, flip(other_shard, 1)], axis=0))

    layer_out_part = dot(weighted, down_local)
    layer_out = (hidden_in[:own_rows, :own_width] + scatter_tokens(layer_out_part)).astype(bf16)

    hidden_own = hidden_in[:own_rows, :own_width]
    scale_two_own = scale_two[:own_rows, None]

    def norm_back(grad_normed, values_own, scale, gain):
        scaled = grad_normed * gain
        inner = jnp.sum(scaled * values_own, axis=1)
        inner = (inner + flip(inner, 1))[:, None]
        values_grad = scale * scaled - values_own * (scale * scale * scale * inner / width)
        return values_grad, jnp.sum(grad_normed * values_own * scale, axis=0)

    hidden_norm_grad, ffn_gain_part = norm_back(
        normed_two_grad, hidden_own, scale_two_own, ffn_gain
    )
    hidden_grad = cotangent.astype(f32) + hidden_norm_grad
    hidden_grad_all = two_by_two(gather4(hidden_grad.astype(bf16)))
    out_weight_grad = tn(context, hidden_grad_all).astype(bf16)
    context_grad = nt(hidden_grad_all, out_local[:head_cols]).astype(bf16)

    query_grad, key_grad, value_grad = attend_back(queries, keys, values, context_grad, seg, lse)
    turned_grad = jnp.concatenate(
        [query_grad.reshape(total, own_heads, HEAD), key_grad[:, None]], axis=1
    )
    projected_grad = (
        jnp.concatenate([turn_back(turned_grad, cosine, sine), value_grad[:, None]], axis=1)
        .reshape(total, head_cols + 2 * HEAD)
        .astype(bf16)
    )
    normed_one_grad = scatter_tokens(nt(projected_grad, qkv_local))
    qkv_weight_grad = tn(normed_one, projected_grad).astype(bf16)

    half = own_width // 2

    def attn_part(feature_half, which):
        first = feature_half * own_width + which * half
        return jnp.concatenate(
            [qkv_weight_grad[first : first + half], out_weight_grad[:, first : first + half]],
            axis=1,
        )

    own_attn = core_sum(attn_part(0, 0), attn_part(0, 1))
    other_attn = core_sum(attn_part(1, 0), attn_part(1, 1))
    own_attn, other_attn = plane_sums(own_attn, other_attn)
    attn_sums = dp_gather(jnp.concatenate([own_attn, flip(other_attn, 1)], axis=0))

    logits_grad = (
        gate_values * (gates_grad - jnp.sum(gate_values * gates_grad, axis=1, keepdims=True))
    ).astype(bf16)
    router_grad_rows = tn(logits_grad, normed_one[:, :own_width])
    normed_one_grad = normed_one_grad + dot(logits_grad[:own_rows], router_weight.T)
    input_norm_grad, attn_gain_part = norm_back(
        normed_one_grad, residual[:own_rows, :own_width], scale_one[:own_rows, None], attn_gain
    )
    input_grad = hidden_grad + input_norm_grad
    gain_parts = jnp.stack([attn_gain_part, ffn_gain_part], axis=0)
    gain_parts = gain_parts + flip(gain_parts, 2)
    small_sums = small_sum(jnp.concatenate([router_grad_rows, gain_parts], axis=0))
    router_grad = small_sums[:experts].T
    attn_gain_grad = small_sums[experts]
    ffn_gain_grad = small_sums[experts + 1]

    gate_rows = 2 * shard_rows // 3
    down_rows = shard_rows - gate_rows

    def spread(v, swap):
        v = v.transpose(1, 0, 2, 3) if swap else v
        return v.reshape(-1, v.shape[-1])

    def expert_out(first, count, which):
        which = which % cs
        mine = spread(expert_sums[:, :, which, first : first + count], False)
        other = spread(
            expert_sums[:, :, which, shard_rows + first : shard_rows + first + count], True
        )
        return mine, other

    def gate_or_up(which):
        mine, other = expert_out(0, gate_rows, which)
        shape = (own_experts, own_width, hidden)
        return by_col(col, mine.reshape(shape), other.reshape(shape), 0).astype(f32)

    gate_grad = gate_or_up(0)
    up_grad = gate_or_up(1)
    down_mine, down_other_sum = [
        jnp.concatenate(list(parts), axis=1)
        for parts in zip(expert_out(gate_rows, down_rows, 0), expert_out(gate_rows, down_rows, 1))
    ]
    shape = (own_experts, hidden, own_width)
    down_grad = by_col(col, down_mine.reshape(shape), down_other_sum.reshape(shape), 0).astype(f32)

    attn_rows = own_attn.shape[0]
    qkv_cols = head_cols + 2 * HEAD

    def attn_out(first, swap):
        block = attn_sums[:, :, :, first : first + attn_rows]
        if swap:
            block = block.transpose(1, 0, 2, 3, 4)
        qkv = block[..., :qkv_cols].transpose(2, 0, 1, 3, 4).reshape(own_width, qkv_cols)
        out = block[..., qkv_cols:].transpose(0, 1, 3, 2, 4).reshape(head_cols, own_width)
        return qkv.astype(f32), out.astype(f32)

    qkv_mine, out_mine = attn_out(0, False)
    qkv_peer, out_peer = attn_out(attn_rows, True)
    qkv_grad = jnp.concatenate(
        [
            by_col(col, qkv_mine[:, :head_cols], qkv_peer[:, :head_cols], 1),
            qkv_mine[:, head_cols:] + qkv_peer[:, head_cols:],
        ],
        axis=1,
    )
    out_grad = by_col(col, out_mine, out_peer, 0)
    return (
        layer_out,
        input_grad,
        attn_gain_grad,
        ffn_gain_grad,
        qkv_grad,
        out_grad,
        router_grad,
        gate_grad,
        up_grad,
        down_grad,
    )


def solution(mesh):
    in_specs = (
        P(("dp", "row"), "col"),
        P(("dp", "row"), "col"),
        P("col"),
        P("col"),
        P("col", "row"),
        P("row", "col"),
        P("col", None),
        P(None, "col", "row"),
        P(None, "col", "row"),
        P(None, "row", "col"),
        P("dp", None),
        P("dp"),
    )
    out_specs = (
        P(("dp", "row"), "col"),
        P(("dp", "row"), "col"),
        P("col"),
        P("col"),
        P("col", "row"),
        P("row", "col"),
        P("col", None),
        P(None, "col", "row"),
        P(None, "col", "row"),
        P(None, "row", "col"),
    )
    return jax.shard_map(local, mesh=mesh, in_specs=in_specs, out_specs=out_specs, check_vma=False)
```

time: 1480 us -> 595 us (0.40)
  waiting for transfers between devices: 885 us -> 155 us
  blocking collectives: 323 us -> 0 us
  starting transfers between devices: 12.4 us -> 130 us
  local copies, waits for them, and re-layouts: 29 us -> 88.2 us
  matrix products: 125 us -> 88.7 us
  other arithmetic: 77.8 us -> 94.8 us
    reduce_scatter x10 -> x0, waiting for transfers between devices: 531 us -> none  [the longest x4 419 us: reduce_cols(): lax.psum_scatter(term_fn(jnp.int32(0), row_count * lax.axis_size('col')),...]
    all_gather x8 -> x3, waiting for transfers between devices: 353 us -> 0.01 us  [the longest x2 0.01 us: dp_gather(): lax.all_gather(v, 'dp', axis=0, tiled=False).reshape(dp_sizes() + v.shape)]
    psum x7 -> x0, blocking collectives: 310 us -> none  [the longest x1 145 us: local(): lax.psum((attn_gain_part, ffn_gain_part), ('dp', 'row'))]
    ppermute x0 -> x83, waiting for transfers between devices: none -> 155 us  [the longest x47 110 us: flip(): return lax.ppermute(v, ('row', 'col'), [(i, i ^ k) for i in range(4)])]
    ppermute x0 -> x83, starting transfers between devices: none -> 130 us  [the longest x36 88.3 us: shift(): return lax.ppermute(v, 'dp', pairs)]
    dot_general x24 -> x23, matrix products: 125 us -> 88.7 us  [the longest x8 33.8 us: dot(): return jnp.dot(a, b, preferred_element_type=f32)]
    slice x1 -> x43, local copies, waits for them, and re-layouts: 0.97 us -> 35.5 us  [the longest x2 6.2 us: expert_out(): mine = spread(expert_sums[:, :, which, first:first + count], False)]
    convert_element_type x9 -> x28, other arithmetic: 20.2 us -> 45.9 us  [the longest x1 16.3 us: local(): normed_one = (residual * scale_one[:, None] * gain_one).astype(bf16)]
  transfers between devices with their start and end apart: 19 -> 86, of which waited for: 16 -> 37; matrix products, arithmetic and copies ran while one was open for 7% -> 30% of each run, Pallas kernels for 0% -> 1%
where the time goes in v1:
time: 595 us; the launch traced here: 587 us
  waiting for transfers between devices  155 us (26%)
  starting transfers between devices  130 us (22%)
  other arithmetic  94.8 us (16%)
  matrix products  88.7 us (15%)
  local copies, waits for them, and re-layouts  88.2 us (15%)
  between operations  16.2 us (3%)
  Pallas kernels  14 us (2%)
    ppermute x47, waiting for transfers between devices, flip(): return lax.ppermute(v, ('row', 'col'), [(i, i ^ k) for i in range(4)])  110 us
    ppermute x36, starting transfers between devices, shift(): return lax.ppermute(v, 'dp', pairs)  88.3 us
    ppermute x36, waiting for transfers between devices, shift(): return lax.ppermute(v, 'dp', pairs)  44.5 us
    ppermute x47, starting transfers between devices, flip(): return lax.ppermute(v, ('row', 'col'), [(i, i ^ k) for i in range(4)])  41.9 us
    dot_general x8, matrix products, dot(): return jnp.dot(a, b, preferred_element_type=f32)  33.8 us
    dot_general x8, matrix products, nt(): lax.dot_general(a, b, (((1,), (1,)), ((), ())), preferred_element_type=f32)  30.5 us
    dot_general x7, matrix products, tn(): lax.dot_general(a, b, (((0,), (0,)), ((), ())), preferred_element_type=f32)  24.3 us
    unnamed x246, local copies, waits for them, and re-layouts  21.4 us
  transfers between devices with their start and end apart: 86, of which 37 were waited for; matrix products, arithmetic and copies ran while one was open for 30% of the time, Pallas kernels for 1%

profile of v1, /device:TPU:1, one launch (start us, length us, event | category | flops | bytes accessed | tf_op | source)
XLA Modules:
  0.0 586.8 jit_solution(9047644562140939066)
XLA Ops:
  34.8 18.5 %collective-permute-done.5 = bf16[384,640]{1,0:T(8,128)(2,1)} collective-permute-done((bf16[384,640]{1,0:T(8,128)(2,1)}, bf16[384,640]{1,0:T(8,128)(2,1)}, u32[]{:S(2)}, u32[]{:S(2)}) %collective-permute-start.5) | collective-permute-done | bytes 491552 | tf_op jit(solution)/shard_map/ppermute | solution.py:23
  67.3 10.8 %collective-permute-done.3 = bf16[256,768]{1,0:T(8,128)(2,1)S(1)} collective-permute-done((bf16[256,768]{1,0:T(8,128)(2,1)S(1)}, bf16[256,768]{1,0:T(8,128)(2,1)S(1)}, u32[]{:S(2)}, u32[]{:S(2)}) %collective-permute-start.3) | collective-permute-done | bytes 393248 | tf_op jit(solution)/shard_map/ppermute | solution.py:23
  78.2 12.4 %collective-permute-done.1 = bf16[256,768]{1,0:T(8,128)(2,1)S(1)} collective-permute-done((bf16[256,768]{1,0:T(8,128)(2,1)S(1)}, bf16[256,768]{1,0:T(8,128)(2,1)S(1)}, u32[]{:S(2)}, u32[]{:S(2)}) %collective-permute-start.1) | collective-permute-done | bytes 393248 | tf_op jit(solution)/shard_map/ppermute | solution.py:23
  90.6 10.9 %multiply_reduce_fusion.1 = f32[1024]{0:T(1024)S(1)} fusion(bf16[512,768]{1,0:T(8,128)(2,1)S(1)} %collective-permute-done, bf16[512,768]{1,0:T(8,128)(2,1)S(1)} %collective-permute-done.2, bf16[256,768]{1,0:T(8,128)(2,1)S(1)} %collective-permute-done.3, bf16[256,768]{1,0:T(8,128)(2,1)S(1)} %collective-permute-done.1, bf16[512,768]{1,0:T(8,128)(2,1)S(1)} %copy-done.26), kind=kLoop, calls=%fused_computation.6 | loop fusion | flops 18873344 | bytes 3149824 | tf_op jit(solution)/shard_map/reduce_sum | solution.py:464
  101.6 16.3 %multiply_convert_fusion.1 = bf16[1024,1536]{1,0:T(8,128)(2,1)S(1)} fusion(f32[1536]{0:T(1024)S(1)} %slice_reduce_fusion, f32[1024]{0:T(1024)S(1)} %add_rsqrt_fusion.1, bf16[512,768]{1,0:T(8,128)(2,1)S(1)} %collective-permute-done, bf16[512,768]{1,0:T(8,128)(2,1)S(1)} %collective-permute-done.2, bf16[256,768]{1,0:T(8,128)(2,1)S(1)} %collective-permute-done.3, ...), kind=kLoop, calls=%fused_computation.5 | loop fusion | flops 20447232 | bytes 6301696 | tf_op jit(solution)/shard_map/convert_element_type | solution.py:465
  138.3 6.6 %attend.1 = (bf16[1024,384]{1,0:T(8,128)(2,1)S(1)}, f32[8,1024]{1,0:T(8,128)S(1)}) custom-call(bf16[1024,384]{1,0:T(8,128)(2,1)S(1)} %copy.128.q_ref, bf16[1024,128]{1,0:T(8,128)(2,1)S(1)} %slice_bitcast_fusion.14.k_ref, bf16[1024,128]{1,0:T(8,128)(2,1)S(1)} %bitcast.217, s32[1024,1]{1,0:T(8,128)S(1)} %copy.129.segk_ref, s32[1,1024]{1,0:T(1,128)S(1)} %bitcast.220), custom_call_target="tpu_custom_call" | custom-call | flops 1610612736 | bytes 2359296 | tf_op jit(solution)/shard_map/attend/pallas_call | solution.py:193
  146.6 4.2 constant_dynamic-slice_fusion.3
  155.9 7.5 %collective-permute-done.9 = bf16[1024,384]{1,0:T(8,128)(2,1)S(1)} collective-permute-done((bf16[1024,384]{1,0:T(8,128)(2,1)S(1)}, bf16[1024,384]{1,0:T(8,128)(2,1)S(1)}, u32[]{:S(2)}, u32[]{:S(2)}) %collective-permute-start.9) | collective-permute-done | bytes 786464 | tf_op jit(solution)/shard_map/ppermute | solution.py:23
  172.5 9.4 %collective-permute-done.10 = bf16[512,384]{1,0:T(8,128)(2,1)} collective-permute-done((bf16[512,384]{1,0:T(8,128)(2,1)}, bf16[512,384]{1,0:T(8,128)(2,1)}, u32[]{:S(2)}, u32[]{:S(2)}) %collective-permute-start.10) | collective-permute-done | bytes 393248 | tf_op jit(solution)/shard_map/ppermute | solution.py:23
  182.0 11.2 %multiply_reduce_fusion = (f32[1024]{0:T(1024)S(1)}, f32[1024,1536]{1,0:T(8,128)}) fusion(bf16[384,768]{1,0:T(8,128)(2,1)} %bitcast.292, bf16[384,768]{1,0:T(8,128)(2,1)} %bitcast.294, bf16[384,768]{1,0:T(8,128)(2,1)} %bitcast.296, bf16[384,768]{1,0:T(8,128)(2,1)} %bitcast.290, bf16[768,768]{1,0:T(8,128)(2,1)} %bitcast.284, bf16[768,768]{1,0:T(8,128)(2,1)} %copy-done.69, ...), kind=kOutput, calls=%fused_computation.4 | convolution fusion | flops 4902616064 | bytes 17305600 | tf_op jit(solution)/shard_map/dot_general | solution.py:330
  200.0 4.4 fusion.44
  204.4 4.4 fusion.43
  211.8 5.4 fusion.41
  236.9 4.6 fusion.42
  248.6 4.6 fusion.40
  257.1 6.3 %fusion.155 = (bf16[1024,1536]{1,0:T(8,128)(2,1)S(1)}, f32[1024,1536]{1,0:T(8,128)S(1)}) fusion(bf16[3,1536,768]{2,1,0:T(8,128)(2,1)S(1)} %bitcast.229, bf16[1024,384]{0,1:T(8,128)(2,1)S(1)} %get-tuple-element.46, bf16[1024,384]{0,1:T(8,128)(2,1)S(1)} %get-tuple-element.45, f32[1024,1536]{1,0:T(8,128)} %fusion.40, f32[1024,1536]{1,0:T(8,128)} %fusion.42), kind=kOutput, calls=%fused_computation.344 | convolution fusion | flops 2423783424 | bytes 25952256 | tf_op jit(solution)/shard_map/dot_general | solution.py:138
  268.7 5.8 convolution_convert_fusion
  274.5 4.3 convolution_convert_fusion.3
  303.0 8.2 %collective-permute-done.34 = bf16[512,768]{1,0:T(8,128)(2,1)S(1)} collective-permute-done((bf16[512,768]{1,0:T(8,128)(2,1)S(1)}, bf16[512,768]{1,0:T(8,128)(2,1)S(1)}, u32[]{:S(2)}, u32[]{:S(2)}) %collective-permute-start.34) | collective-permute-done | bytes 786464 | tf_op jit(solution)/shard_map/ppermute | solution.py:23
  315.4 8.2 %collective-permute-done.35 = bf16[256,768]{1,0:T(8,128)(2,1)S(1)} collective-permute-done((bf16[256,768]{1,0:T(8,128)(2,1)S(1)}, bf16[256,768]{1,0:T(8,128)(2,1)S(1)}, u32[]{:S(2)}, u32[]{:S(2)}) %collective-permute-start.35) | collective-permute-done | bytes 393248 | tf_op jit(solution)/shard_map/ppermute | solution.py:23
  325.6 7.4 %attend_back.1 = (f32[1024,384]{1,0:T(8,128)S(1)}, f32[1024,128]{1,0:T(8,128)S(1)}, f32[1024,128]{1,0:T(8,128)S(1)}) custom-call(bf16[1024,384]{1,0:T(8,128)(2,1)S(1)} %copy-done.1, bf16[1024,128]{1,0:T(8,128)(2,1)S(1)} %copy-done.7, bf16[1024,128]{1,0:T(8,128)(2,1)S(1)} %bitcast.218, bf16[1024,384]{1,0:T(8,128)(2,1)S(1)} %convolution_convert_fusion.6.do_ref, ...), custom_call_target="tpu_custom_call" | custom-call | flops 4026531840 | bytes 3932160 | tf_op jit(solution)/shard_map/attend_back/pallas_call | solution.py:277
  348.2 10.1 %collective-permute-start.60 = (bf16[384,1024]{0,1:T(8,128)(2,1)S(1)}, bf16[384,1024]{0,1:T(8,128)(2,1)S(1)}, u32[]{:S(2)}, u32[]{:S(2)}) collective-permute-start(bf16[384,1024]{0,1:T(8,128)(2,1)S(1)} %broadcast_select_fusion.4), channel_id=1, source_target_pairs={{0,4},{4,0},{8,12},{12,8},{16,20},{20,16},{24,28},{28,24},{32,36},... | collective-permute-start | bytes 2359304 | tf_op jit(solution)/shard_map/ppermute | solution.py:75
  393.4 4.1 collective-permute-start.59
  407.0 4.0 collective-permute-start.68
  422.0 10.8 %collective-permute-done.78 = bf16[864,384]{1,0:T(8,128)(2,1)S(1)} collective-permute-done((bf16[864,384]{1,0:T(8,128)(2,1)S(1)}, bf16[864,384]{1,0:T(8,128)(2,1)S(1)}, u32[]{:S(2)}, u32[]{:S(2)}) %collective-permute-start.78) | collective-permute-done | bytes 663584 | tf_op jit(solution)/shard_map/ppermute | solution.py:75
  434.3 15.0 %collective-permute-done.76 = bf16[864,384]{1,0:T(8,128)(2,1)S(1)} collective-permute-done((bf16[864,384]{1,0:T(8,128)(2,1)S(1)}, bf16[864,384]{1,0:T(8,128)(2,1)S(1)}, u32[]{:S(2)}, u32[]{:S(2)}) %collective-permute-start.76) | collective-permute-done | bytes 663584 | tf_op jit(solution)/shard_map/ppermute | solution.py:75
  453.6 4.5 collective-permute-start.74
  458.1 17.8 %collective-permute-start.73 = (bf16[216,384]{1,0:T(8,128)(2,1)S(1)}, bf16[216,384]{1,0:T(8,128)(2,1)S(1)}, u32[]{:S(2)}, u32[]{:S(2)}) collective-permute-start(bf16[216,384]{1,0:T(8,128)(2,1)S(1)} %get-tuple-element.126), channel_id=1, source_target_pairs={{0,16},{4,20},{8,24},{12,28},{16,0},{20,4},{24,8},{28,12},{32,48},... | collective-permute-start | bytes 497672 | tf_op jit(solution)/shard_map/ppermute | solution.py:75
  489.8 4.3 fusion.157
  499.4 6.2 %collective-permute-done.41 = bf16[256,768]{1,0:T(8,128)(2,1)S(1)} collective-permute-done((bf16[256,768]{1,0:T(8,128)(2,1)S(1)}, bf16[256,768]{1,0:T(8,128)(2,1)S(1)}, u32[]{:S(2)}, u32[]{:S(2)}) %collective-permute-start.41) | collective-permute-done | bytes 393248 | tf_op jit(solution)/shard_map/ppermute | solution.py:23
  507.2 6.7 %collective-permute-done.40 = bf16[256,768]{1,0:T(8,128)(2,1)S(1)} collective-permute-done((bf16[256,768]{1,0:T(8,128)(2,1)S(1)}, bf16[256,768]{1,0:T(8,128)(2,1)S(1)}, u32[]{:S(2)}, u32[]{:S(2)}) %collective-permute-start.40) | collective-permute-done | bytes 393248 | tf_op jit(solution)/shard_map/ppermute | solution.py:23
  541.1 7.1 %collective-permute-start.52 = (f32[8,768]{1,0:T(8,128)S(1)}, f32[8,768]{1,0:T(8,128)S(1)}, u32[]{:S(2)}, u32[]{:S(2)}) collective-permute-start(f32[8,768]{1,0:T(8,128)S(1)} %add_add_fusion.1), channel_id=1, source_target_pairs={{0,4},{4,0},{8,12},{12,8},{16,20},{20,16},{24,28},{28,24},{32,36},... | collective-permute-start | bytes 73736 | tf_op jit(solution)/shard_map/ppermute | solution.py:75
  (583 shorter events, 308.6 us)
Async XLA Ops:
  7.2 159.3 %all-gather.12.cloned.1.call-start = ((), (), s32[]{:S(2)}) async-start(), calls=%async_computation.2 | async-start | bytes 9326592 | tf_op jit(solution)/shard_map/all_gather | solution.py:410
  23.6 529.8 %all-gather.8.cloned.1.call-start = ((), (), s32[]{:S(2)}) async-start(), calls=%async_computation | async-start | bytes 3244032 | tf_op jit(solution)/shard_map/all_gather | solution.py:121
  23.7 39.0 %collective-permute-start = (bf16[512,768]{1,0:T(8,128)(2,1)S(1)}, bf16[512,768]{1,0:T(8,128)(2,1)S(1)}, u32[]{:S(2)}, u32[]{:S(2)}) collective-permute-start(bf16[512,768]{1,0:T(8,128)(2,1)S(1)} %copy-done.26), channel_id=1, source_target_pairs={{0,3},{1,2},{2,1},{3,0},{4,7},{5,6},{6,5},{7,4},{8,11},{9,10},{10,... | collective-permute-start | bytes 2359304 | tf_op jit(solution)/shard_map/ppermute | solution.py:23
  25.1 37.4 %collective-permute-start.2 = (bf16[512,768]{1,0:T(8,128)(2,1)S(1)}, bf16[512,768]{1,0:T(8,128)(2,1)S(1)}, u32[]{:S(2)}, u32[]{:S(2)}) collective-permute-start(bf16[512,768]{1,0:T(8,128)(2,1)S(1)} %copy-done.26), channel_id=1, source_target_pairs={{0,2},{1,3},{2,0},{3,1},{4,6},{5,7},{6,4},{7,5},{8,10},{9,11},{10,... | collective-permute-start | bytes 2359304 | tf_op jit(solution)/shard_map/ppermute | solution.py:23
  28.9 24.4 %collective-permute-start.5 = (bf16[384,640]{1,0:T(8,128)(2,1)}, bf16[384,640]{1,0:T(8,128)(2,1)}, u32[]{:S(2)}, u32[]{:S(2)}) collective-permute-start(bf16[384,640]{1,0:T(8,128)(2,1)} %pad_maximum_fusion.35), channel_id=1, source_target_pairs={{0,1},{1,0},{2,3},{3,2},{4,5},{5,4},{6,7},{7,6},{8,9},{9,8},{10,11... | collective-permute-start | bytes 1474568 | tf_op jit(solution)/shard_map/ppermute | solution.py:23
  30.7 33.6 %collective-permute-start.4 = (f32[8,768]{1,0:T(8,128)S(1)}, f32[8,768]{1,0:T(8,128)S(1)}, u32[]{:S(2)}, u32[]{:S(2)}) collective-permute-start(f32[8,768]{1,0:T(8,128)S(1)} %pad_maximum_fusion.41), channel_id=1, source_target_pairs={{0,1},{1,0},{2,3},{3,2},{4,5},{5,4},{6,7},{7,6},{8,9},{9,8},{10,11... | collective-permute-start | bytes 73736 | tf_op jit(solution)/shard_map/ppermute | solution.py:23
  32.0 122.1 %collective-permute-start.21 = (bf16[512,768]{1,0:T(8,128)(2,1)}, bf16[512,768]{1,0:T(8,128)(2,1)}, u32[]{:S(2)}, u32[]{:S(2)}) collective-permute-start(bf16[512,768]{1,0:T(8,128)(2,1)} %param.13), channel_id=1, source_target_pairs={{0,3},{1,2},{2,1},{3,0},{4,7},{5,6},{6,5},{7,4},{8,11},{9,10},{10,... | collective-permute-start | bytes 2359304 | tf_op jit(solution)/shard_map/ppermute | solution.py:23
  62.6 88.3 %collective-permute-start.23 = (bf16[512,768]{1,0:T(8,128)(2,1)}, bf16[512,768]{1,0:T(8,128)(2,1)}, u32[]{:S(2)}, u32[]{:S(2)}) collective-permute-start(bf16[512,768]{1,0:T(8,128)(2,1)} %param.13), channel_id=1, source_target_pairs={{0,2},{1,3},{2,0},{3,1},{4,6},{5,7},{6,4},{7,5},{8,10},{9,11},{10,... | collective-permute-start | bytes 2359304 | tf_op jit(solution)/shard_map/ppermute | solution.py:23
  64.3 26.2 %collective-permute-start.1 = (bf16[256,768]{1,0:T(8,128)(2,1)S(1)}, bf16[256,768]{1,0:T(8,128)(2,1)S(1)}, u32[]{:S(2)}, u32[]{:S(2)}) collective-permute-start(bf16[256,768]{1,0:T(8,128)(2,1)S(1)} %slice.582), channel_id=1, source_target_pairs={{0,2},{1,3},{2,0},{3,1},{4,6},{5,7},{6,4},{7,5},{8,10},{9,11},{10,... | collective-permute-start | bytes 1179656 | tf_op jit(solution)/shard_map/ppermute | solution.py:23
  145.0 18.5 %collective-permute-start.9 = (bf16[1024,384]{1,0:T(8,128)(2,1)S(1)}, bf16[1024,384]{1,0:T(8,128)(2,1)S(1)}, u32[]{:S(2)}, u32[]{:S(2)}) collective-permute-start(bf16[1024,384]{1,0:T(8,128)(2,1)S(1)} %get-tuple-element.15), channel_id=1, source_target_pairs={{0,2},{1,3},{2,0},{3,1},{4,6},{5,7},{6,4},{7,5},{8,10},{9,11},{10,... | collective-permute-start | bytes 2359304 | tf_op jit(solution)/shard_map/ppermute | solution.py:23
  145.4 20.2 %collective-permute-start.7 = (bf16[1024,384]{1,0:T(8,128)(2,1)S(1)}, bf16[1024,384]{1,0:T(8,128)(2,1)S(1)}, u32[]{:S(2)}, u32[]{:S(2)}) collective-permute-start(bf16[1024,384]{1,0:T(8,128)(2,1)S(1)} %get-tuple-element.15), channel_id=1, source_target_pairs={{0,3},{1,2},{2,1},{3,0},{4,7},{5,6},{6,5},{7,4},{8,11},{9,10},{10,... | collective-permute-start | bytes 2359304 | tf_op jit(solution)/shard_map/ppermute | solution.py:23
  152.6 64.5 %collective-permute-start.24 = (bf16[256,768]{1,0:T(8,128)(2,1)}, bf16[256,768]{1,0:T(8,128)(2,1)}, u32[]{:S(2)}, u32[]{:S(2)}) collective-permute-start(bf16[256,768]{1,0:T(8,128)(2,1)} %slice.622), channel_id=1, source_target_pairs={{0,3},{1,2},{2,1},{3,0},{4,7},{5,6},{6,5},{7,4},{8,11},{9,10},{10,... | collective-permute-start | bytes 1179656 | tf_op jit(solution)/shard_map/ppermute | solution.py:23
  155.9 61.3 %collective-permute-start.22 = (bf16[256,768]{1,0:T(8,128)(2,1)}, bf16[256,768]{1,0:T(8,128)(2,1)}, u32[]{:S(2)}, u32[]{:S(2)}) collective-permute-start(bf16[256,768]{1,0:T(8,128)(2,1)} %slice.621), channel_id=1, source_target_pairs={{0,2},{1,3},{2,0},{3,1},{4,6},{5,7},{6,4},{7,5},{8,10},{9,11},{10,... | collective-permute-start | bytes 1179656 | tf_op jit(solution)/shard_map/ppermute | solution.py:23
  164.4 17.5 %collective-permute-start.10 = (bf16[512,384]{1,0:T(8,128)(2,1)}, bf16[512,384]{1,0:T(8,128)(2,1)}, u32[]{:S(2)}, u32[]{:S(2)}) collective-permute-start(bf16[512,384]{1,0:T(8,128)(2,1)} %get-tuple-element.120), channel_id=1, source_target_pairs={{0,3},{1,2},{2,1},{3,0},{4,7},{5,6},{6,5},{7,4},{8,11},{9,10},{10,... | collective-permute-start | bytes 1179656 | tf_op jit(solution)/shard_map/ppermute | solution.py:23
  264.3 22.0 %collective-permute-start.30 = (bf16[256,768]{1,0:T(8,128)(2,1)S(1)}, bf16[256,768]{1,0:T(8,128)(2,1)}, u32[]{:S(2)}, u32[]{:S(2)}) collective-permute-start(bf16[256,768]{1,0:T(8,128)(2,1)S(1)} %get-tuple-element.71), channel_id=1, source_target_pairs={{0,3},{1,2},{2,1},{3,0},{4,7},{5,6},{6,5},{7,4},{8,11},{9,10},{10,... | collective-permute-start | bytes 1179656 | tf_op jit(solution)/shard_map/ppermute | solution.py:23
  267.2 19.1 %collective-permute-start.25 = (bf16[256,768]{1,0:T(8,128)(2,1)S(1)}, bf16[256,768]{1,0:T(8,128)(2,1)}, u32[]{:S(2)}, u32[]{:S(2)}) collective-permute-start(bf16[256,768]{1,0:T(8,128)(2,1)S(1)} %get-tuple-element.70), channel_id=1, source_target_pairs={{0,2},{1,3},{2,0},{3,1},{4,6},{5,7},{6,4},{7,5},{8,10},{9,11},{10,... | collective-permute-start | bytes 1179656 | tf_op jit(solution)/shard_map/ppermute | solution.py:23
  360.4 50.5 %collective-permute-start.75 = (bf16[3456,384]{1,0:T(8,128)(2,1)}, bf16[3456,384]{1,0:T(8,128)(2,1)}, u32[]{:S(2)}, u32[]{:S(2)}) collective-permute-start(bf16[3456,384]{1,0:T(8,128)(2,1)} %bitcast.86), channel_id=1, source_target_pairs={{0,4},{4,0},{8,12},{12,8},{16,20},{20,16},{24,28},{28,24},{32,36},... | collective-permute-start | bytes 7962632 | tf_op jit(solution)/shard_map/ppermute | solution.py:75
  403.6 159.7 %all-gather.10.cloned.1.call-start = ((), (), s32[]{:S(2)}) async-start(), calls=%async_computation.1 | async-start | bytes 10948608 | tf_op jit(solution)/shard_map/all_gather | solution.py:121
  413.6 19.3 %collective-permute-start.78 = (bf16[864,384]{1,0:T(8,128)(2,1)S(1)}, bf16[864,384]{1,0:T(8,128)(2,1)S(1)}, u32[]{:S(2)}, u32[]{:S(2)}) collective-permute-start(bf16[864,384]{1,0:T(8,128)(2,1)S(1)} %get-tuple-element.86), channel_id=1, source_target_pairs={{0,24},{4,28},{8,0},{12,4},{16,8},{20,12},{24,16},{28,20},{32,56},... | collective-permute-start | bytes 1990664 | tf_op jit(solution)/shard_map/ppermute | solution.py:75
  415.8 18.6 %collective-permute-start.77 = (bf16[864,384]{1,0:T(8,128)(2,1)S(1)}, bf16[864,384]{1,0:T(8,128)(2,1)S(1)}, u32[]{:S(2)}, u32[]{:S(2)}) collective-permute-start(bf16[864,384]{1,0:T(8,128)(2,1)S(1)} %get-tuple-element.87), channel_id=1, source_target_pairs={{0,16},{4,20},{8,24},{12,28},{16,0},{20,4},{24,8},{28,12},{32,48},... | collective-permute-start | bytes 1990664 | tf_op jit(solution)/shard_map/ppermute | solution.py:75
  417.7 31.6 %collective-permute-start.76 = (bf16[864,384]{1,0:T(8,128)(2,1)S(1)}, bf16[864,384]{1,0:T(8,128)(2,1)S(1)}, u32[]{:S(2)}, u32[]{:S(2)}) collective-permute-start(bf16[864,384]{1,0:T(8,128)(2,1)S(1)} %get-tuple-element.85), channel_id=1, source_target_pairs={{0,8},{4,12},{8,16},{12,20},{16,24},{20,28},{24,0},{28,4},{32,40},... | collective-permute-start | bytes 1990664 | tf_op jit(solution)/shard_map/ppermute | solution.py:75
  419.0 33.9 %collective-permute-start.71 = (bf16[864,384]{1,0:T(8,128)(2,1)S(1)}, bf16[864,384]{1,0:T(8,128)(2,1)S(1)}, u32[]{:S(2)}, u32[]{:S(2)}) collective-permute-start(bf16[864,384]{1,0:T(8,128)(2,1)S(1)} %get-tuple-element.83), channel_id=1, source_target_pairs={{0,96},{4,100},{8,104},{12,108},{16,112},{20,116},{24,120},{28,124... | collective-permute-start | bytes 1990664 | tf_op jit(solution)/shard_map/ppermute | solution.py:75
  419.3 33.8 %collective-permute-start.70 = (bf16[864,384]{1,0:T(8,128)(2,1)S(1)}, bf16[864,384]{1,0:T(8,128)(2,1)S(1)}, u32[]{:S(2)}, u32[]{:S(2)}) collective-permute-start(bf16[864,384]{1,0:T(8,128)(2,1)S(1)} %get-tuple-element.84), channel_id=1, source_target_pairs={{0,64},{4,68},{8,72},{12,76},{16,80},{20,84},{24,88},{28,92},{32,9... | collective-permute-start | bytes 1990664 | tf_op jit(solution)/shard_map/ppermute | solution.py:75
  432.9 20.2 %collective-permute-start.69 = (bf16[864,384]{1,0:T(8,128)(2,1)S(1)}, bf16[864,384]{1,0:T(8,128)(2,1)S(1)}, u32[]{:S(2)}, u32[]{:S(2)}) collective-permute-start(bf16[864,384]{1,0:T(8,128)(2,1)S(1)} %get-tuple-element.82), channel_id=1, source_target_pairs={{0,32},{4,36},{8,40},{12,44},{16,48},{20,52},{24,56},{28,60},{32,6... | collective-permute-start | bytes 1990664 | tf_op jit(solution)/shard_map/ppermute | solution.py:75
  449.8 26.1 %collective-permute-start.81 = (bf16[216,384]{1,0:T(8,128)(2,1)S(1)}, bf16[216,384]{1,0:T(8,128)(2,1)S(1)}, u32[]{:S(2)}, u32[]{:S(2)}) collective-permute-start(bf16[216,384]{1,0:T(8,128)(2,1)S(1)} %get-tuple-element.128), channel_id=1, source_target_pairs={{0,96},{4,100},{8,104},{12,108},{16,112},{20,116},{24,120},{28,124... | collective-permute-start | bytes 497672 | tf_op jit(solution)/shard_map/ppermute | solution.py:75
  450.6 25.3 %collective-permute-start.80 = (bf16[216,384]{1,0:T(8,128)(2,1)S(1)}, bf16[216,384]{1,0:T(8,128)(2,1)S(1)}, u32[]{:S(2)}, u32[]{:S(2)}) collective-permute-start(bf16[216,384]{1,0:T(8,128)(2,1)S(1)} %get-tuple-element.129), channel_id=1, source_target_pairs={{0,64},{4,68},{8,72},{12,76},{16,80},{20,84},{24,88},{28,92},{32,9... | collective-permute-start | bytes 497672 | tf_op jit(solution)/shard_map/ppermute | solution.py:75
  452.9 23.0 %collective-permute-start.79 = (bf16[216,384]{1,0:T(8,128)(2,1)S(1)}, bf16[216,384]{1,0:T(8,128)(2,1)S(1)}, u32[]{:S(2)}, u32[]{:S(2)}) collective-permute-start(bf16[216,384]{1,0:T(8,128)(2,1)S(1)} %get-tuple-element.127), channel_id=1, source_target_pairs={{0,32},{4,36},{8,40},{12,44},{16,48},{20,52},{24,56},{28,60},{32,6... | collective-permute-start | bytes 497672 | tf_op jit(solution)/shard_map/ppermute | solution.py:75
  453.6 23.2 %collective-permute-start.74 = (bf16[216,384]{1,0:T(8,128)(2,1)S(1)}, bf16[216,384]{1,0:T(8,128)(2,1)S(1)}, u32[]{:S(2)}, u32[]{:S(2)}) collective-permute-start(bf16[216,384]{1,0:T(8,128)(2,1)S(1)} %get-tuple-element.125), channel_id=1, source_target_pairs={{0,24},{4,28},{8,0},{12,4},{16,8},{20,12},{24,16},{28,20},{32,56},... | collective-permute-start | bytes 497672 | tf_op jit(solution)/shard_map/ppermute | solution.py:75
  458.1 20.5 %collective-permute-start.73 = (bf16[216,384]{1,0:T(8,128)(2,1)S(1)}, bf16[216,384]{1,0:T(8,128)(2,1)S(1)}, u32[]{:S(2)}, u32[]{:S(2)}) collective-permute-start(bf16[216,384]{1,0:T(8,128)(2,1)S(1)} %get-tuple-element.126), channel_id=1, source_target_pairs={{0,16},{4,20},{8,24},{12,28},{16,0},{20,4},{24,8},{28,12},{32,48},... | collective-permute-start | bytes 497672 | tf_op jit(solution)/shard_map/ppermute | solution.py:75
  498.5 17.1 %collective-permute-start.38 = (bf16[256,768]{1,0:T(8,128)(2,1)S(1)}, bf16[256,768]{1,0:T(8,128)(2,1)S(1)}, u32[]{:S(2)}, u32[]{:S(2)}) collective-permute-start(bf16[256,768]{1,0:T(8,128)(2,1)S(1)} %get-tuple-element.65), channel_id=1, source_target_pairs={{0,2},{1,3},{2,0},{3,1},{4,6},{5,7},{6,4},{7,5},{8,10},{9,11},{10,... | collective-permute-start | bytes 1179656 | tf_op jit(solution)/shard_map/ppermute | solution.py:23
  523.2 25.0 %collective-permute-start.20 = (bf16[256,768]{1,0:T(8,128)(2,1)S(1)}, bf16[256,768]{1,0:T(8,128)(2,1)S(1)}, u32[]{:S(2)}, u32[]{:S(2)}) collective-permute-start(bf16[256,768]{1,0:T(8,128)(2,1)S(1)} %get-tuple-element.79), channel_id=1, source_target_pairs={{0,3},{1,2},{2,1},{3,0},{4,7},{5,6},{6,5},{7,4},{8,11},{9,10},{10,... | collective-permute-start | bytes 1179656 | tf_op jit(solution)/shard_map/ppermute | solution.py:23
  524.7 23.5 %collective-permute-start.15 = (bf16[256,768]{1,0:T(8,128)(2,1)S(1)}, bf16[256,768]{1,0:T(8,128)(2,1)S(1)}, u32[]{:S(2)}, u32[]{:S(2)}) collective-permute-start(bf16[256,768]{1,0:T(8,128)(2,1)S(1)} %get-tuple-element.81), channel_id=1, source_target_pairs={{0,2},{1,3},{2,0},{3,1},{4,6},{5,7},{6,4},{7,5},{8,10},{9,11},{10,... | collective-permute-start | bytes 1179656 | tf_op jit(solution)/shard_map/ppermute | solution.py:23
  (175 other events, 2096.7 us)
Sparse Core Ops, SparseCore 0:
  23.7 58.9 all-gather.11
  403.7 72.1 all-gather.7
  483.4 61.4 all-gather.9

commit v2 on v1

v2 whole, which is shorter than its diff:
```python
import functools
import math

import jax
import jax.numpy as jnp
from jax import lax
from jax.experimental import pallas as pl
from jax.experimental.pallas import tpu as pltpu
from jax.sharding import PartitionSpec as P

f32 = jnp.float32
bf16 = jnp.bfloat16

HEAD = 128
GROUP_HEADS = 6
EPS = 1e-06
ROPE_BASE = 10000.0
MASKED = -1e30
BLOCK = 256


MESH = pl.DeviceIdType.MESH
VMEM = pltpu.VMEM
ANY = pl.BlockSpec(memory_space=pl.ANY)
WHOLE = pl.BlockSpec(memory_space=pltpu.VMEM)
HALF = 512
SIDE = 384


def flip(v, k):
    return lax.ppermute(v, ("row", "col"), [(i, i ^ k) for i in range(4)])


def dp_sizes():
    total = lax.axis_size("dp")
    cores = 2 if total % 2 == 0 else 1
    side = math.isqrt(total // cores)
    return side, side, cores


def dp_place():
    xs, zs, cs = dp_sizes()
    d = lax.axis_index("dp")
    return d // (zs * cs), (d // cs) % zs, d % cs


def by_col(col, mine, other, axis):
    return jnp.where(
        col == 0,
        jnp.concatenate([mine, other], axis=axis),
        jnp.concatenate([other, mine], axis=axis),
    )


def nt(a, b):
    return lax.dot_general(a, b, (((1,), (1,)), ((), ())), preferred_element_type=f32)


def nn(a, b):
    return lax.dot_general(a, b, (((1,), (0,)), ((), ())), preferred_element_type=f32)


def tn(a, b):
    return lax.dot_general(a, b, (((0,), (0,)), ((), ())), preferred_element_type=f32)


class Links:
    def __init__(self, send, recv):
        self.send, self.recv = send, recv
        self.used = 0
        self.dp = lax.axis_index("dp")
        self.row = lax.axis_index("row")
        self.col = lax.axis_index("col")
        self.xs, self.zs, self.cs = dp_sizes()
        self.x, self.z, self.core = dp_place()

    def group(self, k):
        row = 1 - self.row if k & 2 else self.row
        col = 1 - self.col if k & 1 else self.col
        return (self.dp, row, col)

    def other_core(self):
        return (self.dp + 1 - 2 * self.core, self.row, self.col)

    def place(self, axis, k):
        x, z = self.x, self.z
        if axis == 0:
            x = (x + k) % self.xs
        else:
            z = (z + k) % self.zs
        return ((x * self.zs + z) * self.cs + self.core, self.row, self.col)

    def greet(self, devices):
        barrier = pltpu.get_barrier_semaphore()
        for device in devices:
            pl.semaphore_signal(barrier, inc=1, device_id=device, device_id_type=MESH)
        pl.semaphore_wait(barrier, len(devices))

    def plane(self):
        return (
            ([self.other_core()] if self.cs == 2 else [])
            + [self.place(0, k) for k in range(1, self.xs)]
            + [self.place(1, k) for k in range(1, self.zs)]
        )

    def copy(self, src, dst, device):
        i = self.used
        self.used += 1
        return pltpu.make_async_remote_copy(
            src_ref=src,
            dst_ref=dst,
            send_sem=self.send.at[i],
            recv_sem=self.recv.at[i],
            device_id=device,
            device_id_type=MESH,
        )

    def go(self, src, dst, device):
        copy = self.copy(src, dst, device)
        copy.start()
        return copy


def at(start, size, step=16):
    return pl.ds(pl.multiple_of(start, step), size)


def gather_group(links, own, dst, wide):
    quarter = HALF // 2
    first = {}
    for k, order in ((2, (1, 0)), (3, (0, 1))):
        for h in order:
            first[k, h] = links.copy(own(h), dst(k, h), links.group(k))
    for key in ((2, 1), (3, 0), (2, 0), (3, 1)):
        first[key].start()
    relay = [
        links.copy(dst(3, 0), dst(1, 0), links.group(2)),
        links.copy(dst(2, 1), dst(1, 1), links.group(3)),
    ]

    def forward():
        first[3, 0].wait_recv()
        relay[0].start()
        first[2, 1].wait_recv()
        relay[1].start()

    def finish():
        first[2, 0].wait_recv()
        first[3, 1].wait_recv()
        for copy in relay:
            copy.wait()
        for copy in first.values():
            copy.wait_send()

    return forward, finish


def gather_inputs_kernel(
    tokens, qkv_weight, small, tokens_all, qkv_all, small_all, send, recv, local
):
    links = Links(send, recv)
    group = [links.group(k) for k in (1, 2, 3)]
    zs, cs = links.zs, links.cs
    links.greet(
        group
        + ([links.other_core()] if cs == 2 else [])
        + [links.place(1, k) for k in range(1, zs)]
    )
    width = tokens.shape[1]
    quarter = HALF // 2

    def own(h):
        return tokens.at[h * quarter : (h + 1) * quarter]

    def dst(k, h):
        rows = (HALF if k & 2 else 0) + h * quarter
        return tokens_all.at[rows : rows + quarter, (k & 1) * width : (k & 1) * width + width]

    share = width // (cs * zs)
    start = links.core * (width // cs) + links.z * share
    theirs = (1 - links.col) * SIDE
    rows = at(start, share)
    there = at(width + start, share)
    fetch = [
        links.copy(
            qkv_weight.at[rows, at(theirs, SIDE, 128)],
            qkv_all.at[there, 0:SIDE],
            links.group(1),
        ),
        links.copy(
            qkv_weight.at[rows, 2 * SIDE :], qkv_all.at[there, SIDE:], links.group(1)
        ),
    ]
    for copy in fetch:
        copy.start()
    little = links.go(small, small_all.at[:, width:], links.group(1))
    forward, finish = gather_group(links, own, dst, width)
    locals_ = [
        pltpu.make_async_copy(tokens, tokens_all.at[0:HALF, 0:width], local.at[0]),
        pltpu.make_async_copy(
            qkv_weight.at[:, at(links.col * SIDE, SIDE, 128)],
            qkv_all.at[0:width, 0:SIDE],
            local.at[1],
        ),
        pltpu.make_async_copy(
            qkv_weight.at[:, 2 * SIDE :], qkv_all.at[0:width, SIDE:], local.at[2]
        ),
        pltpu.make_async_copy(small, small_all.at[:, 0:width], local.at[3]),
    ]
    for copy in locals_:
        copy.start()
    for copy in fetch:
        copy.wait()
    spread = [
        links.go(qkv_all.at[there], qkv_all.at[there], links.place(1, k)) for k in range(1, zs)
    ]
    forward()
    for copy in spread:
        copy.wait()
    if cs == 2:
        block = qkv_all.at[at(width + links.core * (width // 2), width // 2)]
        links.go(block, block, links.other_core()).wait()
    little.wait()
    for copy in locals_:
        copy.wait()
    finish()


def gather_inputs(tokens, qkv_weight, small):
    width = tokens.shape[1]
    return pl.pallas_call(
        gather_inputs_kernel,
        out_shape=(
            jax.ShapeDtypeStruct((2 * HALF, 2 * width), bf16),
            jax.ShapeDtypeStruct((2 * width, SIDE + 2 * HEAD), bf16),
            jax.ShapeDtypeStruct((8, 2 * width), f32),
        ),
        in_specs=[ANY] * 3,
        out_specs=(ANY,) * 3,
        scratch_shapes=[
            pltpu.SemaphoreType.DMA((16,)),
            pltpu.SemaphoreType.DMA((16,)),
            pltpu.SemaphoreType.DMA((4,)),
        ],
        compiler_params=pltpu.CompilerParams(collective_id=0, has_side_effects=True),
        name="gather_inputs",
    )(tokens, qkv_weight, small)


def gather_context_kernel(context, context_all, send, recv, local):
    links = Links(send, recv)
    links.greet([links.group(k) for k in (1, 2, 3)])
    width = context.shape[1]

    def block(k, h):
        return context_all.at[h * HALF : (h + 1) * HALF, k * width : (k + 1) * width]

    mine = pltpu.make_async_copy(context, context_all.at[:, 0:width], local)
    mine.start()
    first = {}
    for k, h in ((2, 0), (3, 1), (2, 1), (3, 0)):
        first[k, 1 - h] = links.go(
            context.at[h * HALF : (h + 1) * HALF], block(k, 1 - h), links.group(k)
        )
    first[3, 0].wait_recv()
    relay = [links.go(block(3, 0), block(1, 1), links.group(2))]
    first[2, 1].wait_recv()
    relay.append(links.go(block(2, 1), block(1, 0), links.group(3)))
    mine.wait()
    first[2, 0].wait_recv()
    first[3, 1].wait_recv()
    for copy in relay:
        copy.wait()
    for copy in first.values():
        copy.wait_send()


def gather_context(context):
    rows, width = context.shape
    return pl.pallas_call(
        gather_context_kernel,
        out_shape=jax.ShapeDtypeStruct((rows, 4 * width), bf16),
        in_specs=[ANY],
        out_specs=ANY,
        scratch_shapes=[
            pltpu.SemaphoreType.DMA((6,)),
            pltpu.SemaphoreType.DMA((6,)),
            pltpu.SemaphoreType.DMA,
        ],
        compiler_params=pltpu.CompilerParams(collective_id=1, has_side_effects=True),
        name="gather_context",
    )(context)


def scatter_group(links, partial, near2, near3, far2, far3, out2, out3):
    width = partial.shape[1] // 2
    quarter = HALF // 2
    n2, n3 = links.group(2), links.group(3)
    start = [
        links.go(partial.at[0:quarter, width:], near2, n2),
        links.go(partial.at[quarter:HALF, width:], near3, n3),
    ]
    direct = [
        links.go(partial.at[HALF + quarter :, width:], far3.at[quarter:], n3),
        links.go(partial.at[HALF : HALF + quarter, 0:width], far2.at[0:quarter], n2),
    ]
    relay = [
        links.copy(out3, far3.at[0:quarter], n3),
        links.copy(out2, far2.at[quarter:], n2),
    ]

    def forward():
        start[0].wait_recv()
        out3[...] = (
            partial[HALF : HALF + quarter, width:].astype(f32) + near2[...].astype(f32)
        ).astype(bf16)
        relay[0].start()
        start[1].wait_recv()
        out2[...] = (
            partial[HALF + quarter :, 0:width].astype(f32) + near3[...].astype(f32)
        ).astype(bf16)
        relay[1].start()

    def finish():
        for copy in direct:
            copy.wait_recv()
        for copy in relay:
            copy.wait_recv()

    def total(rows):
        return (
            partial[rows, 0:width].astype(f32)
            + far2[rows].astype(f32)
            + far3[rows].astype(f32)
        )

    def sent():
        for copy in start + direct + relay:
            copy.wait_send()

    return forward, finish, total, sent


def norm_back_rows(grad, gain, values, scale, inner, width):
    return scale * (grad * gain - values * (scale * inner * (1.0 / width)))


def column(row_vector):
    return jnp.broadcast_to(row_vector, (128, row_vector.shape[1])).T


def half_swap(v):
    return jnp.concatenate([v[:, HALF:], v[:, :HALF]], axis=1)


def add_rows(out, a, b, total_rows, step):
    @pl.loop(0, total_rows // step)
    def _(i):
        rows = at(i * step, step, 16)
        out[rows] = (a[rows].astype(f32) + b[rows].astype(f32)).astype(bf16)


def reduce_kernel(
    partial,
    vectors,
    hidden,
    cot,
    scale,
    gain,
    gate_up,
    down,
    hidden_grad,
    hidden_low,
    vector_sums,
    gain_part,
    shard_up,
    shard_down,
    near2,
    near3,
    far2,
    far3,
    out2,
    out3,
    vec_in,
    low,
    core_up,
    core_down,
    sum_up,
    sum_down,
    in_up,
    in_down,
    part_up,
    part_down,
    in2_up,
    in2_down,
    peer_up,
    peer_down,
    send,
    recv,
    local,
):
    links = Links(send, recv)
    xs, zs, cs = links.xs, links.zs, links.cs
    sizes = (xs, zs)
    places = (links.x, links.z)
    links.greet([links.group(k) for k in (1, 2, 3)] + links.plane())
    width = partial.shape[1] // 2
    quarter = HALF // 2
    forward, finish, total, sent = scatter_group(
        links, partial, near2, near3, far2, far3, out2, out3
    )
    vec_copies = [links.go(vectors, vec_in.at[k - 1], links.group(k)) for k in (1, 2, 3)]
    core_copies = []
    if cs == 2:
        for ab in range(2):
            core_copies.append(
                (
                    links.go(
                        gate_up.at[1 - links.core, ab], core_up.at[ab], links.other_core()
                    ),
                    links.go(
                        down.at[1 - links.core, ab], core_down.at[ab], links.other_core()
                    ),
                )
            )
    up_rows, down_rows = gate_up.shape[2], down.shape[2]

    def core_step(ab):
        for copy in core_copies[ab] if cs == 2 else ():
            copy.wait_recv()
        for mine, came, out, rows in (
            (gate_up.at[links.core, ab], core_up.at[ab], sum_up.at[ab], up_rows),
            (down.at[links.core, ab], core_down.at[ab], sum_down.at[ab], down_rows),
        ):
            add_rows(out, mine, came, rows, 96)

    up1, down1 = up_rows // xs, down_rows // xs
    up2, down2 = up1 // zs, down1 // zs
    first_copies, second_copies = {}, {}

    def first_send(ab):
        n, place = sizes[ab], places[ab]
        for k in range(1, n):
            j = (place + k) % n
            first_copies[ab, k] = (
                links.go(
                    sum_up.at[ab, at(j * up1, up1)], in_up.at[ab, k - 1], links.place(ab, k)
                ),
                links.go(
                    sum_down.at[ab, at(j * down1, down1)],
                    in_down.at[ab, k - 1],
                    links.place(ab, k),
                ),
            )

    def first_sum(ab):
        n, place = sizes[ab], places[ab]
        for k in range(1, n):
            for copy in first_copies[ab, k]:
                copy.wait_recv()
        for mine, came, out, rows, piece in (
            (sum_up, in_up, part_up, up1, up2),
            (sum_down, in_down, part_down, down1, down2),
        ):

            if piece % 16 == 0:

                @pl.loop(0, rows // piece)
                def _(j):
                    own = mine[ab, at(place * rows + j * piece, piece)].astype(f32)
                    for k in range(1, n):
                        own = own + came[ab, k - 1, at(j * piece, piece)].astype(f32)
                    out[ab, j, 0:piece] = own.astype(bf16)

            else:
                own = mine[ab, at(place * rows, rows)].astype(f32)
                for k in range(1, n):
                    own = own + came[ab, k - 1].astype(f32)
                for j in range(rows // piece):
                    out[ab, j, 0:piece] = own[j * piece : (j + 1) * piece].astype(bf16)

    def second_send(ab):
        n, place = sizes[1 - ab], places[1 - ab]
        for k in range(1, n):
            j = (place + k) % n
            second_copies[ab, k] = (
                links.go(part_up.at[ab, j], in2_up.at[ab, k - 1], links.place(1 - ab, k)),
                links.go(part_down.at[ab, j], in2_down.at[ab, k - 1], links.place(1 - ab, k)),
            )

    def second_sum(ab, out_up, out_down):
        n, place = sizes[1 - ab], places[1 - ab]
        for k in range(1, n):
            for copy in second_copies[ab, k]:
                copy.wait_recv()
        for mine, came, out in (
            (part_up, in2_up, out_up),
            (part_down, in2_down, out_down),
        ):
            value = mine[ab, place].astype(f32)
            for k in range(1, n):
                value = value + came[ab, k - 1].astype(f32)
            out[...] = value.astype(bf16)

    for ref in (part_up, part_down):
        piece = up2 if ref is part_up else down2
        if piece < ref.shape[2]:
            ref[:, :, piece:] = jnp.zeros(
                (2, ref.shape[1], ref.shape[2] - piece, ref.shape[3]), bf16
            )

    core_step(0)
    first_send(0)
    forward()
    core_step(1)
    first_send(1)

    for copy in vec_copies:
        copy.wait()
    vec = vectors[...] + vec_in[0] + half_swap(vec_in[1] + vec_in[2])
    vector_sums[...] = vec
    finish()
    inner = column(vec[6:7, 0:HALF])[:, 0:1]
    part = jnp.zeros((8, width), f32)
    for h in range(4):
        rows = slice(h * 128, (h + 1) * 128)
        grad = total(rows)
        values = hidden[rows]
        scale_rows = scale[rows, 0:1]
        back = norm_back_rows(
            grad, gain[0:1, :], values, scale_rows, inner[rows], 2 * width
        )
        back = back + cot[rows].astype(f32)
        hidden_grad[rows] = back
        low[rows] = back.astype(bf16)
        part = part + jnp.sum(
            (grad * values * scale_rows).reshape(16, 8, width), axis=0
        )
    gain_part[...] = jnp.broadcast_to(jnp.sum(part, axis=0, keepdims=True), (8, width))

    def own(h):
        return low.at[h * quarter : (h + 1) * quarter]

    def dst(k, h):
        rows = (HALF if k & 2 else 0) + h * quarter
        return hidden_low.at[rows : rows + quarter, (k & 1) * width : (k & 1) * width + width]

    mine = pltpu.make_async_copy(low, hidden_low.at[0:HALF, 0:width], local)
    mine.start()
    forward_low, finish_low = gather_group(links, own, dst, width)
    first_sum(0)
    second_send(0)
    first_sum(1)
    second_send(1)
    forward_low()
    second_sum(0, shard_up.at[0], shard_down.at[0])
    second_sum(1, peer_up, peer_down)
    peer = [
        links.go(peer_up, shard_up.at[1], links.group(1)),
        links.go(peer_down, shard_down.at[1], links.group(1)),
    ]
    mine.wait()
    finish_low()
    for copy in peer:
        copy.wait()
    sent()
    for pair in core_copies:
        for copy in pair:
            copy.wait_send()
    for copies in (first_copies, second_copies):
        for pair in copies.values():
            for copy in pair:
                copy.wait_send()


def pad16(n):
    return -(-n // 16) * 16


def reduce_step(partial, vectors, hidden, cot, scale, gain, gate_up, down):
    xs, zs, cs = dp_sizes()
    width = hidden.shape[1]
    up_rows, down_rows = gate_up.shape[2], down.shape[2]
    up1, down1 = up_rows // xs, down_rows // xs
    up2, down2 = pad16(up1 // zs), pad16(down1 // zs)
    n1, n2 = max(xs - 1, 1), max(zs - 1, 1)
    quarter = HALF // 2
    return pl.pallas_call(
        reduce_kernel,
        out_shape=(
            jax.ShapeDtypeStruct((HALF, width), f32),
            jax.ShapeDtypeStruct((2 * HALF, 2 * width), bf16),
            jax.ShapeDtypeStruct(vectors.shape, f32),
            jax.ShapeDtypeStruct((8, width), f32),
            jax.ShapeDtypeStruct((2, up2, SIDE), bf16),
            jax.ShapeDtypeStruct((2, down2, SIDE), bf16),
        ),
        in_specs=[WHOLE] * 8,
        out_specs=(WHOLE, ANY, WHOLE, WHOLE, WHOLE, WHOLE),
        scratch_shapes=[
            VMEM((quarter, width), bf16),
            VMEM((quarter, width), bf16),
            VMEM((HALF, width), bf16),
            VMEM((HALF, width), bf16),
            VMEM((quarter, width), bf16),
            VMEM((quarter, width), bf16),
            VMEM((3,) + vectors.shape, f32),
            VMEM((HALF, width), bf16),
            VMEM((2, up_rows, SIDE), bf16),
            VMEM((2, down_rows, SIDE), bf16),
            VMEM((2, up_rows, SIDE), bf16),
            VMEM((2, down_rows, SIDE), bf16),
            VMEM((2, n1, up1, SIDE), bf16),
            VMEM((2, n1, down1, SIDE), bf16),
            VMEM((2, zs, up2, SIDE), bf16),
            VMEM((2, zs, down2, SIDE), bf16),
            VMEM((2, n2, up2, SIDE), bf16),
            VMEM((2, n2, down2, SIDE), bf16),
            VMEM((up2, SIDE), bf16),
            VMEM((down2, SIDE), bf16),
            pltpu.SemaphoreType.DMA((48,)),
            pltpu.SemaphoreType.DMA((48,)),
            pltpu.SemaphoreType.DMA,
        ],
        compiler_params=pltpu.CompilerParams(
            collective_id=2, has_side_effects=True, vmem_limit_bytes=56 * 2**20
        ),
        name="reduce_step",
    )(partial, vectors, hidden, cot, scale, gain, gate_up, down)


def final_kernel(
    partial,
    vectors,
    tokens,
    scale,
    gain,
    hidden_grad,
    router_part,
    layer_partial,
    hidden,
    qkv_part,
    out_part,
    small,
    input_grad,
    layer_out,
    small_out,
    sums,
    near2,
    near3,
    far2,
    far3,
    out2,
    out3,
    lnear2,
    lnear3,
    lfar2,
    lfar3,
    lout2,
    lout3,
    vec_in,
    small_own,
    small_in,
    core_in,
    core_sum,
    in1,
    part,
    in2,
    own_shard,
    peer_shard,
    send,
    recv,
    local,
):
    links = Links(send, recv)
    xs, zs, cs = links.xs, links.zs, links.cs
    sizes, places = (xs, zs), (links.x, links.z)
    links.greet([links.group(k) for k in (1, 2, 3)] + links.plane())
    width = partial.shape[1] // 2
    forward, finish, total, sent = scatter_group(
        links, partial, near2, near3, far2, far3, out2, out3
    )
    vec_copies = [links.go(vectors, vec_in.at[k - 1], links.group(k)) for k in (1, 2, 3)]
    small_copies = [links.go(small, small_in.at[k - 1], links.group(k)) for k in (1, 2, 3)]
    qkv_cols = qkv_part.shape[1]
    core_copies = []
    if cs == 2:
        for ab in range(2):
            first = ab * width + (1 - links.core) * SIDE
            core_copies.append(
                (
                    links.go(
                        qkv_part.at[at(first, SIDE)],
                        core_in.at[ab, :, 0:qkv_cols],
                        links.other_core(),
                    ),
                    links.go(
                        out_part.at[:, at(first, SIDE, 128)],
                        core_in.at[ab, :, qkv_cols:],
                        links.other_core(),
                    ),
                )
            )
    n_first = SIDE // xs
    piece = n_first // zs
    pad = part.shape[2]
    first_copies, second_copies = {}, {}
    if piece < pad:
        part[:, :, piece:] = jnp.zeros((2, zs, pad - piece, part.shape[3]), bf16)

    def core_step(ab):
        first = ab * width + links.core * SIDE
        for copy in core_copies[ab] if cs == 2 else ():
            copy.wait_recv()
        mine = qkv_part[at(first, SIDE)].astype(f32)
        core_sum[ab, :, 0:qkv_cols] = (
            mine + core_in[ab, :, 0:qkv_cols].astype(f32)
        ).astype(bf16)
        mine = out_part[:, at(first, SIDE, 128)].astype(f32)
        core_sum[ab, :, qkv_cols:] = (mine + core_in[ab, :, qkv_cols:].astype(f32)).astype(
            bf16
        )

    def first_send(ab):
        n, place = sizes[ab], places[ab]
        for k in range(1, n):
            j = (place + k) % n
            first_copies[ab, k] = links.go(
                core_sum.at[ab, at(j * n_first, n_first)],
                in1.at[ab, k - 1],
                links.place(ab, k),
            )

    def first_sum(ab):
        n, place = sizes[ab], places[ab]
        for k in range(1, n):
            first_copies[ab, k].wait_recv()

        own = core_sum[ab, at(place * n_first, n_first)].astype(f32)
        for k in range(1, n):
            own = own + in1[ab, k - 1].astype(f32)
        for j in range(zs):
            part[ab, j, 0:piece] = own[j * piece : (j + 1) * piece].astype(bf16)

    def second_send(ab):
        n, place = sizes[1 - ab], places[1 - ab]
        for k in range(1, n):
            j = (place + k) % n
            second_copies[ab, k] = links.go(
                part.at[ab, j], in2.at[ab, k - 1], links.place(1 - ab, k)
            )

    def second_sum(ab, out):
        n, place = sizes[1 - ab], places[1 - ab]
        value = part[ab, place].astype(f32)
        for k in range(1, n):
            second_copies[ab, k].wait_recv()
            value = value + in2[ab, k - 1].astype(f32)
        out[...] = value.astype(bf16)

    core_step(0)
    first_send(0)
    core_step(1)
    first_send(1)
    forward()
    lforward, lfinish, ltotal, lsent = scatter_group(
        links, layer_partial, lnear2, lnear3, lfar2, lfar3, lout2, lout3
    )
    for copy in small_copies:
        copy.wait()

    def swapped(v):
        return jnp.concatenate([v[:, width:], v[:, :width]], axis=1)

    group_sum = small[...] + small_in[1] + swapped(small_in[0] + small_in[2])
    rows = lax.broadcasted_iota(jnp.int32, (8, width), 0)
    small_own[0] = jnp.where(rows < 6, small[:, 0:width], group_sum[:, 0:width])
    stage_copies = []

    def small_stage(stage):
        axis_sizes = (cs, xs, zs)
        base = (0, 1, xs)[stage]
        n = axis_sizes[stage]
        copies = []
        for k in range(1, n):
            device = links.other_core() if stage == 0 else links.place(stage - 1, k)
            copies.append(
                links.go(small_own.at[stage], small_in.at[3 + base + k - 1, :, 0:width], device)
            )

        def done():
            value = small_own[stage]
            for k in range(1, n):
                copies[k - 1].wait()
                value = value + small_in[3 + base + k - 1, :, 0:width]
            small_own[stage + 1] = value

        return done

    done = small_stage(0)
    first_sum(0)
    second_send(0)
    done()
    done = small_stage(1)
    first_sum(1)
    second_send(1)
    done()
    done = small_stage(2)
    second_sum(1, peer_shard)
    peer = links.go(peer_shard, own_shard.at[1], links.group(1))
    second_sum(0, own_shard.at[0])
    done()
    small_out[...] = small_own[3]

    gather_copies = []

    def index(ab, x, z):
        return (x * zs + z) if ab == 0 else (z * xs + x)

    home = []
    for ab in range(2):
        if ab == 1:
            peer.wait()
        here = sums.at[links.core, ab, index(ab, links.x, links.z)]
        mine = pltpu.make_async_copy(own_shard.at[ab], here, local.at[ab])
        mine.start()
        home.append(mine)
        for k in range(1, sizes[1 - ab]):
            gather_copies.append(links.go(own_shard.at[ab], here, links.place(1 - ab, k)))
    lforward()

    for copy in vec_copies:
        copy.wait()
    vec = vectors[...] + vec_in[0] + half_swap(vec_in[1] + vec_in[2])
    inner = column(vec[6:7, 0:HALF])[:, 0:1]
    finish()
    for h in range(4):
        rows = slice(h * 128, (h + 1) * 128)
        grad = total(rows) + router_part[rows]
        back = norm_back_rows(
            grad,
            gain[0:1, :],
            tokens[rows].astype(f32),
            scale[rows, 0:1],
            inner[rows],
            2 * width,
        )
        input_grad[rows] = hidden_grad[rows] + back

    for copy in gather_copies:
        copy.wait()
    for copy in home:
        copy.wait()
    second = []
    for ab in range(2):
        first = (links.x if ab == 0 else links.z) * sizes[1 - ab]
        block = sums.at[links.core, ab, pl.ds(first, sizes[1 - ab])]
        for k in range(1, sizes[ab]):
            second.append(links.go(block, block, links.place(ab, k)))
    for copy in second:
        copy.wait()
    last = None
    if cs == 2:
        block = sums.at[links.core]
        last = links.go(block, block, links.other_core())
    lfinish()
    for h in range(4):
        rows = slice(h * 128, (h + 1) * 128)
        layer_out[rows] = (hidden[rows] + ltotal(rows)).astype(bf16)
    if last is not None:
        last.wait()
    sent()
    lsent()
    for pair in core_copies:
        for copy in pair:
            copy.wait_send()
    for copies in (first_copies, second_copies):
        for copy in copies.values():
            copy.wait_send()


def final_step(
    partial,
    vectors,
    tokens,
    scale,
    gain,
    hidden_grad,
    router_part,
    layer_partial,
    hidden,
    qkv_part,
    out_part,
    small,
):
    xs, zs, cs = dp_sizes()
    width = hidden.shape[1]
    quarter = HALF // 2
    cols = qkv_part.shape[1] + SIDE
    pad = pad16(SIDE // (xs * zs))
    n1, n2 = max(xs - 1, 1), max(zs - 1, 1)
    group_buffers = [
        VMEM((quarter, width), bf16),
        VMEM((quarter, width), bf16),
        VMEM((HALF, width), bf16),
        VMEM((HALF, width), bf16),
        VMEM((quarter, width), bf16),
        VMEM((quarter, width), bf16),
    ]
    return pl.pallas_call(
        final_kernel,
        out_shape=(
            jax.ShapeDtypeStruct((HALF, width), f32),
            jax.ShapeDtypeStruct((HALF, width), bf16),
            jax.ShapeDtypeStruct((8, width), f32),
            jax.ShapeDtypeStruct((cs, 2, xs * zs, pad, cols), bf16),
        ),
        in_specs=[WHOLE] * 12,
        out_specs=(WHOLE, WHOLE, WHOLE, ANY),
        scratch_shapes=group_buffers
        + group_buffers
        + [
            VMEM((3,) + vectors.shape, f32),
            VMEM((4, 8, width), f32),
            VMEM((3 + 1 + xs + zs, 8, 2 * width), f32),
            VMEM((2, SIDE, cols), bf16),
            VMEM((2, SIDE, cols), bf16),
            VMEM((2, n1, SIDE // xs, cols), bf16),
            VMEM((2, zs, pad, cols), bf16),
            VMEM((2, n2, pad, cols), bf16),
            VMEM((2, pad, cols), bf16),
            VMEM((pad, cols), bf16),
            pltpu.SemaphoreType.DMA((64,)),
            pltpu.SemaphoreType.DMA((64,)),
            pltpu.SemaphoreType.DMA((2,)),
        ],
        compiler_params=pltpu.CompilerParams(
            collective_id=3, has_side_effects=True, vmem_limit_bytes=56 * 2**20
        ),
        name="final_step",
    )(
        partial,
        vectors,
        tokens,
        scale,
        gain,
        hidden_grad,
        router_part,
        layer_partial,
        hidden,
        qkv_part,
        out_part,
        small,
    )


def swap_halves(v):
    half = v.shape[-1] // 2
    return jnp.concatenate([v[..., half:], v[..., :half]], axis=-1)


def project_kernel(
    tok, small, weight, routes, cosine, sine, normed_ref, q_ref, k_ref, v_ref, gates_ref, scale_ref
):
    x = tok[...].astype(f32)
    rows, width = x.shape
    scale = lax.rsqrt(jnp.sum(x * x, axis=1, keepdims=True) * (1.0 / width) + EPS)
    normed = (x * scale * small[6:7, :]).astype(bf16)
    normed_ref[...] = normed
    scale_ref[...] = jnp.broadcast_to(scale, scale_ref.shape)
    router = jnp.concatenate([small[...], jnp.zeros((120, width), f32)], axis=0).astype(bf16)
    logits = nt(normed, router)
    lanes = lax.broadcasted_iota(jnp.int32, (rows, 128), 1)
    chosen = lanes == routes[:, 0:1]
    for j in range(1, routes.shape[1]):
        chosen = chosen | (lanes == routes[:, j : j + 1])
    masked = jnp.where(chosen, logits, MASKED)
    raised = jnp.exp(masked - jnp.max(masked, axis=1, keepdims=True))
    raised = jnp.where(chosen, raised, 0.0)
    gates_ref[...] = raised / jnp.sum(raised, axis=1, keepdims=True)
    projected = nn(normed, weight[...])
    for h in range(4):
        part = projected[:, h * HEAD : (h + 1) * HEAD]
        turned = (part * cosine[...] + swap_halves(part) * sine[...]).astype(bf16)
        if h < 3:
            q_ref[:, h * HEAD : (h + 1) * HEAD] = turned
        else:
            k_ref[...] = turned
    v_ref[...] = projected[:, 4 * HEAD :].astype(bf16)


def project(tokens_all, small, weight, routes, cosine, sine):
    total, width = tokens_all.shape
    step = 256

    def rows(cols):
        return pl.BlockSpec((step, cols), lambda i: (i, 0))

    def whole(shape):
        return pl.BlockSpec(shape, lambda i: (0,) * len(shape))

    return pl.pallas_call(
        project_kernel,
        grid=(total // step,),
        out_shape=(
            jax.ShapeDtypeStruct((total, width), bf16),
            jax.ShapeDtypeStruct((total, SIDE), bf16),
            jax.ShapeDtypeStruct((total, HEAD), bf16),
            jax.ShapeDtypeStruct((total, HEAD), bf16),
            jax.ShapeDtypeStruct((total, 128), f32),
            jax.ShapeDtypeStruct((total, 128), f32),
        ),
        in_specs=[
            rows(width),
            whole(small.shape),
            whole(weight.shape),
            rows(routes.shape[1]),
            rows(HEAD),
            rows(HEAD),
        ],
        out_specs=(rows(width), rows(SIDE), rows(HEAD), rows(HEAD), rows(128), rows(128)),
        compiler_params=pltpu.CompilerParams(vmem_limit_bytes=32 * 2**20),
        cost_estimate=pl.CostEstimate(
            flops=2 * total * width * 640, bytes_accessed=10 * 2**20, transcendentals=0
        ),
        name="project",
    )(tokens_all, small, weight, routes, cosine, sine)


def mix_kernel(ctx, tok, weight, small, normed_ref, hidden_ref, scale_ref):
    hidden = tok[...].astype(f32) + nn(ctx[...], weight[...])
    width = hidden.shape[1]
    scale = lax.rsqrt(jnp.sum(hidden * hidden, axis=1, keepdims=True) * (1.0 / width) + EPS)
    normed_ref[...] = (hidden * scale * small[7:8, :]).astype(bf16)
    scale_ref[...] = jnp.broadcast_to(scale, scale_ref.shape)

    @pl.when(pl.program_id(0) < 2)
    def _():
        hidden_ref[...] = hidden[:, : width // 2]


def mix(context_all, tokens_all, weight, small):
    total, width = tokens_all.shape
    step = 256

    def rows(cols):
        return pl.BlockSpec((step, cols), lambda i: (i, 0))

    def whole(shape):
        return pl.BlockSpec(shape, lambda i: (0,) * len(shape))

    return pl.pallas_call(
        mix_kernel,
        grid=(total // step,),
        out_shape=(
            jax.ShapeDtypeStruct((total, width), bf16),
            jax.ShapeDtypeStruct((total // 2, width // 2), f32),
            jax.ShapeDtypeStruct((total, 128), f32),
        ),
        in_specs=[rows(width), rows(width), whole(weight.shape), whole(small.shape)],
        out_specs=(
            rows(width),
            pl.BlockSpec((step, width // 2), lambda i: (jnp.minimum(i, 1), 0)),
            rows(128),
        ),
        compiler_params=pltpu.CompilerParams(vmem_limit_bytes=40 * 2**20),
        cost_estimate=pl.CostEstimate(
            flops=2 * total * width * width, bytes_accessed=14 * 2**20, transcendentals=0
        ),
        name="mix",
    )(context_all, tokens_all, weight, small)


def experts_kernel(
    normed, cot, gate_up, down, gates, weighted_ref, grad_ref, back_ref, out_ref, vec_ref
):
    col = lax.axis_index("col")
    count, _, both = gate_up.shape
    hidden = both // 2
    rows = normed.shape[0]
    lanes = lax.broadcasted_iota(jnp.int32, (rows, 128), 1)
    vec = jnp.zeros((rows, 128), f32)
    inner = jnp.zeros((rows, 1), f32)
    back = out = None
    x, y = normed[...], cot[...]
    for e in range(count):
        here = lanes == col * count + e
        gate = jnp.sum(jnp.where(here, gates[...], 0.0), axis=1, keepdims=True)
        both_pre = nn(x, gate_up[e])
        gate_pre, up_pre = both_pre[:, :hidden], both_pre[:, hidden:]
        sigmoid = 1.0 / (1.0 + jnp.exp(-gate_pre))
        silu = gate_pre * sigmoid
        activated = silu * up_pre
        weighted = (gate * activated).astype(bf16)
        weighted_ref[:, e * hidden : (e + 1) * hidden] = weighted
        down_e = down[e * hidden : (e + 1) * hidden]
        weighted_grad = nt(y, down_e)
        vec = vec + jnp.where(
            here, jnp.sum(activated * weighted_grad, axis=1, keepdims=True), 0.0
        )
        g = gate * weighted_grad
        gate_grad = g * up_pre * (sigmoid * (1.0 + gate_pre * (1.0 - sigmoid)))
        up_grad = g * silu
        inner = inner + jnp.sum(gate_grad * gate_pre + up_grad * up_pre, axis=1, keepdims=True)
        grads = jnp.concatenate([gate_grad, up_grad], axis=1).astype(bf16)
        grad_ref[e] = grads
        back_e = nt(grads, gate_up[e])
        out_e = nn(weighted, down_e)
        back = back_e if back is None else back + back_e
        out = out_e if out is None else out + out_e
    back_ref[...] = back.astype(bf16)
    out_ref[...] = out.astype(bf16)
    vec = jnp.where(lanes == 6, inner, vec)
    vec_ref[...] = vec.T[0:8, :]


def experts_step(normed, cot, gate_up, down, gates):
    total, width = normed.shape
    step = 256
    count, _, both = gate_up.shape

    def rows(cols):
        return pl.BlockSpec((step, cols), lambda i: (i, 0))

    def whole(shape):
        return pl.BlockSpec(shape, lambda i: (0,) * len(shape))

    return pl.pallas_call(
        experts_kernel,
        grid=(total // step,),
        out_shape=(
            jax.ShapeDtypeStruct((total, down.shape[0]), bf16),
            jax.ShapeDtypeStruct((count, total, both), bf16),
            jax.ShapeDtypeStruct((total, width), bf16),
            jax.ShapeDtypeStruct((total, width), bf16),
            jax.ShapeDtypeStruct((8, total), f32),
        ),
        in_specs=[
            rows(width),
            rows(width),
            whole(gate_up.shape),
            whole(down.shape),
            rows(128),
        ],
        out_specs=(
            rows(down.shape[0]),
            pl.BlockSpec((count, step, both), lambda i: (0, i, 0)),
            rows(width),
            rows(width),
            pl.BlockSpec((8, step), lambda i: (0, i)),
        ),
        compiler_params=pltpu.CompilerParams(vmem_limit_bytes=58 * 2**20),
        cost_estimate=pl.CostEstimate(
            flops=6 * total * width * count * both, bytes_accessed=26 * 2**20, transcendentals=0
        ),
        name="experts",
    )(normed, cot, gate_up, down, gates)


def expert_grads_kernel(normed, grads, weighted, cot, up_ref, down_ref):
    width = normed.shape[1]
    half = width // 2
    hidden = weighted.shape[1]
    for ab in range(2):
        part = tn(normed[:, ab * half : (ab + 1) * half], grads[0])
        for which in range(2):
            up_ref[which, ab] = part[:, which * hidden : (which + 1) * hidden].astype(bf16)
    part = tn(weighted[...], cot[...])
    for ab in range(2):
        for which in range(2):
            first = ab * half + which * hidden
            down_ref[which, ab] = part[:, first : first + hidden].astype(bf16)


def expert_grads(normed, grads, weighted, cot):
    total, width = normed.shape
    count, _, both = grads.shape
    hidden = both // 2
    half = width // 2

    def whole(shape):
        return pl.BlockSpec(shape, lambda e: (0,) * len(shape))

    return pl.pallas_call(
        expert_grads_kernel,
        grid=(count,),
        out_shape=(
            jax.ShapeDtypeStruct((2, 2, count * half, hidden), bf16),
            jax.ShapeDtypeStruct((2, 2, count * hidden, hidden), bf16),
        ),
        in_specs=[
            whole(normed.shape),
            pl.BlockSpec((1, total, both), lambda e: (e, 0, 0)),
            pl.BlockSpec((total, hidden), lambda e: (0, e)),
            whole(cot.shape),
        ],
        out_specs=(
            pl.BlockSpec((2, 2, half, hidden), lambda e: (0, 0, e, 0)),
            pl.BlockSpec((2, 2, hidden, hidden), lambda e: (0, 0, e, 0)),
        ),
        compiler_params=pltpu.CompilerParams(vmem_limit_bytes=56 * 2**20),
        cost_estimate=pl.CostEstimate(
            flops=3 * total * width * count * both, bytes_accessed=24 * 2**20, transcendentals=0
        ),
        name="expert_grads",
    )(normed, grads, weighted, cot)


def window(i, block):
    first = max(0, (i + 1) * block - 512 - block)
    return first, (i + 1) * block


def own_places(ref, out, row, half):
    for h in range(2):
        start = pl.multiple_of(half * jnp.bitwise_xor(row, h), half)
        out[h * half : (h + 1) * half] = ref[pl.ds(start, half)]


def allowed_keys(segk_ref, segq_ref, i, first, last):
    block = BLOCK
    width = last - first
    keys = lax.broadcasted_iota(jnp.int32, (width, block), 0) + first
    queries = lax.broadcasted_iota(jnp.int32, (width, block), 1) + i * block
    same = segk_ref[first:last] == segq_ref[:, i * block : (i + 1) * block]
    return (keys <= queries) & same


def attend_kernel(heads, q_ref, k_ref, v_ref, segk_ref, segq_ref, o_ref, lse_ref, q, k, vt):
    row = lax.axis_index("row")
    total = q_ref.shape[0]
    half = total // 2
    own_places(q_ref, q, row, half)
    own_places(k_ref, k, row, half)
    for h in range(2):
        start = pl.multiple_of(half * jnp.bitwise_xor(row, h), half)
        vt[:, h * half : (h + 1) * half] = v_ref[pl.ds(start, half)].astype(f32).T.astype(bf16)
    for i in range(total // BLOCK):
        first, last = window(i, BLOCK)
        here = slice(i * BLOCK, (i + 1) * BLOCK)
        allowed = allowed_keys(segk_ref, segq_ref, i, first, last)
        place = i * BLOCK // half
        start = pl.multiple_of(
            half * jnp.bitwise_xor(row, place) + (i * BLOCK - place * half), BLOCK
        )
        for h in range(heads):
            s = nt(k[first:last], q[here, h * HEAD : (h + 1) * HEAD]) * (HEAD**-0.5)
            s = jnp.where(allowed, s, MASKED)
            top = jnp.max(s, axis=0, keepdims=True)
            p = jnp.exp(s - top)
            total_p = jnp.sum(p, axis=0, keepdims=True)
            p = (p * (1.0 / total_p)).astype(bf16)
            ot = nn(vt[:, first:last], p)
            o_ref[pl.ds(start, BLOCK), h * HEAD : (h + 1) * HEAD] = ot.T.astype(bf16)
            lse_ref[h : h + 1, here] = top + jnp.log(total_p)


def attend(q, k, v, seg):
    total, width = q.shape
    heads = width // HEAD
    return pl.pallas_call(
        functools.partial(attend_kernel, heads),
        out_shape=(
            jax.ShapeDtypeStruct((total, width), bf16),
            jax.ShapeDtypeStruct((8, total), f32),
        ),
        in_specs=[WHOLE] * 5,
        out_specs=(WHOLE, WHOLE),
        scratch_shapes=[
            VMEM((total, width), bf16),
            VMEM((total, HEAD), bf16),
            VMEM((HEAD, total), bf16),
        ],
        compiler_params=pltpu.CompilerParams(vmem_limit_bytes=32 * 2**20),
        cost_estimate=pl.CostEstimate(
            flops=2 * heads * total * total * HEAD * 2,
            bytes_accessed=6 * total * width,
            transcendentals=heads * total * total,
        ),
        name="attend",
    )(q, k, v, seg.reshape(total, 1), seg.reshape(1, total))


def attend_back_kernel(
    heads,
    q_ref,
    k_ref,
    v_ref,
    hidden_low,
    out_weight,
    segk_ref,
    segq_ref,
    lse_ref,
    cos_ref,
    sin_ref,
    grad_ref,
    vec_ref,
    q,
    k,
    v,
    kt,
    do,
    dk,
    dv,
):
    row = lax.axis_index("row")
    total = q_ref.shape[0]
    half = total // 2
    scale = HEAD**-0.5
    own_places(q_ref, q, row, half)
    own_places(k_ref, k, row, half)
    own_places(v_ref, v, row, half)
    for h in range(2):
        start = pl.multiple_of(half * jnp.bitwise_xor(row, h), half)
        do[h * half : (h + 1) * half] = nt(
            hidden_low[pl.ds(start, half)], out_weight[...]
        ).astype(bf16)
    kt[...] = k[...].astype(f32).T.astype(bf16)
    dk[...] = jnp.zeros_like(dk)
    dv[...] = jnp.zeros_like(dv)

    def back(grad, rows):
        return grad * cos_ref[rows] - swap_halves(grad) * sin_ref[rows]

    inners = []
    for i in range(total // BLOCK):
        first, last = window(i, BLOCK)
        here = slice(i * BLOCK, (i + 1) * BLOCK)
        allowed = allowed_keys(segk_ref, segq_ref, i, first, last)
        place = i * BLOCK // half
        start = pl.multiple_of(
            half * jnp.bitwise_xor(row, place) + (i * BLOCK - place * half), BLOCK
        )
        rows = pl.ds(start, BLOCK)
        inner_q = jnp.zeros((BLOCK, 1), f32)
        for h in range(heads):
            cols = slice(h * HEAD, (h + 1) * HEAD)
            s = nt(k[first:last], q[here, cols]) * scale
            s = jnp.where(allowed, s, MASKED)
            p = jnp.exp(s - lse_ref[h : h + 1, here])
            dp = nt(v[first:last], do[here, cols])
            inner = jnp.sum(dp * p, axis=0, keepdims=True)
            ds = (p * (dp - inner)).astype(bf16)
            dq = (nn(kt[:, first:last], ds) * scale).T
            inner_q = inner_q + jnp.sum(dq * q[here, cols].astype(f32), axis=1, keepdims=True)
            grad_ref[rows, cols] = back(dq, rows).astype(bf16)
            dk[first:last] += nn(ds, q[here, cols]) * scale
            dv[first:last] += nn(p.astype(bf16), do[here, cols])
        inners.append(inner_q)
    width = heads * HEAD
    for i in range(total // BLOCK):
        here = slice(i * BLOCK, (i + 1) * BLOCK)
        place = i * BLOCK // half
        start = pl.multiple_of(
            half * jnp.bitwise_xor(row, place) + (i * BLOCK - place * half), BLOCK
        )
        rows = pl.ds(start, BLOCK)
        key_grad, value_grad = dk[here], dv[here]
        inner = inners[i] + jnp.sum(
            key_grad * k[here].astype(f32) + value_grad * v[here].astype(f32),
            axis=1,
            keepdims=True,
        )
        grad_ref[rows, width : width + HEAD] = back(key_grad, rows).astype(bf16)
        grad_ref[rows, width + HEAD :] = value_grad.astype(bf16)
        vec_ref[:, rows] = jnp.broadcast_to(inner, (BLOCK, 128)).T[0:8, :]


def attend_back(q, k, v, hidden_low, out_weight, seg, lse, cosine, sine):
    total, width = q.shape
    heads = width // HEAD
    return pl.pallas_call(
        functools.partial(attend_back_kernel, heads),
        out_shape=(
            jax.ShapeDtypeStruct((total, width + 2 * HEAD), bf16),
            jax.ShapeDtypeStruct((8, total), f32),
        ),
        in_specs=[WHOLE] * 10,
        out_specs=(WHOLE, WHOLE),
        scratch_shapes=[
            VMEM((total, width), bf16),
            VMEM((total, HEAD), bf16),
            VMEM((total, HEAD), bf16),
            VMEM((HEAD, total), bf16),
            VMEM((total, width), bf16),
            VMEM((total, HEAD), f32),
            VMEM((total, HEAD), f32),
        ],
        compiler_params=pltpu.CompilerParams(vmem_limit_bytes=48 * 2**20),
        cost_estimate=pl.CostEstimate(
            flops=5 * heads * total * total * HEAD * 2,
            bytes_accessed=10 * total * width,
            transcendentals=heads * total * total,
        ),
        name="attend_back",
    )(
        q,
        k,
        v,
        hidden_low,
        out_weight,
        seg.reshape(total, 1),
        seg.reshape(1, total),
        lse,
        cosine,
        sine,
    )


def attn_grads_kernel(
    grads,
    qkv_weight,
    normed,
    context,
    hidden_low,
    small,
    gates,
    vec_sums,
    vec_part,
    ffn_part,
    partial_ref,
    qkv_ref,
    out_ref,
    vec_ref,
    router_ref,
    small_ref,
):
    total, width = normed.shape
    half = width // 2
    row = lax.axis_index("row")
    col = lax.axis_index("col")
    rows = 256
    for i in range(total // rows):
        here = slice(i * rows, (i + 1) * rows)
        partial_ref[here] = nt(grads[here], qkv_weight[...]).astype(bf16)
    gate_rows = gates[...].T[0:8, :]
    sums = vec_sums[...]
    mask = lax.broadcasted_iota(jnp.int32, sums.shape, 0) < 6
    sums = jnp.where(mask, sums, 0.0)
    logits_grad = gate_rows * (sums - jnp.sum(gate_rows * sums, axis=0, keepdims=True))
    logits_low = jnp.where(mask, logits_grad, 0.0).astype(bf16)
    router = jnp.where(
        lax.broadcasted_iota(jnp.int32, (8, width), 0) < 6, small[...], 0.0
    )
    router_grad = nn(logits_low, normed[...])
    router_ref[...] = tn(logits_low[:, 0:HALF], router[:, 0:half].astype(bf16))
    pieces = []
    for i in range(width // rows):
        here = slice(i * rows, (i + 1) * rows)
        part = tn(normed[:, here], grads[...])
        qkv_ref[here] = part.astype(bf16)
        gain_sum = jnp.sum(part * qkv_weight[here].astype(f32), axis=1, keepdims=True)
        pieces.append(jnp.broadcast_to(gain_sum, (rows, 128)).T[0:8, :])
    out_ref[...] = tn(context[...], hidden_low[...]).astype(bf16)
    gain_row = jnp.concatenate(pieces, axis=1)
    once = jnp.where((row == 0) & (col == 0), 1.0, 0.0)
    gain_row = gain_row + once * jnp.sum(router_grad * router, axis=0, keepdims=True)
    gain_row = gain_row / small[6:7, :]
    ffn = jnp.concatenate([ffn_part[...], jnp.zeros((8, half), f32)], axis=1)
    index = lax.broadcasted_iota(jnp.int32, (8, width), 0)
    small_ref[...] = jnp.where(
        index < 6, router_grad, jnp.where(index == 6, gain_row, ffn)
    )
    logit_rows = nt(router.astype(bf16), normed[...])
    router_inner = jnp.sum(
        logits_low.astype(f32) * logit_rows, axis=0, keepdims=True
    )
    vec_ref[...] = vec_part[...] + once * router_inner


def attn_grads(
    grads, qkv_weight, normed, context, hidden_low, small, gates, vec_sums, vec_part, ffn_part
):
    total, width = normed.shape
    return pl.pallas_call(
        attn_grads_kernel,
        out_shape=(
            jax.ShapeDtypeStruct((total, width), bf16),
            jax.ShapeDtypeStruct(qkv_weight.shape, bf16),
            jax.ShapeDtypeStruct((context.shape[1], width), bf16),
            jax.ShapeDtypeStruct((8, total), f32),
            jax.ShapeDtypeStruct((HALF, width // 2), f32),
            jax.ShapeDtypeStruct((8, width), f32),
        ),
        in_specs=[WHOLE] * 10,
        out_specs=(WHOLE,) * 6,
        compiler_params=pltpu.CompilerParams(vmem_limit_bytes=56 * 2**20),
        cost_estimate=pl.CostEstimate(
            flops=2 * total * width * (640 * 2 + 384), bytes_accessed=24 * 2**20, transcendentals=0
        ),
        name="attn_grads",
    )(grads, qkv_weight, normed, context, hidden_low, small, gates, vec_sums, vec_part, ffn_part)


def turn_tables(places):
    steps_up = jnp.arange(HEAD // 2, dtype=f32) * (2.0 / HEAD)
    inverse = jnp.exp(-math.log(ROPE_BASE) * steps_up)
    angles = places[:, None] * inverse[None, :]
    cosine, sine = jnp.cos(angles), jnp.sin(angles)
    return (
        jnp.concatenate([cosine, cosine], axis=1),
        jnp.concatenate([-sine, sine], axis=1),
    )


def gather4(x):
    half = x.shape[0] // 2
    a = flip(x, 2)
    b = flip(x, 3)
    c = jnp.concatenate([flip(b[:half], 2), flip(a[half:], 3)], axis=0)
    return x, c, a, b


def two_by_two(blocks):
    return jnp.concatenate(
        [
            jnp.concatenate([blocks[0], blocks[1]], axis=1),
            jnp.concatenate([blocks[2], blocks[3]], axis=1),
        ],
        axis=0,
    )


def local(
    tokens,
    cotangent,
    attn_gain,
    ffn_gain,
    qkv_weight,
    out_weight,
    router_weight,
    gate_weight,
    up_weight,
    down_weight,
    routes,
    segments,
):
    row = lax.axis_index("row")
    col = lax.axis_index("col")
    dp = lax.axis_index("dp")
    dp_count = lax.axis_size("dp")
    xs, zs, cs = dp_sizes()
    own_rows, own_width = tokens.shape
    total = 2 * own_rows
    experts, _, hidden = gate_weight.shape
    own_experts = experts // 2
    hid = own_experts * hidden
    other_col = 1 - col

    rolled = jnp.where(col == 0, out_weight, jnp.roll(out_weight, SIDE, axis=0))
    share = own_width // dp_count

    def dp_rows(v, count):
        return lax.dynamic_slice_in_dim(v, dp * count, count, v.ndim - 2)

    out_piece = dp_rows(rolled, share)
    out_pieces = jnp.concatenate([flip(out_piece, 1), flip(out_piece, 2), flip(out_piece, 3)], 0)

    def expert_half(v, which):
        return lax.dynamic_slice_in_dim(v, which * own_experts, own_experts, 0)

    gate_up_piece = jnp.concatenate(
        [
            dp_rows(expert_half(gate_weight, other_col), share),
            dp_rows(expert_half(up_weight, other_col), share),
        ],
        axis=2,
    ).reshape(own_experts * share, own_width)
    down_share = hid // dp_count
    down_piece = dp_rows(expert_half(down_weight, other_col).reshape(hid, own_width), down_share)
    expert_pieces = flip(jnp.concatenate([gate_up_piece, down_piece], axis=0), 1)
    gathered = lax.all_gather(
        jnp.concatenate([out_pieces, expert_pieces], axis=0), "dp", axis=0, tiled=False
    )
    out_other = (
        gathered[:, : 3 * share]
        .reshape(dp_count, 3, share, own_width)
        .transpose(1, 0, 2, 3)
        .reshape(3, own_width, own_width)
    )
    gate_up_other = (
        gathered[:, 3 * share : 3 * share + own_experts * share]
        .reshape(dp_count, own_experts, share, own_width)
        .transpose(1, 0, 2, 3)
        .reshape(own_experts, own_width, own_width)
    )
    down_other = gathered[:, (3 + own_experts) * share :].reshape(hid, own_width)

    o1, o2, o3 = out_other[0], out_other[1], out_other[2]
    out_local = jnp.concatenate(
        [
            jnp.concatenate([rolled, o2], axis=0),
            jnp.concatenate([o1[SIDE:], o1[:SIDE], o3[SIDE:], o3[:SIDE]], axis=0),
        ],
        axis=1,
    )
    gate_up_own = jnp.concatenate(
        [expert_half(gate_weight, col), expert_half(up_weight, col)], axis=2
    )
    gate_up_local = jnp.concatenate([gate_up_own, gate_up_other], axis=1)
    down_local = jnp.concatenate(
        [expert_half(down_weight, col).reshape(hid, own_width), down_other], axis=1
    )

    def own_order(v):
        return jnp.where(row == 0, v, jnp.roll(v, own_rows, axis=0))

    routes_local = own_order(routes)
    cosine, sine = turn_tables(own_order(jnp.arange(total, dtype=f32)))
    small = jnp.concatenate(
        [router_weight.T.astype(f32), attn_gain[None], ffn_gain[None]], axis=0
    )

    tokens_all, qkv_local, small_all = gather_inputs(tokens, qkv_weight, small)
    normed_one, queries, keys, values, gates, scale_one = project(
        tokens_all, small_all, qkv_local, routes_local, cosine, sine
    )
    context, lse = attend(queries, keys, values, segments)
    context_all = gather_context(context)
    cot_all = two_by_two(gather4(cotangent))
    normed_two, hidden_own, scale_two = mix(context_all, tokens_all, out_local, small_all)
    weighted, pre_grads, normed_two_part, layer_part, expert_vec = experts_step(
        normed_two, cot_all, gate_up_local, down_local, gates
    )
    gate_up_grads, down_grads = expert_grads(normed_two, pre_grads, weighted, cot_all)
    hidden_grad, hidden_low, vec_sums, ffn_part, shard_up, shard_down = reduce_step(
        normed_two_part,
        expert_vec,
        hidden_own,
        cotangent,
        scale_two,
        ffn_gain[None],
        gate_up_grads,
        down_grads,
    )
    up_rows = own_experts * own_width // (xs * zs)
    down_rows = hid // (xs * zs)
    expert_sums = lax.all_gather(
        jnp.concatenate([shard_up[:, :up_rows], shard_down[:, :down_rows]], axis=1),
        "dp",
        axis=0,
        tiled=False,
    ).reshape(xs, zs, cs, 2, up_rows + down_rows, SIDE)

    projected_grad, vec_part = attend_back(
        queries, keys, values, hidden_low, out_local[:SIDE], segments, lse, cosine, sine
    )
    input_part, qkv_part, out_part, input_vec, router_part, small_part = attn_grads(
        projected_grad,
        qkv_local,
        normed_one,
        context,
        hidden_low,
        small_all,
        gates,
        vec_sums,
        vec_part,
        ffn_part,
    )
    input_grad, layer_out, small_sums, attn_sums = final_step(
        input_part,
        input_vec,
        tokens,
        scale_one,
        attn_gain[None],
        hidden_grad,
        router_part,
        layer_part,
        hidden_own,
        qkv_part,
        out_part,
        small_part,
    )
    router_grad = small_sums[:experts].T
    attn_gain_grad = small_sums[6]
    ffn_gain_grad = small_sums[7]

    def spread(v, swap):
        v = v.transpose(1, 0, 2, 3) if swap else v
        return v.reshape(-1, v.shape[-1])

    def expert_out(rows, which):
        which = which % cs
        return [spread(expert_sums[:, :, which, ab, rows], ab == 1) for ab in range(2)]

    def gate_or_up(which):
        mine, other = expert_out(slice(0, up_rows), which)
        shape = (own_experts, own_width, hidden)
        return by_col(col, mine.reshape(shape), other.reshape(shape), 0).astype(f32)

    gate_grad = gate_or_up(0)
    up_grad = gate_or_up(1)
    down_mine, down_peer = [
        jnp.concatenate(list(parts), axis=1)
        for parts in zip(
            expert_out(slice(up_rows, None), 0), expert_out(slice(up_rows, None), 1)
        )
    ]
    shape = (own_experts, hidden, own_width)
    down_grad = by_col(col, down_mine.reshape(shape), down_peer.reshape(shape), 0).astype(f32)

    attn_rows = SIDE // (xs * zs)
    qkv_cols = SIDE + 2 * HEAD

    def attn_out(ab):
        block = attn_sums[:, ab, :, :attn_rows]
        qkv = block[..., :qkv_cols].reshape(own_width * cs // 2, qkv_cols)
        out = block[..., qkv_cols:].transpose(1, 2, 0, 3).reshape(SIDE, SIDE * cs)
        return qkv.astype(f32), out.astype(f32)

    qkv_mine, out_mine = attn_out(0)
    qkv_peer, out_peer = attn_out(1)
    qkv_grad = jnp.concatenate(
        [
            by_col(col, qkv_mine[:, :SIDE], qkv_peer[:, :SIDE], 1),
            qkv_mine[:, SIDE:] + qkv_peer[:, SIDE:],
        ],
        axis=1,
    )
    out_grad = by_col(col, out_mine, out_peer, 0)
    return (
        layer_out,
        input_grad,
        attn_gain_grad,
        ffn_gain_grad,
        qkv_grad,
        out_grad,
        router_grad,
        gate_grad,
        up_grad,
        down_grad,
    )


def solution(mesh):
    in_specs = (
        P(("dp", "row"), "col"),
        P(("dp", "row"), "col"),
        P("col"),
        P("col"),
        P("col", "row"),
        P("row", "col"),
        P("col", None),
        P(None, "col", "row"),
        P(None, "col", "row"),
        P(None, "row", "col"),
        P("dp", None),
        P("dp"),
    )
    out_specs = (
        P(("dp", "row"), "col"),
        P(("dp", "row"), "col"),
        P("col"),
        P("col"),
        P("col", "row"),
        P("row", "col"),
        P("col", None),
        P(None, "col", "row"),
        P(None, "col", "row"),
        P(None, "row", "col"),
    )
    return jax.shard_map(local, mesh=mesh, in_specs=in_specs, out_specs=out_specs, check_vma=False)
```

time: 595 us -> 494 us (0.83)
  Pallas kernels: 14 us -> 340 us
  waiting for transfers between devices: 155 us -> 1.89 us
  starting transfers between devices: 130 us -> 11.6 us
  matrix products: 88.7 us -> 0 us
  other arithmetic: 94.8 us -> 57.9 us
  local copies, waits for them, and re-layouts: 88.2 us -> 62.3 us
    pallas_call x0 -> x9, Pallas kernels: none -> 321 us  [the longest x1 85.2 us: final_step(): pl.pallas_call(final_kernel, out_shape=(jax.ShapeDtypeStruct((HALF, width...]
    ppermute x47 -> x8, waiting for transfers between devices: 110 us -> 1.86 us  [flip(): return lax.ppermute(v, ('row', 'col'), [(i, i ^ k) for i in range(4)])]
    dot_general x23 -> x0, matrix products: 88.7 us -> none  [the longest x8 33.8 us: dot(): return jnp.dot(a, b, preferred_element_type=f32)]
    ppermute x36 -> x0, starting transfers between devices: 88.3 us -> none  [shift(): return lax.ppermute(v, 'dp', pairs)]
    ppermute x36 -> x0, waiting for transfers between devices: 44.5 us -> none  [shift(): return lax.ppermute(v, 'dp', pairs)]
    convert_element_type x22 -> x1, other arithmetic: 38.7 us -> 3.35 us  [local(): by_col(col, down_mine.reshape(shape), down_peer.reshape(shape), 0)]
    ppermute x47 -> x8, starting transfers between devices: 41.9 us -> 11.6 us  [flip(): return lax.ppermute(v, ('row', 'col'), [(i, i ^ k) for i in range(4)])]
    concatenate x13 -> x7, other arithmetic: 13.5 us -> 37.4 us  [the longest x1 19.5 us: local(): jnp.concatenate([jnp.concatenate([rolled, o2], axis=0), jnp.concatenate([...]
  transfers between devices with their start and end apart: 86 -> 10, of which waited for: 37 -> 2; matrix products, arithmetic and copies ran while one was open for 30% -> 7% of each run, Pallas kernels for 1% -> 43%
where the time goes in v2:
time: 494 us; the launch traced here: 488 us
  Pallas kernels  340 us (69%)
  local copies, waits for them, and re-layouts  62.3 us (13%)
  other arithmetic  57.9 us (12%)
  between operations  15 us (3%)
  starting transfers between devices  11.6 us (2%)
    pallas_call x1, Pallas kernels, final_step(): pl.pallas_call(final_kernel, out_shape=(jax.ShapeDtypeStruct((HALF, width...  85.2 us
    pallas_call x1, Pallas kernels, reduce_step(): pl.pallas_call(reduce_kernel, out_shape=(jax.ShapeDtypeStruct((HALF, widt...  68.9 us
    pallas_call x1, Pallas kernels, gather_inputs(): pl.pallas_call(gather_inputs_kernel, out_shape=(jax.ShapeDtypeStruct((2 *...  59.7 us
    pallas_call x1, Pallas kernels, experts_step(): pl.pallas_call(experts_kernel, grid=(total // step,), out_shape=(jax.Shap...  34.6 us
    pallas_call x1, Pallas kernels, gather_context(): pl.pallas_call(gather_context_kernel, out_shape=jax.ShapeDtypeStruct((row...  28.1 us
    concatenate x1, other arithmetic, local(): jnp.concatenate([jnp.concatenate([rolled, o2], axis=0), jnp.concatenate([...  19.5 us
    unnamed x101, local copies, waits for them, and re-layouts  18.9 us
    pallas_call x1, Pallas kernels, expert_grads(): pl.pallas_call(expert_grads_kernel, grid=(count,), out_shape=(jax.ShapeDt...  17 us
  transfers between devices with their start and end apart: 10, of which 2 were waited for; matrix products, arithmetic and copies ran while one was open for 7% of the time, Pallas kernels for 43%

profile of v2, /device:TPU:1, one launch (start us, length us, event | category | flops | bytes accessed | tf_op | source)
XLA Modules:
  0.0 488.2 jit_solution(9372203717740108511)
XLA Ops:
  8.2 3.5 constant_dynamic-slice_fusion
  11.8 3.8 collective-permute-start.3
  17.9 3.1 collective-permute-start
  24.6 1.9 collective-permute-start.4
  27.7 59.7 %gather_inputs.1 = (bf16[1024,1536]{1,0:T(8,128)(2,1)}, bf16[1536,640]{1,0:T(8,128)(2,1)}, f32[8,1536]{1,0:T(8,128)}) custom-call(bf16[512,768]{1,0:T(8,128)(2,1)} %tokens.3, bf16[768,1024]{1,0:T(8,128)(2,1)} %qkv_weight.1, f32[8,768]{1,0:T(8,128)} %pad_maximum_fusion.8.small), custom_call_target="tpu_custom_call" | custom-call | tf_op jit(solution)/shard_map/gather_inputs/pallas_call | solution.py:231
  89.8 2.0 slice.194
  94.7 5.7 %project.1 = (bf16[1024,1536]{1,0:T(8,128)(2,1)S(1)}, bf16[1024,384]{1,0:T(8,128)(2,1)S(1)}, bf16[1024,128]{1,0:T(8,128)(2,1)S(1)}, bf16[1024,128]{1,0:T(8,128)(...) custom-call(bf16[1024,1536]{1,0:T(8,128)(2,1)S(1)} %copy-done.6, f32[8,1536]{1,0:T(8,128)S(1)} %copy-done.9, ...), custom_call_target="tpu_custom_call" | custom-call | flops 2013265920 | bytes 10485760 | tf_op jit(solution)/shard_map/project/pallas_call | solution.py:1002
  109.3 6.6 %attend.1 = (bf16[1024,384]{1,0:T(8,128)(2,1)S(1)}, f32[8,1024]{1,0:T(8,128)S(1)}) custom-call(bf16[1024,384]{1,0:T(8,128)(2,1)S(1)} %copy-done.13, bf16[1024,128]{1,0:T(8,128)(2,1)S(1)} %copy-done.17, bf16[1024,128]{1,0:T(8,128)(2,1)S(1)} %copy-done.20, s32[1024,1]{1,0:T(8,128)S(1)} %copy.44.segk_ref, s32[1,1024]{1,0:T(1,128)S(1)} %bitcast.69), custom_call_target="tpu_custom_call" | custom-call | flops 1610612736 | bytes 2359296 | tf_op jit(solution)/shard_map/attend/pallas_call | solution.py:1261
  116.7 28.1 %gather_context.1.ctx = bf16[1024,1536]{1,0:T(8,128)(2,1)} custom-call(bf16[1024,384]{1,0:T(8,128)(2,1)} %copy-done.2), custom_call_target="tpu_custom_call" | custom-call | tf_op jit(solution)/shard_map/gather_context/pallas_call | solution.py:280
  144.9 4.3 constant_dynamic-slice_fusion.1
  149.1 11.7 %maximum_maximum_fusion.1.cot = bf16[1024,1536]{1,0:T(8,128)(2,1)} fusion(bf16[512,768]{1,0:T(8,128)(2,1)} %collective-permute-done.4, bf16[512,768]{1,0:T(8,128)(2,1)} %collective-permute-done.6, bf16[256,768]{1,0:T(8,128)(2,1)S(1)} %collective-permute-done.7, bf16[256,768]{1,0:T(8,128)(2,1)S(1)} %collective-permute-done.5, bf16[512,768]{1,0:T(8,128)(2,1)S(1)} %copy-done.34), kind=kLoop, calls=%fused_computation.9 | loop fusion | flops 15728640 | bytes 6291456 | tf_op jit(solution)/shard_map/concatenate | solution.py:1515
  160.8 5.3 %fusion.6 = (bf16[32,72,768]{2,1,0:T(8,128)(2,1)}, bf16[32,72,768]{2,1,0:T(8,128)(2,1)S(1)}) fusion(bf16[32,180,768]{2,1,0:T(8,128)(2,1)} %all-gather.8.cloned.1.call-done), kind=kLoop, calls=%fused_computation.53 | loop fusion | bytes 14155776 | tf_op jit(solution)/shard_map/slice | solution.py:1582
  168.7 2.9 slice.196
  171.7 2.5 reshape.118
  174.1 2.4 copy.45
  176.7 2.1 pad_maximum_fusion.1.down
  180.3 19.5 %maximum_maximum_fusion.weight = bf16[1536,1536]{1,0:T(8,128)(2,1)} fusion(bf16[384,768]{1,0:T(8,128)(2,1)S(1)} %bitcast.92, bf16[384,768]{1,0:T(8,128)(2,1)S(1)} %bitcast.93, bf16[384,768]{1,0:T(8,128)(2,1)S(1)} %bitcast.94, bf16[384,768]{1,0:T(8,128)(2,1)S(1)} %bitcast.91, bf16[768,768]{1,0:T(8,128)(2,1)S(1)} %bitcast.82, bf16[768,768]{1,0:T(8,128)(2,1)S(1)} %copy-done.31), kind=kLoop, calls=%fused_computation.1 | loop fusion | flops 28311552 | bytes 9437184 | tf_op jit(solution)/shard_map/concatenate | solution.py:1590
  199.8 9.0 %mix.1 = (bf16[1024,1536]{1,0:T(8,128)(2,1)S(1)}, f32[512,768]{1,0:T(8,128)S(1)}, f32[1024,128]{1,0:T(8,128)S(1)}) custom-call(bf16[1024,1536]{1,0:T(8,128)(2,1)S(1)} %copy-done.1, bf16[1024,1536]{1,0:T(8,128)(2,1)S(1)} %copy-done.7, bf16[1536,1536]{1,0:T(8,128)(2,1)} %maximum_maximum_fusion.weight, f32[8,1536]{1,0:T(8,128)S(1)} %copy-done.10), custom_call_target="tpu_custom_call" | custom-call | flops 4831838208 | bytes 14680064 | tf_op jit(solution)/shard_map/mix/pallas_call | solution.py:1052
  208.8 4.2 pad_maximum_fusion.gate_up
  213.2 34.6 %experts.1 = (bf16[1024,1152]{1,0:T(8,128)(2,1)}, bf16[3,1024,768]{2,1,0:T(8,128)(2,1)}, bf16[1024,1536]{1,0:T(8,128)(2,1)}, bf16[1024,1536]{1,0:T(8,128)(2,1)}, f32[8,1024]{1,0:T(8,128)}) custom-call(bf16[1024,1536]{1,0:T(8,128)(2,1)} %copy-done.22, bf16[1024,1536]{1,0:T(8,128)(2,1)} %maximum_maximum_fusion.1.cot, ...), custom_call_target="tpu_custom_call" | custom-call | flops 21743271936 | bytes 27262976 | tf_op jit(solution)/shard_map/experts/pallas_call | solution.py:1128
  247.8 17.0 %expert_grads.1 = (bf16[2,2,2304,384]{3,2,1,0:T(8,128)(2,1)}, bf16[2,2,1152,384]{3,2,1,0:T(8,128)(2,1)}) custom-call(bf16[1024,1536]{1,0:T(8,128)(2,1)} %copy-done.22, bf16[3,1024,768]{2,1,0:T(8,128)(2,1)} %get-tuple-element.62.grads, bf16[1024,1152]{1,0:T(8,128)(2,1)} %get-tuple-element.63.weighted, bf16[1024,1536]{1,0:T(8,128)(2,1)} %maximum_maximum_fusion.1.cot), custom_call_target="tpu_custom_call" | custom-call | flops 10871635968 | bytes 25165824 | tf_op jit(solution)/shard_map/expert_grads/pallas_call | solution.py:1184
  264.8 68.9 %reduce_step.1 = (f32[512,768]{1,0:T(8,128)}, bf16[1024,1536]{1,0:T(8,128)(2,1)}, f32[8,1024]{1,0:T(8,128)}, f32[8,768]{1,0:T(8,128)}, bf16[2,144,384]{2,1,0:T(8,128)(2,1)}, /*index=5*/bf16[2,80,384]{2,1,0:T(8,128)(2,1)}) custom-call(bf16[1024,1536]{1,0:T(8,128)(2,1)} %get-tuple-element.58.partial, f32[8,1024]{1,0:T(8,128)} %get-tuple-element.59.vectors, ...), custom_call_target="tpu_custom_call" | custom-call | tf_op jit(solution)/shard_map/reduce_step/pallas_call | solution.py:588
  337.8 11.8 %attend_back.1 = (bf16[1024,640]{1,0:T(8,128)(2,1)S(1)}, f32[8,1024]{1,0:T(8,128)S(1)}) custom-call(bf16[1024,384]{1,0:T(8,128)(2,1)S(1)} %copy-done.14, bf16[1024,128]{1,0:T(8,128)(2,1)S(1)} %copy-done.18, bf16[1024,128]{1,0:T(8,128)(2,1)S(1)} %copy-done.21, bf16[1024,1536]{1,0:T(8,128)(2,1)} %get-tuple-element.66.hidden_low, ...), custom_call_target="tpu_custom_call" | custom-call | flops 4026531840 | bytes 3932160 | tf_op jit(solution)/shard_map/attend_back/pallas_call | solution.py:1372
  351.3 13.1 %attn_grads.1 = (bf16[1024,1536]{1,0:T(8,128)(2,1)}, bf16[1536,640]{1,0:T(8,128)(2,1)}, bf16[384,1536]{1,0:T(8,128)(2,1)}, f32[8,1024]{1,0:T(8,128)}, f32[512,768]{1,0:T(8,128)}, /*index=5*/f32[8,1536]{1,0:T(8,128)}) custom-call(bf16[1024,640]{1,0:T(8,128)(2,1)} %copy-done.23, bf16[1536,640]{1,0:T(8,128)(2,1)} %get-tuple-element.51.weight.qkv_weight, ...), custom_call_target="tpu_custom_call" | custom-call | flops 5234491392 | bytes 25165824 | tf_op jit(solution)/shard_map/attn_grads/pallas_call | solution.py:1475
  364.5 85.2 %final_step.1 = (f32[512,768]{1,0:T(8,128)}, bf16[512,768]{1,0:T(8,128)(2,1)}, f32[8,768]{1,0:T(8,128)}, bf16[2,2,16,32,1024]{4,3,2,1,0:T(8,128)(2,1)}) custom-call(bf16[1024,1536]{1,0:T(8,128)(2,1)} %get-tuple-element.73.partial, f32[8,1024]{1,0:T(8,128)} %get-tuple-element.74.vectors, bf16[512,768]{1,0:T(8,128)(2,1)} %tokens.3, f32[1024,128]{1,0:T(8,128)} %copy-done.3, ...), custom_call_target="tpu_custom_call" | custom-call | tf_op jit(solution)/shard_map/final_step/pallas_call | solution.py:910
  449.7 2.2 slice_bitcast_fusion.3
  459.7 2.1 pad_maximum_fusion.2
  462.4 2.3 fusion.4
  464.8 3.9 fusion.5
  469.2 3.3 fusion
  472.5 3.3 fusion.1
  475.8 3.3 fusion.2
  (171 shorter events, 44.0 us)
Async XLA Ops:
  7.2 153.6 %all-gather.8.cloned.1.call-start = ((), (), s32[]{:S(2)}) async-start(), calls=%async_computation.1 | async-start | bytes 9326592 | tf_op jit(solution)/shard_map/all_gather | solution.py:1572
  8.2 7.4 %copy-start.33 = (bf16[768,768]{1,0:T(8,128)(2,1)S(1)}, bf16[768,768]{1,0:T(8,128)(2,1)}, u32[]{:S(2)}) copy-start(bf16[768,768]{1,0:T(8,128)(2,1)} %param.17) | copy-start | bytes 3538948
  11.8 11.0 %collective-permute-start.3 = (bf16[108,768]{1,0:T(8,128)(2,1)S(1)}, bf16[108,768]{1,0:T(8,128)(2,1)S(1)}, u32[]{:S(2)}, u32[]{:S(2)}) collective-permute-start(bf16[108,768]{1,0:T(8,128)(2,1)S(1)} %pad_maximum_fusion.6), channel_id=1, source_target_pairs={{0,1},{1,0},{2,3},{3,2},{4,5},{5,4},{6,7},{7,6},{8,9},{9,8},{10,11... | collective-permute-start | bytes 497672 | tf_op jit(solution)/shard_map/ppermute | solution.py:31
  15.7 8.0 %copy-start.34 = (bf16[512,768]{1,0:T(8,128)(2,1)S(1)}, bf16[512,768]{1,0:T(8,128)(2,1)}, u32[]{:S(2)}) copy-start(bf16[512,768]{1,0:T(8,128)(2,1)} %cot.1) | copy-start | bytes 2359300
  15.7 10.8 %copy-start.46 = (f32[768]{0:T(1024)S(1)}, f32[768]{0:T(1024)}, u32[]{:S(2)}) copy-start(f32[768]{0:T(1024)} %param.14) | copy-start | bytes 9220
  15.7 10.8 %copy-start.47 = (f32[768]{0:T(1024)S(1)}, f32[768]{0:T(1024)}, u32[]{:S(2)}) copy-start(f32[768]{0:T(1024)} %param.15) | copy-start | bytes 9220
  15.7 10.9 %copy-start.41 = (s32[1024,4]{0,1:T(4,128)S(1)}, s32[1024,4]{0,1:T(4,128)}, u32[]{:S(2)}) copy-start(s32[1024,4]{0,1:T(4,128)} %param.22) | copy-start | bytes 49156
  15.7 10.9 %copy-start.45 = (bf16[768,6]{0,1:T(8,128)(2,1)S(1)}, bf16[768,6]{0,1:T(8,128)(2,1)}, u32[]{:S(2)}) copy-start(bf16[768,6]{0,1:T(8,128)(2,1)} %param.18) | copy-start | bytes 27652
  17.1 4.0 collective-permute-start.2
  17.9 3.2 collective-permute-start.1
  17.9 4.9 %collective-permute-start = (bf16[24,768]{1,0:T(8,128)(2,1)S(1)}, bf16[24,768]{1,0:T(8,128)(2,1)S(1)}, u32[]{:S(2)}, u32[]{:S(2)}) collective-permute-start(bf16[24,768]{1,0:T(8,128)(2,1)S(1)} %constant_dynamic-slice_fusion.7), channel_id=1, source_target_pairs={{0,1},{1,0},{2,3},{3,2},{4,5},{5,4},{6,7},{7,6},{8,9},{9,8},{10,11... | collective-permute-start | bytes 110600 | tf_op jit(solution)/shard_map/ppermute | solution.py:31
  23.6 438.8 %all-gather.6.cloned.1.call-start = ((), (), s32[]{:S(2)}) async-start(), calls=%async_computation | async-start | bytes 10948608 | tf_op jit(solution)/shard_map/all_gather | solution.py:1638
  23.7 66.2 %collective-permute-start.6 = (bf16[512,768]{1,0:T(8,128)(2,1)S(1)}, bf16[512,768]{1,0:T(8,128)(2,1)}, u32[]{:S(2)}, u32[]{:S(2)}) collective-permute-start(bf16[512,768]{1,0:T(8,128)(2,1)S(1)} %copy-done.34), channel_id=1, source_target_pairs={{0,2},{1,3},{2,0},{3,1},{4,6},{5,7},{6,4},{7,5},{8,10},{9,11},{10,... | collective-permute-start | bytes 2359304 | tf_op jit(solution)/shard_map/ppermute | solution.py:31
  24.6 68.0 %collective-permute-start.4 = (bf16[512,768]{1,0:T(8,128)(2,1)S(1)}, bf16[512,768]{1,0:T(8,128)(2,1)}, u32[]{:S(2)}, u32[]{:S(2)}) collective-permute-start(bf16[512,768]{1,0:T(8,128)(2,1)S(1)} %copy-done.34), channel_id=1, source_target_pairs={{0,3},{1,2},{2,1},{3,0},{4,7},{5,6},{6,5},{7,4},{8,11},{9,10},{10,... | collective-permute-start | bytes 2359304 | tf_op jit(solution)/shard_map/ppermute | solution.py:31
  26.5 63.2 %copy-start.43 = (f32[1,768]{1,0:T(1,128)}, f32[1,768]{1,0:T(1,128)S(1)}, u32[]{:S(2)}) copy-start(f32[1,768]{1,0:T(1,128)S(1)} %broadcast_in_dim.4.gain) | copy-start | bytes 9220
  26.5 63.2 %copy-start.44 = (f32[1,768]{1,0:T(1,128)}, f32[1,768]{1,0:T(1,128)S(1)}, u32[]{:S(2)}) copy-start(f32[1,768]{1,0:T(1,128)S(1)} %broadcast_in_dim.5.gain) | copy-start | bytes 9220
  89.3 5.3 %copy-start.6 = (bf16[1024,1536]{1,0:T(8,128)(2,1)S(1)}, bf16[1024,1536]{1,0:T(8,128)(2,1)}, u32[]{:S(2)}) copy-start(bf16[1024,1536]{1,0:T(8,128)(2,1)} %get-tuple-element.49.tok) | copy-start | bytes 9437188
  89.4 5.3 %copy-start.8 = (bf16[1536,640]{1,0:T(8,128)(2,1)S(1)}, bf16[1536,640]{1,0:T(8,128)(2,1)}, u32[]{:S(2)}) copy-start(bf16[1536,640]{1,0:T(8,128)(2,1)} %get-tuple-element.51.weight.qkv_weight) | copy-start | bytes 5898244
  89.4 5.3 %copy-start.9 = (f32[8,1536]{1,0:T(8,128)S(1)}, f32[8,1536]{1,0:T(8,128)}, u32[]{:S(2)}) copy-start(f32[8,1536]{1,0:T(8,128)} %get-tuple-element.50.small) | copy-start | bytes 147460
  91.8 57.3 %collective-permute-start.7 = (bf16[256,768]{1,0:T(8,128)(2,1)}, bf16[256,768]{1,0:T(8,128)(2,1)S(1)}, u32[]{:S(2)}, u32[]{:S(2)}) collective-permute-start(bf16[256,768]{1,0:T(8,128)(2,1)} %slice.194), channel_id=1, source_target_pairs={{0,3},{1,2},{2,1},{3,0},{4,7},{5,6},{6,5},{7,4},{8,11},{9,10},{10,... | collective-permute-start | bytes 1179656 | tf_op jit(solution)/shard_map/ppermute | solution.py:31
  94.4 54.8 %collective-permute-start.5 = (bf16[256,768]{1,0:T(8,128)(2,1)}, bf16[256,768]{1,0:T(8,128)(2,1)S(1)}, u32[]{:S(2)}, u32[]{:S(2)}) collective-permute-start(bf16[256,768]{1,0:T(8,128)(2,1)} %slice.193), channel_id=1, source_target_pairs={{0,2},{1,3},{2,0},{3,1},{4,6},{5,7},{6,4},{7,5},{8,10},{9,11},{10,... | collective-permute-start | bytes 1179656 | tf_op jit(solution)/shard_map/ppermute | solution.py:31
  94.7 11.3 %copy-start.5 = (s32[1024]{0:T(1024)S(1)}, s32[1024]{0:T(1024)}, u32[]{:S(2)}) copy-start(s32[1024]{0:T(1024)} %param.23) | copy-start | bytes 12292
  180.2 19.5 %copy-start.1 = (bf16[1024,1536]{1,0:T(8,128)(2,1)S(1)}, bf16[1024,1536]{1,0:T(8,128)(2,1)}, u32[]{:S(2)}) copy-start(bf16[1024,1536]{1,0:T(8,128)(2,1)} %gather_context.1.ctx) | copy-start | bytes 9437188
  180.3 19.5 %copy-start.7 = (bf16[1024,1536]{1,0:T(8,128)(2,1)S(1)}, bf16[1024,1536]{1,0:T(8,128)(2,1)}, u32[]{:S(2)}) copy-start(bf16[1024,1536]{1,0:T(8,128)(2,1)} %get-tuple-element.49.tok) | copy-start | bytes 9437188
  180.3 19.5 %copy-start.10 = (f32[8,1536]{1,0:T(8,128)S(1)}, f32[8,1536]{1,0:T(8,128)}, u32[]{:S(2)}) copy-start(f32[8,1536]{1,0:T(8,128)} %get-tuple-element.50.small) | copy-start | bytes 147460
  199.7 9.0 %copy-start.27 = (bf16[3,768,384]{2,1,0:T(8,128)(2,1)S(1)}, bf16[3,768,384]{2,1,0:T(8,128)(2,1)}, u32[]{:S(2)}) copy-start(bf16[3,768,384]{2,1,0:T(8,128)(2,1)} %get-tuple-element.117) | copy-start | bytes 5308420
  199.8 9.0 %copy-start.28 = (bf16[3,768,384]{2,1,0:T(8,128)(2,1)S(1)}, bf16[3,768,384]{2,1,0:T(8,128)(2,1)}, u32[]{:S(2)}) copy-start(bf16[3,768,384]{2,1,0:T(8,128)(2,1)} %get-tuple-element.118) | copy-start | bytes 5308420
  208.7 4.3 copy-start
  208.8 4.3 copy-start.4
  208.8 4.5 copy-start.22
  333.7 4.1 copy-start.14
  475.8 4.2 copy-start.39
  (27 other events, 50.7 us)
Sparse Core Ops, SparseCore 0:
  23.7 61.0 all-gather.7
  336.6 71.4 all-gather.5

commit v3 on v2

--- a/solution.py
+++ b/solution.py
@@ -42,14 +42,6 @@
     xs, zs, cs = dp_sizes()
     d = lax.axis_index("dp")
     return d // (zs * cs), (d // cs) % zs, d % cs
-
-
-def by_col(col, mine, other, axis):
-    return jnp.where(
-        col == 0,
-        jnp.concatenate([mine, other], axis=axis),
-        jnp.concatenate([other, mine], axis=axis),
-    )
 
 
 def nt(a, b):
@@ -153,6 +145,99 @@
             copy.wait_send()
 
     return forward, finish
+
+
+def unit_rows():
+    xs, zs, _ = dp_sizes()
+    return 768 // (xs * zs), min(SIDE, 768 // (xs * zs))
+
+
+def down_units(hid):
+    xs, zs, _ = dp_sizes()
+    return -(-(hid // unit_rows()[1]) // (xs * zs))
+
+
+def swap_units_kernel(out_weight, gate_weight, up_weight, down_weight, units, send, recv):
+    links = Links(send, recv)
+    links.greet([links.group(k) for k in (1, 2, 3)])
+    rows, down_rows = unit_rows()
+    pieces = links.xs * links.zs
+    place = links.x * links.zs + links.z
+    lanes = at(links.core * SIDE, SIDE, 128)
+    copies = []
+    for k in (1, 2, 3):
+        col = 1 - links.col if k & 1 else links.col
+        index = (place + col * (pieces // 2)) % pieces
+        copies.append(
+            links.go(
+                out_weight.at[index, :, lanes],
+                units.at[(k - 1) * rows : k * rows],
+                links.group(k),
+            )
+        )
+    count = gate_weight.shape[0] // 2
+    first = (1 - links.col) * count
+    for e in range(count):
+        i = links.used
+        links.used += 1
+        to = units.at[(3 + e) * rows : (4 + e) * rows]
+        either = [
+            pltpu.make_async_remote_copy(
+                src_ref=weight.at[first + e, place],
+                dst_ref=to,
+                send_sem=links.send.at[i],
+                recv_sem=links.recv.at[i],
+                device_id=links.group(1),
+                device_id_type=MESH,
+            )
+            for weight in (gate_weight, up_weight)
+        ]
+        for which in range(2):
+
+            @pl.when(links.core == which)
+            def _(copy=either[which]):
+                copy.start()
+
+        copies.append(either[0])
+    blocks = down_weight.shape[0] // 2
+    for j in range(down_units(blocks * down_rows)):
+        index = jnp.minimum(j * pieces + place, blocks - 1)
+        start = (3 + count) * rows + j * down_rows
+        copies.append(
+            links.go(
+                down_weight.at[(1 - links.col) * blocks + index, :, lanes],
+                units.at[start : start + down_rows],
+                links.group(1),
+            )
+        )
+    for copy in copies:
+        copy.wait()
+
+
+def swap_units(out_weight, gate_weight, up_weight, down_weight):
+    xs, zs, _ = dp_sizes()
+    pieces = xs * zs
+    rows, down_rows = unit_rows()
+    experts, width, hidden = gate_weight.shape
+    hid = experts // 2 * hidden
+    total = (3 + experts // 2) * rows + down_units(hid) * down_rows
+    return pl.pallas_call(
+        swap_units_kernel,
+        out_shape=jax.ShapeDtypeStruct((total, SIDE), bf16),
+        in_specs=[ANY] * 4,
+        out_specs=ANY,
+        scratch_shapes=[
+            pltpu.SemaphoreType.DMA((12,)),
+            pltpu.SemaphoreType.DMA((12,)),
+        ],
+        compiler_params=pltpu.CompilerParams(collective_id=4, has_side_effects=True),
+        name="swap_units",
+    )(
+        out_weight.reshape(pieces, rows, width),
+        gate_weight.reshape(experts, pieces, rows, hidden),
+        up_weight.reshape(experts, pieces, rows, hidden),
+        down_weight.reshape(-1, down_rows, width),
+    )
 
 
 def gather_inputs_kernel(
@@ -235,7 +320,7 @@
             jax.ShapeDtypeStruct((2 * width, SIDE + 2 * HEAD), bf16),
             jax.ShapeDtypeStruct((8, 2 * width), f32),
         ),
-        in_specs=[ANY] * 3,
+        in_specs=[WHOLE] * 3,
         out_specs=(ANY,) * 3,
         scratch_shapes=[
             pltpu.SemaphoreType.DMA((16,)),
@@ -280,7 +365,7 @@
     return pl.pallas_call(
         gather_context_kernel,
         out_shape=jax.ShapeDtypeStruct((rows, 4 * width), bf16),
-        in_specs=[ANY],
+        in_specs=[WHOLE],
         out_specs=ANY,
         scratch_shapes=[
             pltpu.SemaphoreType.DMA((6,)),
@@ -637,13 +722,10 @@
     gain,
     hidden_grad,
     router_part,
-    layer_partial,
-    hidden,
     qkv_part,
     out_part,
     small,
     input_grad,
-    layer_out,
     small_out,
     sums,
     near2,
@@ -652,12 +734,6 @@
     far3,
     out2,
     out3,
-    lnear2,
-    lnear3,
-    lfar2,
-    lfar3,
-    lout2,
-    lout3,
     vec_in,
     small_own,
     small_in,
@@ -763,9 +839,6 @@
     core_step(1)
     first_send(1)
     forward()
-    lforward, lfinish, ltotal, lsent = scatter_group(
-        links, layer_partial, lnear2, lnear3, lfar2, lfar3, lout2, lout3
-    )
     for copy in small_copies:
         copy.wait()
 
@@ -827,7 +900,6 @@
         home.append(mine)
         for k in range(1, sizes[1 - ab]):
             gather_copies.append(links.go(own_shard.at[ab], here, links.place(1 - ab, k)))
-    lforward()
 
     for copy in vec_copies:
         copy.wait()
@@ -863,14 +935,9 @@
     if cs == 2:
         block = sums.at[links.core]
         last = links.go(block, block, links.other_core())
-    lfinish()
-    for h in range(4):
-        rows = slice(h * 128, (h + 1) * 128)
-        layer_out[rows] = (hidden[rows] + ltotal(rows)).astype(bf16)
     if last is not None:
         last.wait()
     sent()
-    lsent()
     for pair in core_copies:
         for copy in pair:
             copy.wait_send()
@@ -887,14 +954,12 @@
     gain,
     hidden_grad,
     router_part,
-    layer_partial,
-    hidden,
     qkv_part,
     out_part,
     small,
 ):
     xs, zs, cs = dp_sizes()
-    width = hidden.shape[1]
+    width = hidden_grad.shape[1]
     quarter = HALF // 2
     cols = qkv_part.shape[1] + SIDE
     pad = pad16(SIDE // (xs * zs))
@@ -911,14 +976,12 @@
         final_kernel,
         out_shape=(
             jax.ShapeDtypeStruct((HALF, width), f32),
-            jax.ShapeDtypeStruct((HALF, width), bf16),
             jax.ShapeDtypeStruct((8, width), f32),
             jax.ShapeDtypeStruct((cs, 2, xs * zs, pad, cols), bf16),
         ),
-        in_specs=[WHOLE] * 12,
-        out_specs=(WHOLE, WHOLE, WHOLE, ANY),
+        in_specs=[WHOLE] * 10,
+        out_specs=(WHOLE, WHOLE, ANY),
         scratch_shapes=group_buffers
-        + group_buffers
         + [
             VMEM((3,) + vectors.shape, f32),
             VMEM((4, 8, width), f32),
@@ -946,8 +1009,6 @@
         gain,
         hidden_grad,
         router_part,
-        layer_partial,
-        hidden,
         qkv_part,
         out_part,
         small,
@@ -1027,21 +1088,66 @@
     )(tokens_all, small, weight, routes, cosine, sine)
 
 
-def mix_kernel(ctx, tok, weight, small, normed_ref, hidden_ref, scale_ref):
-    hidden = tok[...].astype(f32) + nn(ctx[...], weight[...])
-    width = hidden.shape[1]
-    scale = lax.rsqrt(jnp.sum(hidden * hidden, axis=1, keepdims=True) * (1.0 / width) + EPS)
+def mix_kernel(
+    ctx,
+    tok,
+    small,
+    out_weight,
+    units,
+    normed_ref,
+    hidden_ref,
+    scale_ref,
+    quarter_ref,
+    weight,
+    sem,
+):
+    pieces, rows = weight.shape[1:3]
+    full = weight.shape[3]
+    width = full // 2
+
+    @pl.when(pl.program_id(0) == 0)
+    def _():
+        col = lax.axis_index("col")
+        half = pieces // 2
+        copies = []
+
+        def fetch(src, dst):
+            copy = pltpu.make_async_copy(src, dst, sem.at[len(copies)])
+            copy.start()
+            copies.append(copy)
+
+        for h in range(2):
+            which = col if h == 0 else 1 - col
+            fetch(
+                out_weight.at[pl.ds(which * half, half)],
+                weight.at[0, h * half : (h + 1) * half, :, 0:width],
+            )
+        for k in (1, 2, 3):
+            for core in range(2):
+                first = (k & 1) * width + core * SIDE
+                fetch(
+                    units.at[:, core, (k - 1) * rows : k * rows],
+                    weight.at[k // 2, :, :, first : first + SIDE],
+                )
+        for copy in copies:
+            copy.wait()
+        quarter_ref[...] = weight[0, 0:half].reshape(SIDE, full)
+
+    hidden = tok[...].astype(f32) + nn(ctx[...], weight[...].reshape(full, full))
+    scale = lax.rsqrt(jnp.sum(hidden * hidden, axis=1, keepdims=True) * (1.0 / full) + EPS)
     normed_ref[...] = (hidden * scale * small[7:8, :]).astype(bf16)
     scale_ref[...] = jnp.broadcast_to(scale, scale_ref.shape)
 
-    @pl.when(pl.program_id(0) < 2)
+    @pl.when(pl.program_id(0) == 0)
     def _():
-        hidden_ref[...] = hidden[:, : width // 2]
-
-
-def mix(context_all, tokens_all, weight, small):
+        hidden_ref[...] = hidden[:, :width]
+
+
+def mix(context_all, tokens_all, small, out_weight, units):
     total, width = tokens_all.shape
-    step = 256
+    step = HALF
+    pieces = units.shape[0]
+    rows_unit = width // 2 // pieces
 
     def rows(cols):
         return pl.BlockSpec((step, cols), lambda i: (i, 0))
@@ -1054,46 +1160,120 @@
         grid=(total // step,),
         out_shape=(
             jax.ShapeDtypeStruct((total, width), bf16),
-            jax.ShapeDtypeStruct((total // 2, width // 2), f32),
+            jax.ShapeDtypeStruct((HALF, width // 2), f32),
             jax.ShapeDtypeStruct((total, 128), f32),
-        ),
-        in_specs=[rows(width), rows(width), whole(weight.shape), whole(small.shape)],
+            jax.ShapeDtypeStruct((SIDE, width), bf16),
+        ),
+        in_specs=[rows(width), rows(width), whole(small.shape), ANY, ANY],
         out_specs=(
             rows(width),
-            pl.BlockSpec((step, width // 2), lambda i: (jnp.minimum(i, 1), 0)),
+            whole((HALF, width // 2)),
             rows(128),
-        ),
-        compiler_params=pltpu.CompilerParams(vmem_limit_bytes=40 * 2**20),
+            whole((SIDE, width)),
+        ),
+        scratch_shapes=[
+            VMEM((2, pieces, rows_unit, width), bf16),
+            pltpu.SemaphoreType.DMA((8,)),
+        ],
+        compiler_params=pltpu.CompilerParams(vmem_limit_bytes=48 * 2**20),
         cost_estimate=pl.CostEstimate(
             flops=2 * total * width * width, bytes_accessed=14 * 2**20, transcendentals=0
         ),
         name="mix",
-    )(context_all, tokens_all, weight, small)
+    )(context_all, tokens_all, small, out_weight, units)
 
 
 def experts_kernel(
-    normed, cot, gate_up, down, gates, weighted_ref, grad_ref, back_ref, out_ref, vec_ref
+    normed,
+    cot_own,
+    cot_1a,
+    cot_1b,
+    cot_2,
+    cot_3,
+    gates,
+    gate_weight,
+    up_weight,
+    down_weight,
+    units,
+    weighted_ref,
+    grad_ref,
+    back_ref,
+    vec_ref,
+    cot,
+    own_ref,
+    o1a,
+    o1b,
+    o2a,
+    o2b,
+    o3a,
+    o3b,
+    gate_up,
+    down,
+    sem,
 ):
     col = lax.axis_index("col")
-    count, _, both = gate_up.shape
+    step = pl.program_id(0)
+    count, _, pieces, unit, both = gate_up.shape
+    blocks, down_unit, full = down.shape
+    width = full // 2
     hidden = both // 2
     rows = normed.shape[0]
+    quarter = HALF // 2
+    copies = []
+
+    def fetch(src, dst):
+        copies.append(pltpu.make_async_copy(src, dst, sem.at[len(copies)]))
+
+    for e in range(count):
+        for which, weight in enumerate((gate_weight, up_weight)):
+            cols = slice(which * hidden, (which + 1) * hidden)
+            fetch(weight.at[col * count + e], gate_up.at[e, 0, :, :, cols])
+            fetch(
+                units.at[:, which, (3 + e) * unit : (4 + e) * unit], gate_up.at[e, 1, :, :, cols]
+            )
+    fetch(down_weight.at[pl.ds(col * blocks, blocks)], down.at[:, :, 0:width])
+    for j in range(-(-blocks // pieces)):
+        n = min(pieces, blocks - j * pieces)
+        start = (3 + count) * unit + j * down_unit
+        for core in range(2):
+            first = width + core * SIDE
+            fetch(
+                units.at[0:n, core, start : start + down_unit],
+                down.at[j * pieces : j * pieces + n, :, first : first + SIDE],
+            )
+
+    @pl.when(step == 0)
+    def _():
+        for copy in copies:
+            copy.start()
+        cot[:, :width] = cot_own[...]
+        cot[0:quarter, width:] = cot_1a[...]
+        cot[quarter:, width:] = cot_1b[...]
+        for copy in copies:
+            copy.wait()
+
+    @pl.when(step == 1)
+    def _():
+        cot[:, :width] = cot_2[...]
+        cot[:, width:] = cot_3[...]
+
     lanes = lax.broadcasted_iota(jnp.int32, (rows, 128), 1)
     vec = jnp.zeros((rows, 128), f32)
     inner = jnp.zeros((rows, 1), f32)
     back = out = None
     x, y = normed[...], cot[...]
     for e in range(count):
+        weight = gate_up[e].reshape(full, both)
+        down_e = down[...].reshape(count, hidden, full)[e]
         here = lanes == col * count + e
         gate = jnp.sum(jnp.where(here, gates[...], 0.0), axis=1, keepdims=True)
-        both_pre = nn(x, gate_up[e])
+        both_pre = nn(x, weight)
         gate_pre, up_pre = both_pre[:, :hidden], both_pre[:, hidden:]
         sigmoid = 1.0 / (1.0 + jnp.exp(-gate_pre))
         silu = gate_pre * sigmoid
         activated = silu * up_pre
         weighted = (gate * activated).astype(bf16)
         weighted_ref[:, e * hidden : (e + 1) * hidden] = weighted
-        down_e = down[e * hidden : (e + 1) * hidden]
         weighted_grad = nt(y, down_e)
         vec = vec + jnp.where(
             here, jnp.sum(activated * weighted_grad, axis=1, keepdims=True), 0.0
@@ -1104,20 +1284,38 @@
         inner = inner + jnp.sum(gate_grad * gate_pre + up_grad * up_pre, axis=1, keepdims=True)
         grads = jnp.concatenate([gate_grad, up_grad], axis=1).astype(bf16)
         grad_ref[e] = grads
-        back_e = nt(grads, gate_up[e])
+        back_e = nt(grads, weight)
         out_e = nn(weighted, down_e)
         back = back_e if back is None else back + back_e
         out = out_e if out is None else out + out_e
     back_ref[...] = back.astype(bf16)
-    out_ref[...] = out.astype(bf16)
     vec = jnp.where(lanes == 6, inner, vec)
     vec_ref[...] = vec.T[0:8, :]
 
-
-def experts_step(normed, cot, gate_up, down, gates):
+    @pl.when(step == 0)
+    def _():
+        own_ref[...] = out[:, :width]
+        o1a[...] = out[:quarter, width:].astype(bf16)
+        o1b[...] = out[quarter:, width:].astype(bf16)
+
+    @pl.when(step == 1)
+    def _():
+        o2a[...] = out[:quarter, :width].astype(bf16)
+        o2b[...] = out[quarter:, :width].astype(bf16)
+        o3a[...] = out[:quarter, width:].astype(bf16)
+        o3b[...] = out[quarter:, width:].astype(bf16)
+
+
+def experts_step(normed, cot_blocks, gates, gate_weight, up_weight, down_weight, units):
     total, width = normed.shape
-    step = 256
-    count, _, both = gate_up.shape
+    step = HALF
+    experts, own_width, hidden = gate_weight.shape
+    count = experts // 2
+    both = 2 * hidden
+    hid = count * hidden
+    pieces = units.shape[0]
+    unit, down_unit = unit_rows()
+    quarter = jax.ShapeDtypeStruct((HALF // 2, own_width), bf16)
 
     def rows(cols):
         return pl.BlockSpec((step, cols), lambda i: (i, 0))
@@ -1129,40 +1327,61 @@
         experts_kernel,
         grid=(total // step,),
         out_shape=(
-            jax.ShapeDtypeStruct((total, down.shape[0]), bf16),
+            jax.ShapeDtypeStruct((total, hid), bf16),
             jax.ShapeDtypeStruct((count, total, both), bf16),
             jax.ShapeDtypeStruct((total, width), bf16),
+            jax.ShapeDtypeStruct((8, total), f32),
             jax.ShapeDtypeStruct((total, width), bf16),
-            jax.ShapeDtypeStruct((8, total), f32),
-        ),
-        in_specs=[
-            rows(width),
-            rows(width),
-            whole(gate_up.shape),
-            whole(down.shape),
-            rows(128),
-        ],
+            jax.ShapeDtypeStruct((HALF, own_width), f32),
+        )
+        + (quarter,) * 6,
+        in_specs=[rows(width)]
+        + [whole(block.shape) for block in cot_blocks]
+        + [rows(128)]
+        + [ANY] * 4,
         out_specs=(
-            rows(down.shape[0]),
+            rows(hid),
             pl.BlockSpec((count, step, both), lambda i: (0, i, 0)),
             rows(width),
+            pl.BlockSpec((8, step), lambda i: (0, i)),
             rows(width),
-            pl.BlockSpec((8, step), lambda i: (0, i)),
-        ),
-        compiler_params=pltpu.CompilerParams(vmem_limit_bytes=58 * 2**20),
+            whole((HALF, own_width)),
+        )
+        + (whole(quarter.shape),) * 6,
+        scratch_shapes=[
+            VMEM((count, 2, pieces, unit, both), bf16),
+            VMEM((hid // down_unit, down_unit, width), bf16),
+            pltpu.SemaphoreType.DMA((24,)),
+        ],
+        compiler_params=pltpu.CompilerParams(vmem_limit_bytes=60 * 2**20),
         cost_estimate=pl.CostEstimate(
             flops=6 * total * width * count * both, bytes_accessed=26 * 2**20, transcendentals=0
         ),
         name="experts",
-    )(normed, cot, gate_up, down, gates)
-
-
-def expert_grads_kernel(normed, grads, weighted, cot, up_ref, down_ref):
+    )(
+        normed,
+        *cot_blocks,
+        gates,
+        gate_weight.reshape(experts, pieces, unit, hidden),
+        up_weight.reshape(experts, pieces, unit, hidden),
+        down_weight.reshape(-1, down_unit, own_width),
+        units,
+    )
+
+
+def expert_grads_kernel(normed, grads, weighted, cot, up_ref, down_ref, normed_t):
     width = normed.shape[1]
     half = width // 2
     hidden = weighted.shape[1]
+
+    @pl.when(pl.program_id(0) == 0)
+    def _():
+        for i in range(4):
+            rows = slice(i * 256, (i + 1) * 256)
+            normed_t[:, rows] = normed[rows].T
+
     for ab in range(2):
-        part = tn(normed[:, ab * half : (ab + 1) * half], grads[0])
+        part = nn(normed_t[ab * half : (ab + 1) * half], grads[0])
         for which in range(2):
             up_ref[which, ab] = part[:, which * hidden : (which + 1) * hidden].astype(bf16)
     part = tn(weighted[...], cot[...])
@@ -1198,6 +1417,7 @@
             pl.BlockSpec((2, 2, half, hidden), lambda e: (0, 0, e, 0)),
             pl.BlockSpec((2, 2, hidden, hidden), lambda e: (0, 0, e, 0)),
         ),
+        scratch_shapes=[VMEM((width, total), bf16)],
         compiler_params=pltpu.CompilerParams(vmem_limit_bytes=56 * 2**20),
         cost_estimate=pl.CostEstimate(
             flops=3 * total * width * count * both, bytes_accessed=24 * 2**20, transcendentals=0
@@ -1492,6 +1712,108 @@
     )(grads, qkv_weight, normed, context, hidden_low, small, gates, vec_sums, vec_part, ffn_part)
 
 
+def expert_finish_kernel(col_ref, by_x, by_z, gate_ref, up_ref, down_ref):
+    ab = pl.program_id(0)
+    rows = gate_ref.shape[0]
+    down_rows = down_ref.shape[0]
+
+    def write(block):
+        pieces = block.shape[0]
+        step, down_step = rows // pieces, down_rows // pieces
+        for p in range(pieces):
+            here = slice(p * step, (p + 1) * step)
+            gate_ref[here] = block[p, 0, 0, 0:step].astype(f32)
+            up_ref[here] = block[p, 1, 0, 0:step].astype(f32)
+            here = slice(p * down_step, (p + 1) * down_step)
+            for core in range(2):
+                down_ref[here, core * SIDE : (core + 1) * SIDE] = block[
+                    p, core, 0, step : step + down_step
+                ].astype(f32)
+
+    @pl.when(ab == 0)
+    def _():
+        write(by_x.at[0])
+
+    @pl.when(ab == 1)
+    def _():
+        write(by_z.at[:, 0])
+
+
+def expert_finish(sums, col, up_rows, down_rows):
+    xs, zs, cs = dp_sizes()
+    piece = sums.shape[-2]
+
+    def half(ab, col_ref):
+        return jnp.where(ab == 0, col_ref[0], 1 - col_ref[0])
+
+    def out_spec(rows, cols):
+        return pl.BlockSpec(
+            (rows, cols), lambda ab, j, col_ref: (half(ab, col_ref) * xs + j, 0)
+        )
+
+    return pl.pallas_call(
+        expert_finish_kernel,
+        grid_spec=pltpu.PrefetchScalarGridSpec(
+            num_scalar_prefetch=1,
+            grid=(2, xs),
+            in_specs=[
+                pl.BlockSpec(
+                    (1, zs, cs, 1, piece, SIDE),
+                    lambda ab, j, col_ref: (jnp.where(ab == 0, j, xs - 1), 0, 0, 0, 0, 0),
+                ),
+                pl.BlockSpec(
+                    (xs, 1, cs, 1, piece, SIDE),
+                    lambda ab, j, col_ref: (0, jnp.where(ab == 0, 0, j), 0, 1, 0, 0),
+                ),
+            ],
+            out_specs=(
+                out_spec(up_rows * zs, SIDE),
+                out_spec(up_rows * zs, SIDE),
+                out_spec(down_rows * zs, 2 * SIDE),
+            ),
+        ),
+        out_shape=(
+            jax.ShapeDtypeStruct((2 * up_rows * xs * zs, SIDE), f32),
+            jax.ShapeDtypeStruct((2 * up_rows * xs * zs, SIDE), f32),
+            jax.ShapeDtypeStruct((2 * down_rows * xs * zs, 2 * SIDE), f32),
+        ),
+        compiler_params=pltpu.CompilerParams(vmem_limit_bytes=48 * 2**20),
+        name="expert_finish",
+    )(col.reshape(1), sums, sums)
+
+
+def attn_finish_kernel(sums, qkv_ref, out_ref):
+    col = lax.axis_index("col")
+    cores, _, pieces = sums.shape[:3]
+    rows = SIDE // pieces
+    cols = SIDE + 2 * HEAD
+    for core in range(cores):
+        kept = None
+        here = slice(core * SIDE, (core + 1) * SIDE)
+        for ab in range(2):
+            half = col if ab == 0 else 1 - col
+            block = sums[core, ab].astype(f32)[:, 0:rows].reshape(SIDE, cols + SIDE)
+            qkv_ref[here, at(half * SIDE, SIDE, 128)] = block[:, 0:SIDE]
+            out_ref[at(half * SIDE, SIDE), here] = block[:, cols:]
+            pair = block[:, SIDE:cols]
+            kept = pair if kept is None else kept + pair
+        qkv_ref[here, 2 * SIDE :] = kept
+
+
+def attn_finish(sums):
+    return pl.pallas_call(
+        attn_finish_kernel,
+        out_shape=(
+            jax.ShapeDtypeStruct((2 * SIDE, 2 * SIDE + 2 * HEAD), f32),
+            jax.ShapeDtypeStruct((2 * SIDE, 2 * SIDE), f32),
+        ),
+        in_specs=[WHOLE],
+        out_specs=(WHOLE, WHOLE),
+        compiler_params=pltpu.CompilerParams(vmem_limit_bytes=48 * 2**20),
+        name="attn_finish",
+    )(sums)
+
+
 def turn_tables(places):
     steps_up = jnp.arange(HEAD // 2, dtype=f32) * (2.0 / HEAD)
     inverse = jnp.exp(-math.log(ROPE_BASE) * steps_up)
@@ -1500,24 +1822,6 @@
     return (
         jnp.concatenate([cosine, cosine], axis=1),
         jnp.concatenate([-sine, sine], axis=1),
-    )
-
-
-def gather4(x):
-    half = x.shape[0] // 2
-    a = flip(x, 2)
-    b = flip(x, 3)
-    c = jnp.concatenate([flip(b[:half], 2), flip(a[half:], 3)], axis=0)
-    return x, c, a, b
-
-
-def two_by_two(blocks):
-    return jnp.concatenate(
-        [
-            jnp.concatenate([blocks[0], blocks[1]], axis=1),
-            jnp.concatenate([blocks[2], blocks[3]], axis=1),
-        ],
-        axis=0,
     )
 
 
@@ -1537,70 +1841,18 @@
 ):
     row = lax.axis_index("row")
     col = lax.axis_index("col")
-    dp = lax.axis_index("dp")
-    dp_count = lax.axis_size("dp")
     xs, zs, cs = dp_sizes()
     own_rows, own_width = tokens.shape
     total = 2 * own_rows
+    quarter = own_rows // 2
     experts, _, hidden = gate_weight.shape
     own_experts = experts // 2
     hid = own_experts * hidden
-    other_col = 1 - col
-
-    rolled = jnp.where(col == 0, out_weight, jnp.roll(out_weight, SIDE, axis=0))
-    share = own_width // dp_count
-
-    def dp_rows(v, count):
-        return lax.dynamic_slice_in_dim(v, dp * count, count, v.ndim - 2)
-
-    out_piece = dp_rows(rolled, share)
-    out_pieces = jnp.concatenate([flip(out_piece, 1), flip(out_piece, 2), flip(out_piece, 3)], 0)
-
-    def expert_half(v, which):
-        return lax.dynamic_slice_in_dim(v, which * own_experts, own_experts, 0)
-
-    gate_up_piece = jnp.concatenate(
-        [
-            dp_rows(expert_half(gate_weight, other_col), share),
-            dp_rows(expert_half(up_weight, other_col), share),
-        ],
-        axis=2,
-    ).reshape(own_experts * share, own_width)
-    down_share = hid // dp_count
-    down_piece = dp_rows(expert_half(down_weight, other_col).reshape(hid, own_width), down_share)
-    expert_pieces = flip(jnp.concatenate([gate_up_piece, down_piece], axis=0), 1)
-    gathered = lax.all_gather(
-        jnp.concatenate([out_pieces, expert_pieces], axis=0), "dp", axis=0, tiled=False
-    )
-    out_other = (
-        gathered[:, : 3 * share]
-        .reshape(dp_count, 3, share, own_width)
-        .transpose(1, 0, 2, 3)
-        .reshape(3, own_width, own_width)
-    )
-    gate_up_other = (
-        gathered[:, 3 * share : 3 * share + own_experts * share]
-        .reshape(dp_count, own_experts, share, own_width)
-        .transpose(1, 0, 2, 3)
-        .reshape(own_experts, own_width, own_width)
-    )
-    down_other = gathered[:, (3 + own_experts) * share :].reshape(hid, own_width)
-
-    o1, o2, o3 = out_other[0], out_other[1], out_other[2]
-    out_local = jnp.concatenate(
-        [
-            jnp.concatenate([rolled, o2], axis=0),
-            jnp.concatenate([o1[SIDE:], o1[:SIDE], o3[SIDE:], o3[:SIDE]], axis=0),
-        ],
-        axis=1,
-    )
-    gate_up_own = jnp.concatenate(
-        [expert_half(gate_weight, col), expert_half(up_weight, col)], axis=2
-    )
-    gate_up_local = jnp.concatenate([gate_up_own, gate_up_other], axis=1)
-    down_local = jnp.concatenate(
-        [expert_half(down_weight, col).reshape(hid, own_width), down_other], axis=1
-    )
+    pieces = xs * zs
+
+    units = swap_units(out_weight, gate_weight, up_weight, down_weight)
+    units = lax.all_gather(units, "dp", axis=0, tiled=False)
+    units = units.reshape((pieces, cs) + units.shape[1:])
 
     def own_order(v):
         return jnp.where(row == 0, v, jnp.roll(v, own_rows, axis=0))
@@ -1612,16 +1864,45 @@
     )
 
     tokens_all, qkv_local, small_all = gather_inputs(tokens, qkv_weight, small)
+    cot_own, tokens_all = lax.optimization_barrier((cotangent, tokens_all))
+    cot_2 = flip(cot_own, 2)
+    cot_3 = flip(cot_own, 3)
     normed_one, queries, keys, values, gates, scale_one = project(
         tokens_all, small_all, qkv_local, routes_local, cosine, sine
     )
     context, lse = attend(queries, keys, values, segments)
+    cot_1a = flip(cot_3[:quarter], 2)
+    cot_1b = flip(cot_2[quarter:], 3)
     context_all = gather_context(context)
-    cot_all = two_by_two(gather4(cotangent))
-    normed_two, hidden_own, scale_two = mix(context_all, tokens_all, out_local, small_all)
-    weighted, pre_grads, normed_two_part, layer_part, expert_vec = experts_step(
-        normed_two, cot_all, gate_up_local, down_local, gates
-    )
+    normed_two, hidden_own, scale_two, out_quarter = mix(
+        context_all, tokens_all, small_all, out_weight.reshape(pieces, -1, own_width), units
+    )
+    (
+        weighted,
+        pre_grads,
+        normed_two_part,
+        expert_vec,
+        cot_all,
+        layer_own,
+        o1a,
+        o1b,
+        o2a,
+        o2b,
+        o3a,
+        o3b,
+    ) = experts_step(
+        normed_two,
+        (cot_own, cot_1a, cot_1b, cot_2, cot_3),
+        gates,
+        gate_weight,
+        up_weight,
+        down_weight,
+        units,
+    )
+    pass_3 = flip(o1a, 2)
+    pass_2 = flip(o1b, 3)
+    far_3b = flip(o3b, 3)
+    far_2a = flip(o2a, 2)
     gate_up_grads, down_grads = expert_grads(normed_two, pre_grads, weighted, cot_all)
     hidden_grad, hidden_low, vec_sums, ffn_part, shard_up, shard_down = reduce_step(
         normed_two_part,
@@ -1633,17 +1914,19 @@
         gate_up_grads,
         down_grads,
     )
-    up_rows = own_experts * own_width // (xs * zs)
-    down_rows = hid // (xs * zs)
+    up_rows = own_experts * own_width // pieces
+    down_rows = hid // pieces
     expert_sums = lax.all_gather(
         jnp.concatenate([shard_up[:, :up_rows], shard_down[:, :down_rows]], axis=1),
         "dp",
         axis=0,
         tiled=False,
     ).reshape(xs, zs, cs, 2, up_rows + down_rows, SIDE)
+    far_3a = flip((o3a.astype(f32) + pass_3.astype(f32)).astype(bf16), 3)
+    far_2b = flip((o2b.astype(f32) + pass_2.astype(f32)).astype(bf16), 2)
 
     projected_grad, vec_part = attend_back(
-        queries, keys, values, hidden_low, out_local[:SIDE], segments, lse, cosine, sine
+        queries, keys, values, hidden_low, out_quarter, segments, lse, cosine, sine
     )
     input_part, qkv_part, out_part, input_vec, router_part, small_part = attn_grads(
         projected_grad,
@@ -1657,7 +1940,13 @@
         vec_part,
         ffn_part,
     )
-    input_grad, layer_out, small_sums, attn_sums = final_step(
+    layer_out = (
+        hidden_own
+        + layer_own
+        + jnp.concatenate([far_2a, far_2b], axis=0).astype(f32)
+        + jnp.concatenate([far_3a, far_3b], axis=0).astype(f32)
+    ).astype(bf16)
+    input_grad, small_sums, attn_sums = final_step(
         input_part,
         input_vec,
         tokens,
@@ -1665,8 +1954,6 @@
         attn_gain[None],
         hidden_grad,
         router_part,
-        layer_part,
-        hidden_own,
         qkv_part,
         out_part,
         small_part,
@@ -1674,50 +1961,11 @@
     router_grad = small_sums[:experts].T
     attn_gain_grad = small_sums[6]
     ffn_gain_grad = small_sums[7]
-
-    def spread(v, swap):
-        v = v.transpose(1, 0, 2, 3) if swap else v
-        return v.reshape(-1, v.shape[-1])
-
-    def expert_out(rows, which):
-        which = which % cs
-        return [spread(expert_sums[:, :, which, ab, rows], ab == 1) for ab in range(2)]
-
-    def gate_or_up(which):
-        mine, other = expert_out(slice(0, up_rows), which)
-        shape = (own_experts, own_width, hidden)
-        return by_col(col, mine.reshape(shape), other.reshape(shape), 0).astype(f32)
-
-    gate_grad = gate_or_up(0)
-    up_grad = gate_or_up(1)
-    down_mine, down_peer = [
-        jnp.concatenate(list(parts), axis=1)
-        for parts in zip(
-            expert_out(slice(up_rows, None), 0), expert_out(slice(up_rows, None), 1)
-        )
-    ]
-    shape = (own_experts, hidden, own_width)
-    down_grad = by_col(col, down_mine.reshape(shape), down_peer.reshape(shape), 0).astype(f32)
-
-    attn_rows = SIDE // (xs * zs)
-    qkv_cols = SIDE + 2 * HEAD
-
-    def attn_out(ab):
-        block = attn_sums[:, ab, :, :attn_rows]
-        qkv = block[..., :qkv_cols].reshape(own_width * cs // 2, qkv_cols)
-        out = block[..., qkv_cols:].transpose(1, 2, 0, 3).reshape(SIDE, SIDE * cs)
-        return qkv.astype(f32), out.astype(f32)
-
-    qkv_mine, out_mine = attn_out(0)
-    qkv_peer, out_peer = attn_out(1)
-    qkv_grad = jnp.concatenate(
-        [
-            by_col(col, qkv_mine[:, :SIDE], qkv_peer[:, :SIDE], 1),
-            qkv_mine[:, SIDE:] + qkv_peer[:, SIDE:],
-        ],
-        axis=1,
-    )
-    out_grad = by_col(col, out_mine, out_peer, 0)
+    qkv_grad, out_grad = attn_finish(attn_sums)
+    gate_grad, up_grad, down_grad = expert_finish(expert_sums, col, up_rows, down_rows)
+    gate_grad = gate_grad.reshape(experts, own_width, hidden)
+    up_grad = up_grad.reshape(experts, own_width, hidden)
+    down_grad = down_grad.reshape(experts, hidden, own_width)
     return (
         layer_out,
         input_grad,

time: 494 us -> 405 us (0.82)
  other arithmetic: 57.9 us -> 6.03 us
  local copies, waits for them, and re-layouts: 62.3 us -> 20.8 us
  Pallas kernels: 340 us -> 347 us
    concatenate x7 -> x0, other arithmetic: 39.6 us -> none  [the longest x1 19.5 us: local(): jnp.concatenate([jnp.concatenate([rolled, o2], axis=0), jnp.concatenate([...]
    pallas_call x0 -> x3, Pallas kernels: none -> 26.7 us  [the longest x1 12.8 us: expert_finish(): pl.pallas_call(expert_finish_kernel, grid_spec=pltpu.PrefetchScalarGridSp...]
    pallas_call x1, Pallas kernels: 59.7 us -> 36.8 us  [gather_inputs(): pl.pallas_call(gather_inputs_kernel, out_shape=(jax.ShapeDtypeStruct((2 *...]
    slice x15 -> x2, local copies, waits for them, and re-layouts: 22.5 us -> 3.53 us  [the longest x1 1.77 us: local(): cot_1b = flip(cot_2[quarter:], 3)]
    pallas_call x1, Pallas kernels: 34.6 us -> 47.5 us  [experts_step(): pl.pallas_call(experts_kernel, grid=(total // step,), out_shape=(jax.Shap...]
    pallas_call x1, Pallas kernels: 85.2 us -> 72.4 us  [final_step(): pl.pallas_call(final_kernel, out_shape=(jax.ShapeDtypeStruct((HALF, width...]
    convert_element_type x7 -> x3, other arithmetic: 10.6 us -> 1.38 us  [the longest x1 1.19 us: local(): layer_out = (hidden_own + layer_own + jnp.concatenate([far_2a, far_2b], a...]
    dynamic_slice x5 -> x0, local copies, waits for them, and re-layouts: 8.79 us -> none  [the longest x2 7.8 us: expert_half(): return lax.dynamic_slice_in_dim(v, which * own_experts, own_experts, 0)]
  transfers between devices with their start and end apart: 10 -> 12, of which waited for: 2 -> 0; matrix products, arithmetic and copies ran while one was open for 7% -> 3% of each run, Pallas kernels for 43% -> 48%
where the time goes in v3:
time: 405 us; the launch traced here: 399 us
  Pallas kernels  347 us (86%)
  local copies, waits for them, and re-layouts  20.8 us (5%)
  between operations  14.7 us (4%)
  starting transfers between devices  10.2 us (3%)
  other arithmetic  6.03 us (1%)
    pallas_call x1, Pallas kernels, final_step(): pl.pallas_call(final_kernel, out_shape=(jax.ShapeDtypeStruct((HALF, width...  72.4 us
    pallas_call x1, Pallas kernels, reduce_step(): pl.pallas_call(reduce_kernel, out_shape=(jax.ShapeDtypeStruct((HALF, widt...  67.4 us
    pallas_call x1, Pallas kernels, experts_step(): pl.pallas_call(experts_kernel, grid=(total // step,), out_shape=(jax.Shap...  47.5 us
    pallas_call x1, Pallas kernels, gather_inputs(): pl.pallas_call(gather_inputs_kernel, out_shape=(jax.ShapeDtypeStruct((2 *...  36.8 us
    pallas_call x1, Pallas kernels, gather_context(): pl.pallas_call(gather_context_kernel, out_shape=jax.ShapeDtypeStruct((row...  29.3 us
    pallas_call x1, Pallas kernels, expert_grads(): pl.pallas_call(expert_grads_kernel, grid=(count,), out_shape=(jax.ShapeDt...  17.9 us
    unnamed x64, local copies, waits for them, and re-layouts  13.9 us
    pallas_call x1, Pallas kernels, attn_grads(): pl.pallas_call(attn_grads_kernel, out_shape=(jax.ShapeDtypeStruct((total,...  13.1 us
  transfers between devices with their start and end apart: 12, of which 0 were waited for; matrix products, arithmetic and copies ran while one was open for 3% of the time, Pallas kernels for 48%

profile of v3, /device:TPU:1, one launch (start us, length us, event | category | flops | bytes accessed | tf_op | source)
XLA Modules:
  0.0 398.6 jit_solution(17098584272706280631)
XLA Ops:
  7.3 11.0 %swap_units.1 = bf16[384,384]{1,0:T(8,128)(2,1)} custom-call(bf16[16,48,768]{2,1,0:T(8,128)(2,1)} %bitcast.16, bf16[6,16,48,384]{3,2,1,0:T(8,128)(2,1)} %bitcast.23, bf16[6,16,48,384]{3,2,1,0:T(8,128)(2,1)} %bitcast.25, bf16[48,48,768]{2,1,0:T(8,128)(2,1)} %bitcast.27), custom_call_target="tpu_custom_call" | custom-call | tf_op jit(solution)/shard_map/swap_units/pallas_call | solution.py:224
  19.1 36.8 %gather_inputs.1 = (bf16[1024,1536]{1,0:T(8,128)(2,1)}, bf16[1536,640]{1,0:T(8,128)(2,1)}, f32[8,1536]{1,0:T(8,128)}) custom-call(bf16[512,768]{1,0:T(8,128)(2,1)} %tokens.3, bf16[768,1024]{1,0:T(8,128)(2,1)} %qkv_weight.1, f32[8,768]{1,0:T(8,128)} %pad_maximum_fusion.3.small), custom_call_target="tpu_custom_call" | custom-call | tf_op jit(solution)/shard_map/gather_inputs/pallas_call | solution.py:316
  57.0 1.9 fusion
  58.9 1.0 copy.30
  60.0 1.0 copy.31
  63.4 1.5 copy-done.9
  64.9 5.7 %project.1 = (bf16[1024,1536]{1,0:T(8,128)(2,1)S(1)}, bf16[1024,384]{1,0:T(8,128)(2,1)S(1)}, bf16[1024,128]{1,0:T(8,128)(2,1)S(1)}, bf16[1024,128]{1,0:T(8,128)(...) custom-call(bf16[1024,1536]{1,0:T(8,128)(2,1)S(1)} %copy-done.8, f32[8,1536]{1,0:T(8,128)S(1)} %copy-done.10, ...), custom_call_target="tpu_custom_call" | custom-call | flops 2013265920 | bytes 10485760 | tf_op jit(solution)/shard_map/project/pallas_call | solution.py:1063
  70.6 6.6 %attend.1 = (bf16[1024,384]{1,0:T(8,128)(2,1)S(1)}, f32[8,1024]{1,0:T(8,128)S(1)}) custom-call(bf16[1024,384]{1,0:T(8,128)(2,1)S(1)} %get-tuple-element.67.q_ref, bf16[1024,128]{1,0:T(8,128)(2,1)S(1)} %get-tuple-element.68.k_ref, bf16[1024,128]{1,0:T(8,128)(2,1)S(1)} %get-tuple-element.69.v_ref, s32[1024,1]{1,0:T(8,128)S(1)} %copy.32.segk_ref, ...), custom_call_target="tpu_custom_call" | custom-call | flops 1610612736 | bytes 2359296 | tf_op jit(solution)/shard_map/attend/pallas_call | solution.py:1481
  78.1 29.3 %gather_context.1.ctx = bf16[1024,1536]{1,0:T(8,128)(2,1)} custom-call(bf16[1024,384]{1,0:T(8,128)(2,1)} %copy-done.4), custom_call_target="tpu_custom_call" | custom-call | tf_op jit(solution)/shard_map/gather_context/pallas_call | solution.py:365
  107.5 1.8 slice.45
  109.3 1.9 collective-permute-start.3
  111.2 1.8 slice.44
  113.0 11.5 %mix.1 = (bf16[1024,1536]{1,0:T(8,128)(2,1)}, f32[512,768]{1,0:T(8,128)S(1)}, f32[1024,128]{1,0:T(8,128)S(1)}, bf16[384,1536]{1,0:T(8,128)(2,1)S(1)}) custom-call(bf16[1024,1536]{1,0:T(8,128)(2,1)} %gather_context.1.ctx, bf16[1024,1536]{1,0:T(8,128)(2,1)} %get-tuple-element.64.tok, f32[8,1536]{1,0:T(8,128)S(1)} %copy-done.10, ...), custom_call_target="tpu_custom_call" | custom-call | flops 4831838208 | bytes 14680064 | tf_op jit(solution)/shard_map/mix/pallas_call | solution.py:1158
  124.5 1.1 copy-done
  126.4 1.0 copy-done.14
  127.4 47.5 %experts.1 = (bf16[1024,1152]{1,0:T(8,128)(2,1)}, bf16[3,1024,768]{2,1,0:T(8,128)(2,1)}, bf16[1024,1536]{1,0:T(8,128)(2,1)}, f32[8,1024]{1,0:T(8,128)}, bf16[102...) custom-call(bf16[1024,1536]{1,0:T(8,128)(2,1)} %get-tuple-element.72, ...), custom_call_target="tpu_custom_call" | custom-call | flops 21743271936 | bytes 27262976 | tf_op jit(solution)/shard_map/experts/pallas_call | solution.py:1326
  175.0 17.9 %expert_grads.1 = (bf16[2,2,2304,384]{3,2,1,0:T(8,128)(2,1)}, bf16[2,2,1152,384]{3,2,1,0:T(8,128)(2,1)}) custom-call(bf16[1024,1536]{1,0:T(8,128)(2,1)} %get-tuple-element.72.normed, bf16[3,1024,768]{2,1,0:T(8,128)(2,1)} %get-tuple-element.85.grads, bf16[1024,1152]{1,0:T(8,128)(2,1)} %get-tuple-element.86.weighted, bf16[1024,1536]{1,0:T(8,128)(2,1)} %get-tuple-element.87.cot), custom_call_target="tpu_custom_call" | custom-call | flops 10871635968 | bytes 25165824 | tf_op jit(solution)/shard_map/expert_grads/pallas_call | solution.py:1403
  192.8 67.4 %reduce_step.1 = (f32[512,768]{1,0:T(8,128)}, bf16[1024,1536]{1,0:T(8,128)(2,1)}, f32[8,1024]{1,0:T(8,128)}, f32[8,768]{1,0:T(8,128)}, bf16[2,144,384]{2,1,0:T(8,128)(2,1)}, /*index=5*/bf16[2,80,384]{2,1,0:T(8,128)(2,1)}) custom-call(bf16[1024,1536]{1,0:T(8,128)(2,1)} %get-tuple-element.82.partial, f32[8,1024]{1,0:T(8,128)} %get-tuple-element.83.vectors, ...), custom_call_target="tpu_custom_call" | custom-call | tf_op jit(solution)/shard_map/reduce_step/pallas_call | solution.py:673
  261.2 1.7 pad_maximum_fusion.2
  262.9 2.2 collective-permute-start.5
  265.1 1.5 collective-permute-start.7
  267.5 1.3 copy-done.15
  268.8 12.0 %attend_back.1 = (bf16[1024,640]{1,0:T(8,128)(2,1)S(1)}, f32[8,1024]{1,0:T(8,128)S(1)}) custom-call(bf16[1024,384]{1,0:T(8,128)(2,1)S(1)} %copy-done.13, bf16[1024,128]{1,0:T(8,128)(2,1)S(1)} %get-tuple-element.68.k_ref, bf16[1024,128]{1,0:T(8,128)(2,1)S(1)} %get-tuple-element.69.v_ref, bf16[1024,1536]{1,0:T(8,128)(2,1)} %get-tuple-element.90.hidden_low, ...), custom_call_target="tpu_custom_call" | custom-call | flops 4026531840 | bytes 3932160 | tf_op jit(solution)/shard_map/attend_back/pallas_call | solution.py:1592
  280.8 1.1 copy-done.17
  282.1 2.4 collective-permute-start.8
  284.5 13.1 %attn_grads.1 = (bf16[1024,1536]{1,0:T(8,128)(2,1)}, bf16[1536,640]{1,0:T(8,128)(2,1)}, bf16[384,1536]{1,0:T(8,128)(2,1)}, f32[8,1024]{1,0:T(8,128)}, f32[512,768]{1,0:T(8,128)}, /*index=5*/f32[8,1536]{1,0:T(8,128)}) custom-call(bf16[1024,640]{1,0:T(8,128)(2,1)} %copy-done.17, bf16[1536,640]{1,0:T(8,128)(2,1)} %get-tuple-element.66.weight.qkv_weight, ...), custom_call_target="tpu_custom_call" | custom-call | flops 5234491392 | bytes 25165824 | tf_op jit(solution)/shard_map/attn_grads/pallas_call | solution.py:1695
  297.6 72.4 %final_step.1 = (f32[512,768]{1,0:T(8,128)}, f32[8,768]{1,0:T(8,128)}, bf16[2,2,16,32,1024]{4,3,2,1,0:T(8,128)(2,1)}) custom-call(bf16[1024,1536]{1,0:T(8,128)(2,1)} %get-tuple-element.98.partial, f32[8,1024]{1,0:T(8,128)} %get-tuple-element.99.vectors, bf16[512,768]{1,0:T(8,128)(2,1)} %tokens.3, f32[1024,128]{1,0:T(8,128)} %copy-done.5, ...), custom_call_target="tpu_custom_call" | custom-call | tf_op jit(solution)/shard_map/final_step/pallas_call | solution.py:975
  370.0 2.2 copy-done.2
  372.2 2.9 attn_finish.1
  376.4 1.2 add_convert_fusion
  377.6 12.8 %expert_finish.1 = (f32[4608,384]{1,0:T(8,128)}, f32[4608,384]{1,0:T(8,128)}, f32[2304,768]{1,0:T(8,128)}) custom-call(s32[1]{0:T(128)} %bitcast.9.col_ref, bf16[4,4,2,2,216,384]{5,4,3,2,1,0:T(8,128)(2,1)} %bitcast.21, bf16[4,4,2,2,216,384]{5,4,3,2,1,0:T(8,128)(2,1)} %bitcast.22), custom_call_target="tpu_custom_call" | custom-call | tf_op jit(solution)/shard_map/expert_finish/pallas_call | solution.py:1754
  390.4 1.1 copy.35
  (98 shorter events, 9.3 us)
Async XLA Ops:
  7.2 105.8 %all-gather.5.cloned.1.call-start = ((), (), s32[]{:S(2)}) async-start(), calls=%async_computation | async-start | bytes 9732096 | tf_op jit(solution)/shard_map/all_gather | solution.py:1854
  7.2 11.1 %copy-start.29 = (f32[768]{0:T(1024)S(1)}, f32[768]{0:T(1024)}, u32[]{:S(2)}) copy-start(f32[768]{0:T(1024)} %param.14) | copy-start | bytes 9220
  7.2 11.1 %copy-start.30 = (f32[768]{0:T(1024)S(1)}, f32[768]{0:T(1024)}, u32[]{:S(2)}) copy-start(f32[768]{0:T(1024)} %param.15) | copy-start | bytes 9220
  7.2 11.2 %copy-start.28 = (bf16[768,6]{0,1:T(8,128)(2,1)S(1)}, bf16[768,6]{0,1:T(8,128)(2,1)}, u32[]{:S(2)}) copy-start(bf16[768,6]{0,1:T(8,128)(2,1)} %param.18) | copy-start | bytes 27652
  18.3 38.7 %copy-start.24 = (s32[1024,4]{0,1:T(4,128)S(1)}, s32[1024,4]{0,1:T(4,128)}, u32[]{:S(2)}) copy-start(s32[1024,4]{0,1:T(4,128)} %param.22) | copy-start | bytes 49156
  18.3 359.3 %all-gather.7.cloned.1.call-start = ((), (), s32[]{:S(2)}) async-start(), calls=%async_computation.1 | async-start | bytes 10948608 | tf_op jit(solution)/shard_map/all_gather | solution.py:1919
  18.4 40.5 %copy-start.26 = (f32[1,768]{1,0:T(1,128)}, f32[1,768]{1,0:T(1,128)S(1)}, u32[]{:S(2)}) copy-start(f32[1,768]{1,0:T(1,128)S(1)} %broadcast_in_dim.4.gain) | copy-start | bytes 9220
  18.4 40.5 %copy-start.27 = (f32[1,768]{1,0:T(1,128)}, f32[1,768]{1,0:T(1,128)S(1)}, u32[]{:S(2)}) copy-start(f32[1,768]{1,0:T(1,128)S(1)} %broadcast_in_dim.5.gain) | copy-start | bytes 9220
  55.8 5.2 %copy-start.7 = (s32[1024]{0:T(1024)S(1)}, s32[1024]{0:T(1024)}, u32[]{:S(2)}) copy-start(s32[1024]{0:T(1024)} %param.23) | copy-start | bytes 12292
  55.9 51.6 %collective-permute-start.2 = (bf16[512,768]{1,0:T(8,128)(2,1)}, bf16[512,768]{1,0:T(8,128)(2,1)}, u32[]{:S(2)}, u32[]{:S(2)}) collective-permute-start(bf16[512,768]{1,0:T(8,128)(2,1)} %cot.1), channel_id=1, source_target_pairs={{0,2},{1,3},{2,0},{3,1},{4,6},{5,7},{6,4},{7,5},{8,10},{9,11},{10,... | collective-permute-start | bytes 2359304 | tf_op jit(solution)/shard_map/ppermute | solution.py:31
  55.9 55.3 %collective-permute-start = (bf16[512,768]{1,0:T(8,128)(2,1)}, bf16[512,768]{1,0:T(8,128)(2,1)}, u32[]{:S(2)}, u32[]{:S(2)}) collective-permute-start(bf16[512,768]{1,0:T(8,128)(2,1)} %cot.1), channel_id=1, source_target_pairs={{0,3},{1,2},{2,1},{3,0},{4,7},{5,6},{6,5},{7,4},{8,11},{9,10},{10,... | collective-permute-start | bytes 2359304 | tf_op jit(solution)/shard_map/ppermute | solution.py:31
  70.6 6.6 %copy-start.5 = (f32[1024,128]{1,0:T(8,128)}, f32[1024,128]{1,0:T(8,128)S(1)}, u32[]{:S(2)}) copy-start(f32[1024,128]{1,0:T(8,128)S(1)} %get-tuple-element.100.scale) | copy-start | bytes 1572868
  70.6 6.6 %copy-start.11 = (bf16[1024,1536]{1,0:T(8,128)(2,1)}, bf16[1024,1536]{1,0:T(8,128)(2,1)S(1)}, u32[]{:S(2)}) copy-start(bf16[1024,1536]{1,0:T(8,128)(2,1)S(1)} %get-tuple-element.94.normed) | copy-start | bytes 9437188
  70.6 6.6 %copy-start.12 = (bf16[1024,384]{1,0:T(8,128)(2,1)}, bf16[1024,384]{1,0:T(8,128)(2,1)S(1)}, u32[]{:S(2)}) copy-start(bf16[1024,384]{1,0:T(8,128)(2,1)S(1)} %get-tuple-element.67.q_ref) | copy-start | bytes 2359300
  70.6 6.6 %copy-start.16 = (f32[1024,128]{1,0:T(8,128)}, f32[1024,128]{1,0:T(8,128)S(1)}, u32[]{:S(2)}) copy-start(f32[1024,128]{1,0:T(8,128)S(1)} %get-tuple-element.74.gates) | copy-start | bytes 1572868
  78.1 34.9 %copy-start.3 = (bf16[768,768]{1,0:T(8,128)(2,1)S(1)}, bf16[768,768]{1,0:T(8,128)(2,1)}, u32[]{:S(2)}) copy-start(bf16[768,768]{1,0:T(8,128)(2,1)} %param.17) | copy-start | bytes 3538948
  109.3 18.2 %collective-permute-start.3 = (bf16[256,768]{1,0:T(8,128)(2,1)}, bf16[256,768]{1,0:T(8,128)(2,1)}, u32[]{:S(2)}, u32[]{:S(2)}) collective-permute-start(bf16[256,768]{1,0:T(8,128)(2,1)} %slice.45), channel_id=1, source_target_pairs={{0,3},{1,2},{2,1},{3,0},{4,7},{5,6},{6,5},{7,4},{8,11},{9,10},{10,... | collective-permute-start | bytes 1179656 | tf_op jit(solution)/shard_map/ppermute | solution.py:31
  113.0 14.5 %collective-permute-start.1 = (bf16[256,768]{1,0:T(8,128)(2,1)}, bf16[256,768]{1,0:T(8,128)(2,1)}, u32[]{:S(2)}, u32[]{:S(2)}) collective-permute-start(bf16[256,768]{1,0:T(8,128)(2,1)} %slice.44), channel_id=1, source_target_pairs={{0,2},{1,3},{2,0},{3,1},{4,6},{5,7},{6,4},{7,5},{8,10},{9,11},{10,... | collective-permute-start | bytes 1179656 | tf_op jit(solution)/shard_map/ppermute | solution.py:31
  192.8 74.7 %copy-start.13 = (bf16[1024,384]{1,0:T(8,128)(2,1)S(1)}, bf16[1024,384]{1,0:T(8,128)(2,1)}, u32[]{:S(2)}) copy-start(bf16[1024,384]{1,0:T(8,128)(2,1)} %copy-done.12) | copy-start | bytes 2359300
  262.9 18.9 %collective-permute-start.5 = (bf16[256,768]{1,0:T(8,128)(2,1)}, bf16[256,768]{1,0:T(8,128)(2,1)S(1)}, u32[]{:S(2)}, u32[]{:S(2)}) collective-permute-start(bf16[256,768]{1,0:T(8,128)(2,1)} %get-tuple-element.78), channel_id=1, source_target_pairs={{0,3},{1,2},{2,1},{3,0},{4,7},{5,6},{6,5},{7,4},{8,11},{9,10},{10,... | collective-permute-start | bytes 1179656 | tf_op jit(solution)/shard_map/ppermute | solution.py:31
  265.1 111.2 %collective-permute-start.4 = (bf16[256,768]{1,0:T(8,128)(2,1)}, bf16[256,768]{1,0:T(8,128)(2,1)S(1)}, u32[]{:S(2)}, u32[]{:S(2)}) collective-permute-start(bf16[256,768]{1,0:T(8,128)(2,1)} %get-tuple-element.76), channel_id=1, source_target_pairs={{0,2},{1,3},{2,0},{3,1},{4,6},{5,7},{6,4},{7,5},{8,10},{9,11},{10,... | collective-permute-start | bytes 1179656 | tf_op jit(solution)/shard_map/ppermute | solution.py:31
  265.1 16.9 %collective-permute-start.7 = (bf16[256,768]{1,0:T(8,128)(2,1)}, bf16[256,768]{1,0:T(8,128)(2,1)S(1)}, u32[]{:S(2)}, u32[]{:S(2)}) collective-permute-start(bf16[256,768]{1,0:T(8,128)(2,1)} %get-tuple-element.80), channel_id=1, source_target_pairs={{0,2},{1,3},{2,0},{3,1},{4,6},{5,7},{6,4},{7,5},{8,10},{9,11},{10,... | collective-permute-start | bytes 1179656 | tf_op jit(solution)/shard_map/ppermute | solution.py:31
  266.6 109.7 %collective-permute-start.9 = (bf16[256,768]{1,0:T(8,128)(2,1)}, bf16[256,768]{1,0:T(8,128)(2,1)S(1)}, u32[]{:S(2)}, u32[]{:S(2)}) collective-permute-start(bf16[256,768]{1,0:T(8,128)(2,1)} %get-tuple-element.81), channel_id=1, source_target_pairs={{0,3},{1,2},{2,1},{3,0},{4,7},{5,6},{6,5},{7,4},{8,11},{9,10},{10,... | collective-permute-start | bytes 1179656 | tf_op jit(solution)/shard_map/ppermute | solution.py:31
  268.8 13.1 %copy-start.23 = (bf16[256,768]{1,0:T(8,128)(2,1)S(1)}, bf16[256,768]{1,0:T(8,128)(2,1)}, u32[]{:S(2)}) copy-start(bf16[256,768]{1,0:T(8,128)(2,1)} %get-tuple-element.77) | copy-start | bytes 1179652
  268.8 13.3 %copy-start.22 = (bf16[256,768]{1,0:T(8,128)(2,1)S(1)}, bf16[256,768]{1,0:T(8,128)(2,1)}, u32[]{:S(2)}) copy-start(bf16[256,768]{1,0:T(8,128)(2,1)} %get-tuple-element.79) | copy-start | bytes 1179652
  281.8 2.7 copy-start.18
  281.9 94.4 %collective-permute-start.6 = (bf16[256,768]{1,0:T(8,128)(2,1)S(1)}, bf16[256,768]{1,0:T(8,128)(2,1)S(1)}, u32[]{:S(2)}, u32[]{:S(2)}) collective-permute-start(bf16[256,768]{1,0:T(8,128)(2,1)S(1)} %add_convert_fusion.2), channel_id=1, source_target_pairs={{0,2},{1,3},{2,0},{3,1},{4,6},{5,7},{6,4},{7,5},{8,10},{9,11},{10,... | collective-permute-start | bytes 1179656 | tf_op jit(solution)/shard_map/ppermute | solution.py:31
  282.1 94.2 %collective-permute-start.8 = (bf16[256,768]{1,0:T(8,128)(2,1)S(1)}, bf16[256,768]{1,0:T(8,128)(2,1)S(1)}, u32[]{:S(2)}, u32[]{:S(2)}) collective-permute-start(bf16[256,768]{1,0:T(8,128)(2,1)S(1)} %add_convert_fusion.1), channel_id=1, source_target_pairs={{0,3},{1,2},{2,1},{3,0},{4,7},{5,6},{6,5},{7,4},{8,11},{9,10},{10,... | collective-permute-start | bytes 1179656 | tf_op jit(solution)/shard_map/ppermute | solution.py:31
  372.2 2.9 copy-start.25
  372.2 4.1 %copy-start.1 = (f32[512,768]{1,0:T(8,128)S(1)}, f32[512,768]{1,0:T(8,128)}, u32[]{:S(2)}) copy-start(f32[512,768]{1,0:T(8,128)} %copy-done) | copy-start | bytes 4718596
  372.2 4.2 %copy-start.21 = (f32[512,768]{1,0:T(8,128)S(1)}, f32[512,768]{1,0:T(8,128)}, u32[]{:S(2)}) copy-start(f32[512,768]{1,0:T(8,128)} %get-tuple-element.75) | copy-start | bytes 4718596
  377.6 12.8 %copy-start.20 = (f32[512,768]{1,0:T(8,128)S(1)}, f32[512,768]{1,0:T(8,128)}, u32[]{:S(2)}) copy-start(f32[512,768]{1,0:T(8,128)} %get-tuple-element.136) | copy-start | bytes 4718596
  (11 other events, 15.2 us)
Sparse Core Ops, SparseCore 0:
  18.4 60.1 all-gather.4
  263.0 68.8 all-gather.6
